TPU v7x, 32 devices: a whole 2x2x4 slice. The times are simulated.
32 devices in a mesh: experts: 2 (over y), context: 4 (over z), dp: 4 (over x, core).
Axes of the slice: x: 2, y: 2, z: 4, core: 2. Of those that a mesh axis runs over, the one named last changes fastest.
Arguments:
- decoder_input: bfloat16 [8, 2048, 1024], P(('experts', 'dp'), 'context'), may hold values from -6 to 6
- gain_attn: float32 [1024], replicated, may hold values from 0.5 to 1.5
- query_weight: bfloat16 [1024, 1024], replicated, may hold values from -0.1875 to 0.1875
- keyval_weight: bfloat16 [1024, 1024], replicated, may hold values from -0.1875 to 0.1875
- output_weight: bfloat16 [1024, 1024], replicated, may hold values from -0.75 to 0.75
- gain_moe: float32 [1024], replicated, may hold values from 0.5 to 1.5
- w_router: bfloat16 [1024, 32], replicated, may hold values from -0.09375 to 0.09375
- w_gateup: bfloat16 [32, 1024, 1024], P('experts'), may hold values from -0.1875 to 0.1875
- w_down: bfloat16 [32, 512, 1024], P('experts'), may hold values from -0.75 to 0.75
- top_idx: int32 [8, 2048, 8], P(('experts', 'dp'), 'context'), may hold values from 0 to 31, all different within a row
- slot_order: int32 [8, 4, 512], P(('experts', 'dp'), 'context'), may hold values from 0 to 511, each once within a row
- cotangent: bfloat16 [8, 2048, 1024], P(('experts', 'dp'), 'context'), may hold values from -6 to 6
Outputs:
- layer_output: bfloat16 [8, 2048, 1024], P(('experts', 'dp'), 'context')
- grad_input: bfloat16 [8, 2048, 1024], P(('experts', 'dp'), 'context')
- grad_gain_attn: float32 [1024], P(('experts', 'context', 'dp'))
- grad_query: float32 [1024, 1024], P(('experts', 'context', 'dp'))
- grad_keyval: float32 [1024, 1024], P(('experts', 'context', 'dp'))
- grad_out: float32 [1024, 1024], P(('experts', 'context', 'dp'))
- grad_gain_moe: float32 [1024], P(('experts', 'context', 'dp'))
- grad_router: float32 [1024, 32], P(('experts', 'context', 'dp'))
- grad_gateup: float32 [32, 1024, 1024], P('experts', ('context', 'dp'))
- grad_down: float32 [32, 512, 1024], P('experts', None, ('context', 'dp'))
Inputs may be any that keep to these rules, and one draw needn't show every extreme that they name: `top_idx`: each token names 8 different experts; every expert is named by some token. `slot_order`: within each routing group every value appears once.
All inputs are finite; a program needn't handle non-finite values.
Results may differ from a plain program's by a relative error of at most 0.02.
Values may be sent and summed in bfloat16 or wider, within the bound.
No kernel may reach another device: no remote copies, remote signals or barrier semaphores. Data moves between devices by JAX's collectives and lax.ppermute only.
A program may use at most 256 MiB of HBM per device.

v0:
```python
import jax
import jax.numpy as jnp
from jax import lax
from jax.sharding import PartitionSpec as P

KVH = 8
HD = 64
FF = 512
EXPERTS = 32
TOPK = 8
BLOCK = 256
CAP = 160


EPSILON = 1e-06
MASKED = -1e30


def rotary_tables(offset, length, head_size):
    half_size = head_size // 2
    places = (offset + jnp.arange(length)).astype(jnp.float32)
    frequency = 10000.0 ** (-jnp.arange(half_size).astype(jnp.float32) * 2.0 / head_size)
    angles = places[:, None] * frequency[None, :]
    return (jnp.cos(angles)[:, None, :], jnp.sin(angles)[:, None, :])


def rotate(tensor, cos_table, sin_table):
    half_size = tensor.shape[-1] // 2
    first_half = tensor[..., :half_size]
    second_half = tensor[..., half_size:]
    return jnp.concatenate(
        [
            first_half * cos_table - second_half * sin_table,
            second_half * cos_table + first_half * sin_table,
        ],
        axis=-1,
    )


def norm_forward(tensor, gain):
    inverse = lax.rsqrt(jnp.mean(tensor * tensor, axis=-1, keepdims=True) + EPSILON)
    return (tensor * inverse * gain, inverse)


def norm_backward(tensor, inverse, gain, upstream):
    scaled = gain * upstream
    grad_gain = jnp.sum(upstream * tensor * inverse, axis=0)
    grad_tensor = inverse * scaled - tensor * inverse**3 * jnp.mean(
        tensor * scaled, axis=-1, keepdims=True
    )
    return (grad_tensor, grad_gain)


def on_device(
    decoder_input,
    gain_attn,
    query_weight,
    keyval_weight,
    output_weight,
    gain_moe,
    w_router,
    w_gateup,
    w_down,
    top_idx,
    slot_order,
    cotangent,
):
    inputs = decoder_input[0].astype(jnp.float32)
    length = inputs.shape[0]
    width = inputs.shape[1]
    heads = query_weight.shape[1] // HD
    kv_width = keyval_weight.shape[1]
    kv_half = kv_width // 2
    grouped = heads // KVH
    scale = HD ** (-0.5)
    offset = lax.axis_index("context") * length
    cos_table, sin_table = rotary_tables(offset, length, HD)
    normed_rows, inverse_attn = norm_forward(inputs, gain_attn)
    normed_low = normed_rows.astype(jnp.bfloat16)
    query_unrotated = jnp.dot(normed_low, query_weight, preferred_element_type=jnp.float32)
    keyval_unrotated = jnp.dot(normed_low, keyval_weight, preferred_element_type=jnp.float32)
    queries = (
        rotate(query_unrotated.reshape(length, heads, HD), cos_table, sin_table)
        .astype(jnp.bfloat16)
        .reshape(length, KVH, grouped, HD)
    )
    keys_turned = rotate(
        keyval_unrotated[:, :kv_half].reshape(length, KVH, HD), cos_table, sin_table
    ).reshape(length, kv_half)
    keyval = jnp.concatenate([keys_turned, keyval_unrotated[:, kv_half:]], axis=1).astype(
        jnp.bfloat16
    )
    query_block = (offset + jnp.arange(length)) // BLOCK

    def block_scores(block_rows, block_start):
        keys_part = block_rows[:, :kv_half].reshape(BLOCK, KVH, HD)
        values_part = block_rows[:, kv_half:].reshape(BLOCK, KVH, HD)
        scores = (
            jnp.einsum("qhgd,khd->hgqk", queries, keys_part, preferred_element_type=jnp.float32)
            * scale
        )
        allowed = (block_start // BLOCK <= query_block)[None, None, :, None]
        return (jnp.where(allowed, scores, MASKED), allowed, keys_part, values_part)

    start_state = (
        jnp.full((KVH, grouped, length), MASKED, jnp.float32),
        jnp.zeros((KVH, grouped, length), jnp.float32),
        jnp.zeros((length, KVH, grouped, HD), jnp.float32),
    )
    blocks = lax.all_gather(keyval, "context", axis=0, tiled=True).reshape(-1, BLOCK, kv_width)

    def attend_step(state_now, block_item):
        running_max, running_sum, weighted = state_now
        block_rows, number = block_item
        scores, allowed, keys_part, values_part = block_scores(block_rows, number * BLOCK)
        new_max = jnp.maximum(running_max, jnp.max(scores, axis=-1))
        weights = jnp.where(allowed, jnp.exp(scores - new_max[..., None]), 0.0)
        factor = jnp.exp(running_max - new_max)
        running_sum = running_sum * factor + jnp.sum(weights, axis=-1)
        update = jnp.einsum(
            "hgqk,khd->qhgd",
            weights.astype(jnp.bfloat16),
            values_part,
            preferred_element_type=jnp.float32,
        )
        weighted = weighted * jnp.transpose(factor, (2, 0, 1))[..., None] + update
        return ((new_max, running_sum, weighted), None)

    running_max, running_sum, weighted = lax.scan(
        attend_step, start_state, (blocks, jnp.arange(blocks.shape[0]))
    )[0]
    log_total = running_max + jnp.log(running_sum)
    attention_output = weighted / jnp.transpose(running_sum, (2, 0, 1))[..., None]
    attn_low = attention_output.reshape(length, heads * HD).astype(jnp.bfloat16)
    residual_middle = inputs + jnp.dot(attn_low, output_weight, preferred_element_type=jnp.float32)
    normed_moe, inverse_moe = norm_forward(residual_middle, gain_moe)
    moe_low = normed_moe.astype(jnp.bfloat16)
    logits = jnp.dot(moe_low, w_router, preferred_element_type=jnp.float32)
    chosen_ids = top_idx[0]
    chosen_hot = (chosen_ids[:, :, None] == jnp.arange(EXPERTS)[None, None, :]).astype(jnp.int32)
    chosen_float = chosen_hot.astype(jnp.float32)
    selected = jnp.sum(logits[:, None, :] * chosen_float, axis=2)
    gates = jax.nn.softmax(selected, axis=-1)
    rank_order = slot_order[0, 0]
    earlier = (rank_order[None, :] < rank_order[:, None]).astype(jnp.int32)
    before_count = jnp.dot(earlier, jnp.sum(chosen_hot, axis=1))
    slot_index = jnp.sum(before_count[:, None, :] * chosen_hot, axis=2)
    kept_pair = slot_index < CAP
    target = jnp.where(kept_pair, chosen_ids * CAP + slot_index, EXPERTS * CAP).reshape(-1)
    reading = jnp.minimum(target, EXPERTS * CAP - 1)
    owners = lax.axis_size("experts")
    local_experts = w_gateup.shape[0]
    outgoing = (
        jnp.zeros((EXPERTS * CAP, width), jnp.bfloat16)
        .at[target]
        .set(jnp.repeat(moe_low, TOPK, axis=0), mode="drop")
    )
    received = lax.all_to_all(
        outgoing.reshape(owners, local_experts, CAP, width),
        "experts",
        split_axis=0,
        concat_axis=0,
        tiled=True,
    )
    both = jnp.einsum("nesd,edf->nesf", received, w_gateup, preferred_element_type=jnp.float32)
    hidden = (jax.nn.silu(both[..., :FF]) * both[..., FF:]).astype(jnp.bfloat16)
    result = jnp.einsum(
        "nesf,efd->nesd", hidden, w_down, preferred_element_type=jnp.float32
    ).astype(jnp.bfloat16)
    returned = lax.all_to_all(result, "experts", split_axis=0, concat_axis=0, tiled=True).reshape(
        EXPERTS * CAP, width
    )
    picked = jnp.take(returned, reading, axis=0).reshape(length, TOPK, width)
    gate_kept = jnp.where(kept_pair, gates, 0.0)
    mixed = jnp.einsum("tk,tkd->td", gate_kept, picked, preferred_element_type=jnp.float32)
    layer_output = (residual_middle + mixed).astype(jnp.bfloat16)[None]
    upstream = cotangent[0].astype(jnp.float32)
    grad_gates = jnp.where(
        kept_pair,
        jnp.einsum("td,tkd->tk", upstream, picked, preferred_element_type=jnp.float32),
        0.0,
    )
    pair_grads = (
        (gate_kept[:, :, None] * upstream[:, None, :])
        .astype(jnp.bfloat16)
        .reshape(length * TOPK, width)
    )
    grad_slots = (
        jnp.zeros((EXPERTS * CAP, width), jnp.bfloat16).at[target].set(pair_grads, mode="drop")
    )
    grad_arrived = lax.all_to_all(
        grad_slots.reshape(owners, local_experts, CAP, width),
        "experts",
        split_axis=0,
        concat_axis=0,
        tiled=True,
    )
    gate_pre = both[..., :FF]
    up_pre = both[..., FF:]
    sigmoid = jax.nn.sigmoid(gate_pre)
    activated = gate_pre * sigmoid
    hidden = (activated * up_pre).astype(jnp.bfloat16)
    grad_hidden = jnp.einsum(
        "nesd,efd->nesf", grad_arrived, w_down, preferred_element_type=jnp.float32
    )
    down_local = jnp.einsum(
        "nesf,nesd->efd", hidden, grad_arrived, preferred_element_type=jnp.float32
    )
    grad_both = jnp.concatenate(
        [
            grad_hidden * up_pre * sigmoid * (1.0 + gate_pre * (1.0 - sigmoid)),
            grad_hidden * activated,
        ],
        axis=-1,
    ).astype(jnp.bfloat16)
    gateup_local = jnp.einsum(
        "nesd,nesf->edf", received, grad_both, preferred_element_type=jnp.float32
    )
    grad_rows = jnp.einsum(
        "nesf,edf->nesd", grad_both, w_gateup, preferred_element_type=jnp.float32
    ).astype(jnp.bfloat16)
    rows_back = lax.all_to_all(
        grad_rows, "experts", split_axis=0, concat_axis=0, tiled=True
    ).reshape(EXPERTS * CAP, width)
    back_pairs = jnp.take(rows_back, reading, axis=0).reshape(length, TOPK, width)
    grad_moe_rows = jnp.einsum(
        "tk,tkd->td", kept_pair.astype(jnp.float32), back_pairs, preferred_element_type=jnp.float32
    )
    grad_selected = gates * (grad_gates - jnp.sum(gates * grad_gates, axis=1, keepdims=True))
    grad_logits = jnp.sum(grad_selected[:, :, None] * chosen_float, axis=1).astype(jnp.bfloat16)
    router_local = jnp.einsum("td,te->de", moe_low, grad_logits, preferred_element_type=jnp.float32)
    grad_moe_rows = grad_moe_rows + jnp.einsum(
        "te,de->td", grad_logits, w_router, preferred_element_type=jnp.float32
    )
    grad_middle, gain_moe_local = norm_backward(
        residual_middle, inverse_moe, gain_moe, grad_moe_rows
    )
    grad_middle = grad_middle + upstream
    grad_attn = grad_middle.astype(jnp.bfloat16)
    out_local = jnp.einsum("tf,td->fd", attn_low, grad_attn, preferred_element_type=jnp.float32)
    grad_heads = (
        jnp.einsum("td,fd->tf", grad_attn, output_weight, preferred_element_type=jnp.float32)
        .astype(jnp.bfloat16)
        .reshape(length, KVH, grouped, HD)
    )
    row_terms = jnp.transpose(
        jnp.sum(grad_heads.astype(jnp.float32) * attention_output, axis=-1), (1, 2, 0)
    )
    grad_queries = jnp.zeros((length, KVH, grouped, HD), jnp.float32)
    blocks = lax.all_gather(keyval, "context", axis=0, tiled=True).reshape(-1, BLOCK, kv_width)

    def back_step(grad_now, block_item):
        block_rows, number = block_item
        scores, allowed, keys_part, values_part = block_scores(block_rows, number * BLOCK)
        probs = jnp.where(allowed, jnp.exp(scores - log_total[..., None]), 0.0)
        grad_values = jnp.einsum(
            "hgqk,qhgd->khd",
            probs.astype(jnp.bfloat16),
            grad_heads,
            preferred_element_type=jnp.float32,
        )
        grad_probs = jnp.einsum(
            "qhgd,khd->hgqk", grad_heads, values_part, preferred_element_type=jnp.float32
        )
        grad_scores = (probs * (grad_probs - row_terms[..., None])).astype(jnp.bfloat16)
        grad_now = grad_now + scale * jnp.einsum(
            "hgqk,khd->qhgd", grad_scores, keys_part, preferred_element_type=jnp.float32
        )
        grad_keys = scale * jnp.einsum(
            "hgqk,qhgd->khd", grad_scores, queries, preferred_element_type=jnp.float32
        )
        return (
            grad_now,
            jnp.concatenate(
                [grad_keys.reshape(BLOCK, kv_half), grad_values.reshape(BLOCK, kv_half)], axis=1
            ),
        )

    grad_queries, block_grads = lax.scan(
        back_step, grad_queries, (blocks, jnp.arange(blocks.shape[0]))
    )
    grad_keyvals = block_grads.reshape(-1, kv_width)
    grad_queries, grad_keyvals = (grad_queries, grad_keyvals)
    grad_keyval_own = lax.psum_scatter(
        grad_keyvals.astype(jnp.bfloat16), "context", scatter_dimension=0, tiled=True
    ).astype(jnp.float32)
    grad_query_pre = (
        rotate(grad_queries.reshape(length, heads, HD), cos_table, -sin_table)
        .reshape(length, heads * HD)
        .astype(jnp.bfloat16)
    )
    grad_keys_pre = rotate(
        grad_keyval_own[:, :kv_half].reshape(length, KVH, HD), cos_table, -sin_table
    ).reshape(length, kv_half)
    grad_keyval_pre = jnp.concatenate([grad_keys_pre, grad_keyval_own[:, kv_half:]], axis=1).astype(
        jnp.bfloat16
    )
    query_local = jnp.einsum(
        "td,tf->df", normed_low, grad_query_pre, preferred_element_type=jnp.float32
    )
    keyval_local = jnp.einsum(
        "td,tf->df", normed_low, grad_keyval_pre, preferred_element_type=jnp.float32
    )
    grad_normed = jnp.einsum(
        "tf,df->td", grad_query_pre, query_weight, preferred_element_type=jnp.float32
    )
    grad_normed = grad_normed + jnp.einsum(
        "tf,df->td", grad_keyval_pre, keyval_weight, preferred_element_type=jnp.float32
    )
    grad_inputs, gain_attn_local = norm_backward(inputs, inverse_attn, gain_attn, grad_normed)
    grad_input = (grad_inputs + grad_middle).astype(jnp.bfloat16)[None]
    dense_sums = (
        lax.psum_scatter(
            gain_attn_local, ("experts", "context", "dp"), scatter_dimension=0, tiled=True
        ),
        lax.psum_scatter(
            query_local, ("experts", "context", "dp"), scatter_dimension=0, tiled=True
        ),
        lax.psum_scatter(
            keyval_local, ("experts", "context", "dp"), scatter_dimension=0, tiled=True
        ),
        lax.psum_scatter(out_local, ("experts", "context", "dp"), scatter_dimension=0, tiled=True),
        lax.psum_scatter(
            gain_moe_local, ("experts", "context", "dp"), scatter_dimension=0, tiled=True
        ),
        lax.psum_scatter(
            router_local, ("experts", "context", "dp"), scatter_dimension=0, tiled=True
        ),
    )
    expert_sums = (
        lax.psum_scatter(
            gateup_local.astype(jnp.bfloat16), ("context", "dp"), scatter_dimension=1, tiled=True
        ).astype(jnp.float32),
        lax.psum_scatter(
            down_local.astype(jnp.bfloat16), ("context", "dp"), scatter_dimension=2, tiled=True
        ).astype(jnp.float32),
    )
    summed = tuple(dense_sums) + tuple(expert_sums)
    return (
        layer_output,
        grad_input,
        summed[0],
        summed[1],
        summed[2],
        summed[3],
        summed[4],
        summed[5],
        summed[6],
        summed[7],
    )


def solution(mesh):
    in_specs = (
        P(("experts", "dp"), "context", None),
        P(),
        P(),
        P(),
        P(),
        P(),
        P(),
        P("experts", None, None),
        P("experts", None, None),
        P(("experts", "dp"), "context", None),
        P(("experts", "dp"), "context", None),
        P(("experts", "dp"), "context", None),
    )
    out_specs = (
        P(("experts", "dp"), "context", None),
        P(("experts", "dp"), "context", None),
        P(("experts", "context", "dp")),
        P(("experts", "context", "dp"), None),
        P(("experts", "context", "dp"), None),
        P(("experts", "context", "dp"), None),
        P(("experts", "context", "dp")),
        P(("experts", "context", "dp"), None),
        P("experts", ("context", "dp"), None),
        P("experts", None, ("context", "dp")),
    )
    return jax.shard_map(
        on_device, mesh=mesh, in_specs=in_specs, out_specs=out_specs, check_vma=False
    )
```

profile of v0, /device:TPU:0, one launch (start us, length us, event | category | flops | bytes accessed | tf_op | source)
XLA Modules:
  0.0 2236.9 jit_solution(12755223432762280625)
XLA Ops:
  36.1 67.6 %all-gather.2.cloned.1.call-done = bf16[2048,1024]{1,0:T(8,128)(2,1)} async-done(((bf16[512,1024]{1,0:T(8,128)(2,1)}), bf16[2048,1024]{1,0:T(8,128)(2,1)}) %all-gather.2.cloned.1.call-update) | async-done | bytes 4194320 | tf_op jit(solution)/shard_map/all_gather | solution.py:110
  110.1 75.0 %while.32 = (s32[]{:T(128)}, f32[8,2,512]{2,1,0:T(2,128)S(1)}, f32[8,2,512]{2,1,0:T(2,128)S(1)}, f32[512,8,2,64]{0,3,2,1:T(8,128)}, s32[8]{0:T(128)S(1)}, /*inde...) while((s32[]{:T(128)}, f32[8,2,512]{2,1,0:T(2,128)S(1)}, ...), condition=%wide.region_4.5_spmd.clone, body=%wide.region_1.4_spmd.clone.sunk | while | flops 565764608 | bytes 50334088 | solution.py:129
  192.1 25.2 %scatter_custom_fusion = bf16[5120,1024]{1,0:T(8,128)(2,1)} fusion(s32[4096]{0:T(1024)S(1)} %bitcast.375, bf16[]{:T(256)} %constant.196.clone.1, bf16[512,1024]{1,0:T(8,128)(2,1)S(1)} %multiply_convert_fusion.1), kind=kCustom, calls=%fused_computation.102 | custom fusion | bytes 11534338 | tf_op jit(solution)/shard_map/scatter | solution.py:156
  217.3 127.9 %all_to_all.20 = bf16[2,16,160,1024]{3,2,1,0:T(8,128)(2,1)} all-to-all(bf16[2,16,160,1024]{3,2,1,0:T(8,128)(2,1)} %bitcast.343), channel_id=1, replica_groups=mesh['experts'=2,'context'=4,'dp'=4] {'experts'}, dimensions={0} | all-to-all | bytes 20971520 | tf_op jit(solution)/shard_map/all_to_all | solution.py:158
  345.1 24.5 %fusion.73 = f32[2,16,160,1024]{3,2,0,1:T(8,128)} fusion(bf16[16,1024,1024]{2,1,0:T(8,128)(2,1)} %param.25, bf16[2,16,160,1024]{3,2,1,0:T(8,128)(2,1)} %all_to_all.20), kind=kOutput, calls=%fused_computation.109 | convolution fusion | flops 10737418240 | bytes 65011712 | tf_op jit(solution)/shard_map/nesd,edf->nesf/dot_general | solution.py:165
  417.6 109.0 %all-to-all-done.1 = bf16[2,16,160,1024]{3,2,1,0:T(8,128)(2,1)} async-done(((bf16[2,16,160,1024]{3,2,1,0:T(8,128)(2,1)}), bf16[2,16,160,1024]{3,2,1,0:T(8,128)(2,1)}, u32[]{:S(2)}, u32[]{:S(2)}) %all-to-all-start.1) | async-done | bytes 10485792 | tf_op jit(solution)/shard_map/all_to_all | solution.py:170
  526.6 26.5 %gather_fusion = bf16[4096,1024]{1,0:T(8,128)(2,1)} fusion(bf16[5120,1024]{1,0:T(8,128)(2,1)} %bitcast.24, s32[4096]{0:T(1024)S(1)} %broadcast_clamp_fusion), kind=kCustom, calls=%fused_computation.clone | custom fusion | bytes 16793600 | tf_op jit(solution)/shard_map/jit(_take)/gather | solution.py:173
  565.7 26.2 %scatter_custom_fusion.1 = bf16[5120,1024]{1,0:T(8,128)(2,1)} fusion(s32[4096]{0:T(1024)} %bitcast.376, f32[512,1024]{1,0:T(8,128)} %bitcast_convert_fusion.2, f32[4096]{0:T(1024)S(1)} %broadcast_select_fusion.4, bf16[]{:T(256)} %constant.196.clone.1), kind=kCustom, calls=%fused_computation.95 | custom fusion | flops 8388608 | bytes 12599808 | tf_op jit(solution)/shard_map/scatter | solution.py:189
  591.9 126.3 %all_to_all.21 = bf16[2,16,160,1024]{3,2,1,0:T(8,128)(2,1)} all-to-all(bf16[2,16,160,1024]{3,2,1,0:T(8,128)(2,1)} %bitcast.342), channel_id=1, replica_groups=mesh['experts'=2,'context'=4,'dp'=4] {'experts'}, dimensions={0} | all-to-all | bytes 20971520 | tf_op jit(solution)/shard_map/all_to_all | solution.py:191
  718.3 24.8 %fusion.52 = (bf16[2,16,160,512]{3,2,0,1:T(8,128)(2,1)}, bf16[2,16,160,512]{3,2,0,1:T(8,128)(2,1)}) fusion(f32[2,16,160,1024]{3,2,0,1:T(8,128)} %fusion.73, bf16[16,512,1024]{2,1,0:T(8,128)(2,1)} %param.26, bf16[2,16,160,1024]{3,2,1,0:T(8,128)(2,1)} %all_to_all.21), kind=kOutput, calls=%fused_computation.84 | convolution fusion | flops 5402787840 | bytes 58720256 | tf_op jit(solution)/shard_map/nesd,efd->nesf/dot_general | solution.py:203
  743.0 20.8 convert_bitcast_fusion
  791.3 102.8 %all-to-all-done.3 = bf16[2,16,160,1024]{3,2,1,0:T(8,128)(2,1)} async-done(((bf16[2,16,160,1024]{3,2,1,0:T(8,128)(2,1)}), bf16[2,16,160,1024]{3,2,1,0:T(8,128)(2,1)}, u32[]{:S(2)}, u32[]{:S(2)}) %all-to-all-start.3) | async-done | bytes 10485792 | tf_op jit(solution)/shard_map/all_to_all | solution.py:222
  894.0 26.6 %gather_fusion.1 = bf16[4096,1024]{1,0:T(8,128)(2,1)} fusion(bf16[5120,1024]{1,0:T(8,128)(2,1)} %bitcast.36, s32[4096]{0:T(1024)S(1)} %broadcast_clamp_fusion), kind=kCustom, calls=%fused_computation.1.clone | custom fusion | bytes 16793600 | tf_op jit(solution)/shard_map/jit(_take)/gather | solution.py:225
  941.6 135.8 %while.33 = (s32[]{:T(128)}, f32[512,8,2,64]{0,3,2,1:T(8,128)}, bf16[8,256,1024]{2,1,0:T(8,128)(2,1)}, bf16[8,256,1024]{1,2,0:T(8,128)(2,1)}, s32[8]{0:T(128)S(1...) while((s32[]{:T(128)}, f32[512,8,2,64]{0,3,2,1:T(8,128)}, ...), condition=%wide.region_18.20_spmd.clone, body=%wide.region_17.19_spmd.clone.sunk | while | flops 1370235392 | bytes 73762728 | solution.py:279
  1077.5 15.9 bitcast_convert_fusion.1
  1093.5 25.4 %bitcast_convert_fusion = bf16[16,1024,1024]{2,1,0:T(8,128)(2,1)} fusion(bf16[2,16,160,1024]{3,2,1,0:T(8,128)(2,1)} %all_to_all.20, bf16[2,16,160,512]{3,2,0,1:T(8,128)(2,1)} %get-tuple-element.439, bf16[2,16,160,512]{3,2,0,1:T(8,128)(2,1)} %get-tuple-element.438), kind=kOutput, calls=%fused_computation.67 | convolution fusion | flops 10775166976 | bytes 54525952 | tf_op jit(solution)/shard_map/nesd,nesf->edf/dot_general | solution.py:216
  1134.4 18.4 reduce-scatter.8.cloned.1.call-done
  1174.0 42.7 %all-reduce.2 = (f32[1024]{0:T(1024)S(1)}, f32[1024]{0:T(1024)S(1)}) all-reduce(f32[1024]{0:T(1024)S(1)} %get-tuple-element.387, f32[1024]{0:T(1024)S(1)} %copy-done.48), channel_id=3, replica_groups=mesh['experts'=2,'context'=4,'dp'=4] {'experts','context','dp'}, use_global_device_ids=true, to_apply=%region_22.24.clone | all-reduce | flops 2048 | bytes 16384
  1221.8 114.6 %reduce-scatter.20.cloned.1.call-done = bf16[16,512,64]{1,2,0:T(8,128)(2,1)} async-done(((bf16[16,512,1024]{1,2,0:T(8,128)(2,1)}), bf16[16,512,64]{1,2,0:T(8,128)(2,1)}) %reduce-scatter.20.cloned.1.call-update) | async-done | bytes 1048592 | tf_op jit(solution)/shard_map/reduce_scatter | solution.py:334
  1339.2 333.5 %reduce-scatter.18.cloned.1.call-done = bf16[16,64,1024]{2,1,0:T(8,128)(2,1)} async-done(((bf16[16,1024,1024]{2,1,0:T(8,128)(2,1)}), bf16[16,64,1024]{2,1,0:T(8,128)(2,1)}) %reduce-scatter.18.cloned.1.call-update) | async-done | bytes 2097168 | tf_op jit(solution)/shard_map/reduce_scatter | solution.py:331
  1676.8 131.6 %reduce-scatter.16.cloned.1.call-done = f32[32,32]{1,0:T(8,128)} async-done(((f32[1024,32]{1,0:T(8,128)}), f32[32,32]{1,0:T(8,128)}) %reduce-scatter.16.cloned.1.call-update) | async-done | bytes 4112 | tf_op jit(solution)/shard_map/reduce_scatter | solution.py:326
  1808.5 140.1 %reduce-scatter.14.cloned.1.call-done = f32[32,1024]{1,0:T(8,128)} async-done(((f32[1024,1024]{1,0:T(8,128)}), f32[32,1024]{1,0:T(8,128)}) %reduce-scatter.14.cloned.1.call-update) | async-done | bytes 131088 | tf_op jit(solution)/shard_map/reduce_scatter | solution.py:322
  1948.6 140.6 %reduce-scatter.10.cloned.1.call-done = f32[32,1024]{1,0:T(8,128)} async-done(((f32[1024,1024]{1,0:T(8,128)}), f32[32,1024]{1,0:T(8,128)}) %reduce-scatter.10.cloned.1.call-update) | async-done | bytes 131088 | tf_op jit(solution)/shard_map/reduce_scatter | solution.py:316
  2089.2 140.7 %reduce-scatter.12.cloned.1.call-done = f32[32,1024]{1,0:T(8,128)} async-done(((f32[1024,1024]{1,0:T(8,128)}), f32[32,1024]{1,0:T(8,128)}) %reduce-scatter.12.cloned.1.call-update) | async-done | bytes 131088 | tf_op jit(solution)/shard_map/reduce_scatter | solution.py:319
  (468 shorter events, 398.1 us)
Async XLA Ops:
  7.2 96.5 %all-gather.2.cloned.1.call-start = ((), (), s32[]{:S(2)}) async-start(), calls=%async_computation.11 | async-start | bytes 5242880 | tf_op jit(solution)/shard_map/all_gather | solution.py:110
  15.2 20.1 copy-start.26
  17.7 14.4 copy-start.13
  36.1 155.9 %copy-start.47 = (s32[4096,1]{0,1:T(1,128)}, s32[4096,1]{0,1:T(1,128)S(1)}, u32[]{:S(2)}) copy-start(s32[4096,1]{0,1:T(1,128)S(1)} %compare_select_fusion) | copy-start | bytes 49156
  191.1 26.1 %copy-start.44 = (f32[512]{0:T(512)}, f32[512]{0:T(512)S(1)}, u32[]{:S(2)}) copy-start(f32[512]{0:T(512)S(1)} %get-tuple-element.458) | copy-start | bytes 6148
  192.1 25.2 %copy-start.9 = (bf16[512,1024]{1,0:T(8,128)(2,1)}, bf16[512,1024]{1,0:T(8,128)(2,1)S(1)}, u32[]{:S(2)}) copy-start(bf16[512,1024]{1,0:T(8,128)(2,1)S(1)} %multiply_convert_fusion.1) | copy-start | bytes 3145732
  404.5 11.9 copy-start.10
  404.6 11.9 copy-start.37
  404.6 122.1 %all-to-all-start.1 = ((bf16[2,16,160,1024]{3,2,1,0:T(8,128)(2,1)}), bf16[2,16,160,1024]{3,2,1,0:T(8,128)(2,1)}, u32[]{:S(2)}, u32[]{:S(2)}) async-start(bf16[2,16,160,1024]{3,2,1,0:T(8,128)(2,1)} %copy.96), calls=%async_computation.1 | async-start | bytes 20971520 | tf_op jit(solution)/shard_map/all_to_all | solution.py:170
  413.7 139.5 %copy-start.54 = (pred[4096]{0:T(1024)(128)(4,1)}, pred[4096]{0:T(1024)(128)(4,1)S(1)}, u32[]{:S(2)}) copy-start(pred[4096]{0:T(1024)(128)(4,1)S(1)} %compare_and_fusion) | copy-start | bytes 12292
  417.0 109.6 %copy-start.46 = (f32[512]{0:T(512)}, f32[512]{0:T(512)S(1)}, u32[]{:S(2)}) copy-start(f32[512]{0:T(512)S(1)} %reduce_max.21) | copy-start | bytes 6148
  526.6 26.5 %copy-start.17 = (bf16[1,512,1024]{2,1,0:T(8,128)(2,1)S(1)}, bf16[1,512,1024]{2,1,0:T(8,128)(2,1)}, u32[]{:S(2)}) copy-start(bf16[1,512,1024]{2,1,0:T(8,128)(2,1)} %param.29) | copy-start | bytes 3145732
  773.8 10.0 copy-start.38
  773.8 10.1 copy-start.55
  773.8 120.2 %all-to-all-start.3 = ((bf16[2,16,160,1024]{3,2,1,0:T(8,128)(2,1)}), bf16[2,16,160,1024]{3,2,1,0:T(8,128)(2,1)}, u32[]{:S(2)}, u32[]{:S(2)}) async-start(bf16[2,16,160,1024]{3,2,1,0:T(8,128)(2,1)} %copy.99), calls=%async_computation.3 | async-start | bytes 20971520 | tf_op jit(solution)/shard_map/all_to_all | solution.py:222
  781.6 371.2 %reduce-scatter.8.cloned.1.call-start = ((), (), s32[]{:S(2)}) async-start(), calls=%async_computation.12 | async-start | bytes 5242880 | tf_op jit(solution)/shard_map/reduce_scatter | solution.py:284
  783.9 144.2 %copy-start.35 = (bf16[512,32]{0,1:T(8,128)(2,1)}, bf16[512,32]{0,1:T(8,128)(2,1)S(1)}, u32[]{:S(2)}) copy-start(bf16[512,32]{0,1:T(8,128)(2,1)S(1)} %fusion.119) | copy-start | bytes 98308
  1077.4 258.9 %reduce-scatter.20.cloned.1.call-start = ((), (), s32[]{:S(2)}) async-start(), calls=%async_computation.18 | async-start | bytes 17825792 | tf_op jit(solution)/shard_map/reduce_scatter | solution.py:334
  1093.4 579.3 %reduce-scatter.18.cloned.1.call-start = ((), (), s32[]{:S(2)}) async-start(), calls=%async_computation.17 | async-start | bytes 35651584 | tf_op jit(solution)/shard_map/reduce_scatter | solution.py:331
  1118.9 689.6 %reduce-scatter.16.cloned.1.call-start = ((), (), s32[]{:S(2)}) async-start(), calls=%async_computation.16 | async-start | bytes 540672 | tf_op jit(solution)/shard_map/reduce_scatter | solution.py:326
  1121.4 827.2 %reduce-scatter.14.cloned.1.call-start = ((), (), s32[]{:S(2)}) async-start(), calls=%async_computation.15 | async-start | bytes 4325376 | tf_op jit(solution)/shard_map/reduce_scatter | solution.py:322
  1126.8 962.4 %reduce-scatter.10.cloned.1.call-start = ((), (), s32[]{:S(2)}) async-start(), calls=%async_computation.13 | async-start | bytes 4325376 | tf_op jit(solution)/shard_map/reduce_scatter | solution.py:316
  1134.1 1095.7 %reduce-scatter.12.cloned.1.call-start = ((), (), s32[]{:S(2)}) async-start(), calls=%async_computation.14 | async-start | bytes 4325376 | tf_op jit(solution)/shard_map/reduce_scatter | solution.py:319
  1171.0 47.0 %copy-start.49 = (f32[512]{0:T(512)S(1)}, f32[512]{0:T(512)}, u32[]{:S(2)}) copy-start(f32[512]{0:T(512)} %get-tuple-element.455) | copy-start | bytes 6148
  (78 other events, 215.4 us)
Sparse Core Ops, SparseCore 0:
  20.2 83.4 all-gather.1
  1077.5 75.2 reduce-scatter.7
  1157.5 178.8 reduce-scatter.19
  1341.1 331.6 reduce-scatter.17
  1675.5 132.9 reduce-scatter.15
  1811.2 137.3 reduce-scatter.13
  1951.4 137.7 reduce-scatter.9
  2092.0 137.7 reduce-scatter.11
where the time goes:
time: 2240 us
  waiting for transfers between devices  1300 us (58%)
  blocking collectives  297 us (13%)
  matrix products  280 us (12%)
  local copies, waits for them, and re-layouts  219 us (10%)
  other arithmetic  98.6 us (4%)
    reduce_scatter x1, waiting for transfers between devices, on_device(): lax.psum_scatter(gateup_local.astype(jnp.bfloat16), ('context', 'dp'), sc...  334 us
    reduce_scatter x1, waiting for transfers between devices, on_device(): lax.psum_scatter(keyval_local, ('experts', 'context', 'dp'), scatter_dime...  141 us
    reduce_scatter x1, waiting for transfers between devices, on_device(): lax.psum_scatter(query_local, ('experts', 'context', 'dp'), scatter_dimen...  141 us
    reduce_scatter x1, waiting for transfers between devices, on_device(): lax.psum_scatter(out_local, ('experts', 'context', 'dp'), scatter_dimensi...  140 us
    reduce_scatter x1, waiting for transfers between devices, on_device(): lax.psum_scatter(router_local, ('experts', 'context', 'dp'), scatter_dime...  132 us
    all_to_all x1, blocking collectives, on_device(): lax.all_to_all(outgoing.reshape(owners, local_experts, CAP, width), 'expe...  128 us
    all_to_all x1, blocking collectives, on_device(): lax.all_to_all(grad_slots.reshape(owners, local_experts, CAP, width), 'ex...  126 us
    reduce_scatter x1, waiting for transfers between devices, on_device(): lax.psum_scatter(down_local.astype(jnp.bfloat16), ('context', 'dp'), scat...  115 us
  transfers between devices with their start and end apart: 10, of which 10 were waited for; matrix products, arithmetic and copies ran while one was open for 5% of the time, Pallas kernels for 0%

commit v1 on v0

--- a/solution.py
+++ b/solution.py
@@ -1,6 +1,10 @@
+import functools
+
 import jax
 import jax.numpy as jnp
 from jax import lax
+from jax.experimental import pallas as pl
+from jax.experimental.pallas import tpu as pltpu
 from jax.sharding import PartitionSpec as P
 
 KVH = 8
@@ -14,6 +18,9 @@
 
 EPSILON = 1e-06
 MASKED = -1e30
+VMEM_LIMIT = 56 * 1024 * 1024
+F32 = jnp.float32
+BF16 = jnp.bfloat16
 
 
 def rotary_tables(offset, length, head_size):
@@ -49,6 +56,397 @@
         tensor * scaled, axis=-1, keepdims=True
     )
     return (grad_tensor, grad_gain)
+
+
+def hop(value, axis, stride):
+    count = lax.axis_size(axis)
+    return lax.ppermute(value, axis, [(i, i ^ stride) for i in range(count)])
+
+
+def turn(value, axis, step):
+    count = lax.axis_size(axis)
+    return lax.ppermute(value, axis, [(i, (i + step) % count) for i in range(count)])
+
+
+def core_hop(value):
+    return hop(value, "dp", 1)
+
+
+def x_hop(value):
+    return hop(value, "dp", lax.axis_size("dp") // 2)
+
+
+def add_low(*terms):
+    total = terms[0].astype(F32)
+    for term in terms[1:]:
+        total = total + term.astype(F32)
+    return total.astype(BF16)
+
+
+def packed_rows(table, width):
+    experts, tokens = table.shape
+    parts = width // tokens
+    return jnp.transpose(
+        table.reshape(parts, experts // parts, tokens), (1, 0, 2)
+    ).reshape(experts // parts, width)
+
+
+def unpacked_rows(rows, tokens):
+    count, width = rows.shape
+    parts = width // tokens
+    return jnp.transpose(rows.reshape(count, parts, tokens), (1, 0, 2)).reshape(
+        count * parts, tokens
+    )
+
+
+def gather_groups(first, second):
+    owners = lax.axis_size("experts")
+    chips = [(first, second)]
+    from_x = (x_hop(first), x_hop(second))
+    from_y = [(turn(first, "experts", k), turn(second, "experts", k)) for k in range(1, owners)]
+    chips.append(from_x)
+    chips.extend(from_y)
+    for k in range(1, owners):
+        chips.append((x_hop(from_y[k - 1][0]), turn(from_x[1], "experts", k)))
+    return [[chip, (core_hop(chip[0]), core_hop(chip[1]))] for chip in chips]
+
+
+def return_groups(chips):
+    owners = lax.axis_size("experts")
+    sums = [None] * len(chips)
+    order = list(range(owners + 1, 2 * owners)) + list(range(1, owners + 1)) + [0]
+    for number in order:
+        own, other = chips[number]
+        sums[number] = [add_low(own[i], core_hop(other[i])) for i in range(2)]
+    for k in range(1, owners):
+        diagonal = sums[owners + k]
+        sums[1 + k][0] = add_low(sums[1 + k][0], x_hop(diagonal[0]))
+        sums[1][1] = add_low(sums[1][1], turn(diagonal[1], "experts", -k))
+    result = []
+    for i in range(2):
+        total = sums[0][i].astype(F32) + x_hop(sums[1][i]).astype(F32)
+        for k in range(1, owners):
+            total = total + turn(sums[1 + k][i], "experts", -k).astype(F32)
+        result.append(total)
+    return result
+
+
+def expert_place(expert, rows):
+    return lax.div(expert, rows), lax.rem(expert, rows)
+
+
+def picked_row(block, part, row, tokens):
+    chosen = block[:, :tokens]
+    for number in range(1, block.shape[1] // tokens):
+        chosen = jnp.where(part == number, block[:, number * tokens : (number + 1) * tokens], chosen)
+    places = lax.broadcasted_iota(jnp.int32, chosen.shape, 0)
+    return jnp.sum(jnp.where(places == row, chosen, 0.0), axis=0, keepdims=True)
+
+
+def dispatch_kernel(groups, own_experts, place_ref, *refs):
+    sources = refs[: 4 * groups]
+    xs_ref, gus_ref, table_ref = refs[-3:]
+    half = sources[0].shape[0]
+    tokens = 2 * half
+    base = place_ref[0]
+    for number in range(groups):
+        x0, x1, u0, u1 = sources[4 * number : 4 * number + 4]
+        gate_block = x1[half:, :].astype(F32)
+        slot_block = u1[half:, :].astype(F32)
+        picks = []
+        gate_columns = []
+        places = lax.broadcasted_iota(jnp.int32, (CAP, tokens), 0).astype(F32)
+        for e in range(own_experts):
+            part, row = expert_place(base + e, gate_block.shape[0])
+            slot_row = picked_row(slot_block, part, row, tokens)
+            gate_row = picked_row(gate_block, part, row, tokens)
+            table_ref[number, e : e + 1, :] = slot_row
+            table_ref[number, own_experts + e : own_experts + e + 1, :] = gate_row
+            match = places == slot_row
+            picks.append(jnp.where(match, 1.0, 0.0).astype(BF16))
+            gate_columns.append(jnp.sum(jnp.where(match, gate_row, 0.0), axis=1, keepdims=True))
+        pick = jnp.concatenate(picks, axis=0)
+        left, right = pick[:, :half], pick[:, half:]
+        rows = jnp.dot(left, x0[...], preferred_element_type=F32) + jnp.dot(
+            right, x1[:half, :], preferred_element_type=F32
+        )
+        grads = jnp.dot(left, u0[...], preferred_element_type=F32) + jnp.dot(
+            right, u1[:half, :], preferred_element_type=F32
+        )
+        for e in range(own_experts):
+            span = slice(e * CAP, (e + 1) * CAP)
+            xs_ref[e, number] = rows[span].astype(BF16)
+            gus_ref[e, number] = (grads[span] * gate_columns[e]).astype(BF16)
+
+
+def dispatch(place, pair, pairs, own_experts, rows_pieces, grad_pieces, earlier):
+    groups = len(rows_pieces)
+    half, width = rows_pieces[0][0].shape
+    tokens = 2 * half
+    operands = []
+    for rows, grads in zip(rows_pieces, grad_pieces):
+        operands += [rows[0], rows[1], grads[0], grads[1]]
+    whole = lambda array: pl.BlockSpec(array.shape, lambda i, s: (0, 0))
+    slots_shape = (own_experts, pairs * groups, CAP, width)
+    table_shape = (pairs * groups, 2 * own_experts, tokens)
+    slots_block = (own_experts, groups, CAP, width)
+    out_specs = [
+        pl.BlockSpec(slots_block, lambda i, s: (0, pair, 0, 0)),
+        pl.BlockSpec(slots_block, lambda i, s: (0, pair, 0, 0)),
+        pl.BlockSpec((groups, 2 * own_experts, tokens), lambda i, s: (pair, 0, 0)),
+    ]
+    in_specs = [whole(array) for array in operands]
+    aliases = {}
+    if earlier is not None:
+        aliases = {1 + len(operands) + i: i for i in range(3)}
+        in_specs += [pl.BlockSpec(memory_space=pl.ANY)] * 3
+        operands = operands + list(earlier)
+    flops = 2 * 2 * groups * own_experts * CAP * tokens * width
+    return pl.pallas_call(
+        functools.partial(dispatch_kernel, groups, own_experts),
+        out_shape=[
+            jax.ShapeDtypeStruct(slots_shape, BF16),
+            jax.ShapeDtypeStruct(slots_shape, BF16),
+            jax.ShapeDtypeStruct(table_shape, F32),
+        ],
+        grid_spec=pltpu.PrefetchScalarGridSpec(
+            num_scalar_prefetch=1, grid=(1,), in_specs=in_specs, out_specs=out_specs
+        ),
+        input_output_aliases=aliases,
+        compiler_params=pltpu.CompilerParams(vmem_limit_bytes=VMEM_LIMIT),
+        cost_estimate=pl.CostEstimate(
+            flops=flops, bytes_accessed=4 * groups * (tokens + own_experts * CAP) * width, transcendentals=0
+        ),
+        name="dispatch",
+    )(place, *operands)
+
+
+def experts_kernel(chunks, spans, place_ref, xs_ref, gus_ref, up_ref, down_ref, outs_ref, rows_ref, terms_ref,
+                   send_ref, keep_ref, x_all, gu_all, grad_all, hidden_all, piece):
+    step = pl.program_id(0)
+    chunk = xs_ref.shape[1]
+    ff = down_ref.shape[1]
+
+    @pl.when(step < chunks)
+    def _():
+        x = xs_ref[0]
+        gu = gus_ref[0]
+        both = jnp.dot(x, up_ref[0], preferred_element_type=F32)
+        gate_pre, up_pre = both[:, :ff], both[:, ff:]
+        sigmoid = jax.nn.sigmoid(gate_pre)
+        activated = gate_pre * sigmoid
+        hidden = (activated * up_pre).astype(BF16)
+        grad_hidden = lax.dot_general(
+            gu, down_ref[0], (((1,), (1,)), ((), ())), preferred_element_type=F32
+        )
+        terms = jnp.sum(grad_hidden * hidden.astype(F32), axis=1, keepdims=True)
+        terms_ref[...] = jnp.broadcast_to(terms, terms_ref.shape)
+        outs_ref[...] = jnp.dot(hidden, down_ref[0], preferred_element_type=F32).astype(BF16)
+        grad_gate = grad_hidden * up_pre * sigmoid * (1.0 + gate_pre * (1.0 - sigmoid))
+        grad_both = jnp.concatenate(
+            [grad_gate.astype(BF16), (grad_hidden * activated).astype(BF16)], axis=1
+        )
+        rows_ref[...] = lax.dot_general(
+            grad_both, up_ref[0], (((1,), (1,)), ((), ())), preferred_element_type=F32
+        ).astype(BF16)
+        at = pl.ds(pl.multiple_of(step * chunk, chunk), chunk)
+        x_all[at, :] = x
+        gu_all[at, :] = gu
+        grad_all[at, :] = grad_both
+        hidden_all[at, :] = hidden
+
+    @pl.when(step >= chunks)
+    def _():
+        number = step - chunks
+        relative = lax.rem(number, 2) * 2 + jnp.where(number < 2, 1, 0)
+        owner = lax.bitwise_xor(place_ref[1], relative)
+        rows = piece.shape[0]
+        columns = pl.ds(pl.multiple_of(owner * rows, rows), rows)
+        over_rows = (((0,), (0,)), ((), ()))
+        width = grad_all.shape[1]
+        piece[:, :width] = lax.dot_general(
+            x_all[:, columns], grad_all[...], over_rows, preferred_element_type=F32
+        )
+        piece[:, width:] = lax.dot_general(
+            gu_all[:, columns], hidden_all[...], over_rows, preferred_element_type=F32
+        )
+        part = rows // spans
+
+        def put(target):
+            for near in range(spans):
+                wanted = lax.bitwise_xor(place_ref[2], near)
+                at = pl.ds(pl.multiple_of(wanted * part, part), part)
+                target[0, near * part : (near + 1) * part, :] = piece[at, :].astype(BF16)
+
+        @pl.when(number < 2)
+        def _():
+            put(send_ref)
+
+        @pl.when(number >= 2)
+        def _():
+            put(keep_ref)
+
+
+def experts_work(place, number, slots, slot_grads, w_gateup, w_down, contexts, spans):
+    own_experts, total, width = slots.shape
+    ff = w_down.shape[1]
+    chunk = 256
+    chunks = total // chunk
+    rows = width // contexts
+    place = place.at[0].add(number)
+    half = contexts // 2
+    row_block = lambda s, p: (jnp.minimum(s, chunks - 1), 0)
+    slot_block = lambda s, p: (number, jnp.minimum(s, chunks - 1), 0)
+    piece_width = w_gateup.shape[2] + ff
+    flops = 2 * 3 * total * width * 3 * ff
+    return pl.pallas_call(
+        functools.partial(experts_kernel, chunks, spans),
+        out_shape=[
+            jax.ShapeDtypeStruct((total, width), BF16),
+            jax.ShapeDtypeStruct((total, width), BF16),
+            jax.ShapeDtypeStruct((total, 128), F32),
+            jax.ShapeDtypeStruct((half, rows, piece_width), BF16),
+            jax.ShapeDtypeStruct((half, rows, piece_width), BF16),
+        ],
+        grid_spec=pltpu.PrefetchScalarGridSpec(
+            num_scalar_prefetch=1,
+            grid=(chunks + contexts,),
+            in_specs=[
+                pl.BlockSpec((1, chunk, width), slot_block),
+                pl.BlockSpec((1, chunk, width), slot_block),
+                pl.BlockSpec((1,) + w_gateup.shape[1:], lambda s, p: (p[0], 0, 0)),
+                pl.BlockSpec((1,) + w_down.shape[1:], lambda s, p: (p[0], 0, 0)),
+            ],
+            out_specs=[
+                pl.BlockSpec((chunk, width), row_block),
+                pl.BlockSpec((chunk, width), row_block),
+                pl.BlockSpec((chunk, 128), row_block),
+                pl.BlockSpec((1, rows, piece_width), lambda s, p: (jnp.clip(s - chunks, 0, half - 1), 0, 0)),
+                pl.BlockSpec(
+                    (1, rows, piece_width), lambda s, p: (jnp.clip(s - chunks - half, 0, half - 1), 0, 0)
+                ),
+            ],
+            scratch_shapes=[
+                pltpu.VMEM((total, width), BF16),
+                pltpu.VMEM((total, width), BF16),
+                pltpu.VMEM((total, 2 * ff), BF16),
+                pltpu.VMEM((total, ff), BF16),
+                pltpu.VMEM((rows, piece_width), F32),
+            ],
+        ),
+        compiler_params=pltpu.CompilerParams(vmem_limit_bytes=VMEM_LIMIT),
+        cost_estimate=pl.CostEstimate(
+            flops=flops, bytes_accessed=8 * total * width + 12 * width * ff, transcendentals=total * ff
+        ),
+        name="experts",
+    )(place, slots, slot_grads, w_gateup, w_down)
+
+
+def combine_kernel(groups, own_experts, place_ref, table_ref, *refs):
+    outs = refs[:own_experts]
+    rows = refs[own_experts : 2 * own_experts]
+    terms = refs[2 * own_experts : 3 * own_experts]
+    results = refs[3 * own_experts :]
+    tokens = table_ref.shape[2]
+    half = tokens // 2
+    over_rows = (((0,), (0,)), ((), ()))
+    base = place_ref[0]
+    for number in range(groups):
+        mix0, mix1, row0, row1 = results[4 * number : 4 * number + 4]
+        extra_rows = row1.shape[0] - half
+        span = slice(number * CAP, (number + 1) * CAP)
+        places = lax.broadcasted_iota(jnp.int32, (CAP, tokens), 0).astype(F32)
+        extra_places = lax.broadcasted_iota(jnp.int32, (extra_rows, tokens), 0)
+        picks, weighted = [], []
+        extras = [jnp.zeros((extra_rows, tokens), F32) for _ in range(EXPERTS // extra_rows)]
+        for e in range(own_experts):
+            slot_row = table_ref[number, e : e + 1, :]
+            gate_row = table_ref[number, own_experts + e : own_experts + e + 1, :]
+            match = places == slot_row
+            picks.append(jnp.where(match, 1.0, 0.0).astype(BF16))
+            weighted.append(jnp.where(match, gate_row, 0.0).astype(BF16))
+            term_row = jnp.sum(jnp.where(match, terms[e][span, 0:1], 0.0), axis=0, keepdims=True)
+            part, row = expert_place(base + e, extra_rows)
+            for k in range(len(extras)):
+                extras[k] = jnp.where(
+                    jnp.logical_and(extra_places == row, part == k), term_row, extras[k]
+                )
+        pick = jnp.concatenate(picks, axis=0)
+        weights = jnp.concatenate(weighted, axis=0)
+        out_block = jnp.concatenate([ref[span, :] for ref in outs], axis=0)
+        row_block = jnp.concatenate([ref[span, :] for ref in rows], axis=0)
+        mixture = lax.dot_general(weights, out_block, over_rows, preferred_element_type=F32)
+        summed = lax.dot_general(pick, row_block, over_rows, preferred_element_type=F32)
+        mix0[...] = mixture[:half].astype(BF16)
+        mix1[...] = mixture[half:].astype(BF16)
+        row0[...] = summed[:half].astype(BF16)
+        row1[:half, :] = summed[half:].astype(BF16)
+        for k, extra in enumerate(extras):
+            row1[half:, k * tokens : (k + 1) * tokens] = extra.astype(BF16)
+
+
+def combine(place, pair, groups, table, outs, rows, terms, extra_rows):
+    own_experts = len(outs)
+    tokens = table.shape[2]
+    width = outs[0].shape[1]
+    half = tokens // 2
+    piece = lambda count: jax.ShapeDtypeStruct((count, width), BF16)
+    out_shape = [piece(half), piece(half), piece(half), piece(half + extra_rows)] * groups
+    slot_spec = pl.BlockSpec((groups * CAP, width), lambda i, s: (pair, 0))
+    term_spec = pl.BlockSpec((groups * CAP, 128), lambda i, s: (pair, 0))
+    results = pl.pallas_call(
+        functools.partial(combine_kernel, groups, own_experts),
+        out_shape=out_shape,
+        grid_spec=pltpu.PrefetchScalarGridSpec(
+            num_scalar_prefetch=1,
+            grid=(1,),
+            in_specs=[pl.BlockSpec((groups,) + table.shape[1:], lambda i, s: (pair, 0, 0))]
+            + [slot_spec] * (2 * own_experts)
+            + [term_spec] * own_experts,
+            out_specs=[pl.BlockSpec(shape.shape, lambda i, s: (0, 0)) for shape in out_shape],
+        ),
+        compiler_params=pltpu.CompilerParams(vmem_limit_bytes=VMEM_LIMIT),
+        cost_estimate=pl.CostEstimate(
+            flops=4 * groups * own_experts * CAP * tokens * width,
+            bytes_accessed=4 * groups * (tokens + own_experts * CAP) * width,
+            transcendentals=0,
+        ),
+        name="combine",
+    )(place, table, *outs, *rows, *terms)
+    mixtures, sums = [], []
+    for number in range(groups):
+        mix0, mix1, row0, row1 = results[4 * number : 4 * number + 4]
+        mixtures.append((mix0, mix1))
+        sums.append((row0, row1))
+    return mixtures, sums
+
+
+def halved(matrix, axis, stride):
+    bit = jnp.bitwise_and(lax.div(lax.axis_index(axis), stride), 1)
+    kept = lax.dynamic_index_in_dim(matrix, bit, 0, keepdims=False)
+    sent = lax.dynamic_index_in_dim(matrix, 1 - bit, 0, keepdims=False)
+    return kept.astype(F32) + hop(sent.astype(BF16), axis, stride).astype(F32)
+
+
+def summed_rows(matrix):
+    rows, columns = matrix.shape
+    owners, contexts, spans = (lax.axis_size(a) for a in ("experts", "context", "dp"))
+    part = rows // (owners * contexts * spans)
+    count, stride = spans, 1
+    while count > 1:
+        matrix = jnp.moveaxis(matrix.reshape(-1, count // 2, 2, part, columns), 2, 0)
+        matrix = halved(matrix, "dp", stride).reshape(-1, columns)
+        count, stride = count // 2, stride * 2
+    count = owners
+    while count > 1:
+        matrix = halved(matrix.reshape(2, -1, columns), "experts", count // 2)
+        count //= 2
+    count, stride = contexts, 1
+    while count > 1:
+        matrix = jnp.moveaxis(matrix.reshape(count // 2, 2, part, columns), 1, 0)
+        matrix = halved(matrix, "context", stride).reshape(-1, columns)
+        count, stride = count // 2, stride * 2
+    return matrix
 
 
 def on_device(
@@ -65,15 +463,35 @@
     slot_order,
     cotangent,
 ):
+    owners, contexts, spans = (lax.axis_size(a) for a in ("experts", "context", "dp"))
     inputs = decoder_input[0].astype(jnp.float32)
     length = inputs.shape[0]
     width = inputs.shape[1]
+    half = length // 2
     heads = query_weight.shape[1] // HD
     kv_width = keyval_weight.shape[1]
     kv_half = kv_width // 2
     grouped = heads // KVH
     scale = HD ** (-0.5)
-    offset = lax.axis_index("context") * length
+    local_experts = w_gateup.shape[0]
+    own_experts = local_experts // spans
+    y_place, z_place, dp_place = (lax.axis_index(a) for a in ("experts", "context", "dp"))
+
+    ids = top_idx[0].T
+    chosen = jnp.any(ids[None, :, :] == jnp.arange(EXPERTS)[:, None, None], axis=1)
+    rank_order = slot_order[0, 0]
+    earlier = (rank_order[:, None] < rank_order[None, :]).astype(BF16)
+    before = jnp.dot(chosen.astype(BF16), earlier, preferred_element_type=F32)
+    kept = jnp.logical_and(chosen, before < CAP)
+    slot_table = jnp.where(kept, before, -1.0)
+    upstream_low = cotangent[0]
+    upstream = upstream_low.astype(jnp.float32)
+    upstream_groups = gather_groups(
+        upstream_low[:half],
+        jnp.concatenate([upstream_low[half:], packed_rows(slot_table, width).astype(BF16)], axis=0),
+    )
+
+    offset = z_place * length
     cos_table, sin_table = rotary_tables(offset, length, HD)
     normed_rows, inverse_attn = norm_forward(inputs, gain_attn)
     normed_low = normed_rows.astype(jnp.bfloat16)
@@ -135,107 +553,66 @@
     residual_middle = inputs + jnp.dot(attn_low, output_weight, preferred_element_type=jnp.float32)
     normed_moe, inverse_moe = norm_forward(residual_middle, gain_moe)
     moe_low = normed_moe.astype(jnp.bfloat16)
-    logits = jnp.dot(moe_low, w_router, preferred_element_type=jnp.float32)
-    chosen_ids = top_idx[0]
-    chosen_hot = (chosen_ids[:, :, None] == jnp.arange(EXPERTS)[None, None, :]).astype(jnp.int32)
-    chosen_float = chosen_hot.astype(jnp.float32)
-    selected = jnp.sum(logits[:, None, :] * chosen_float, axis=2)
-    gates = jax.nn.softmax(selected, axis=-1)
-    rank_order = slot_order[0, 0]
-    earlier = (rank_order[None, :] < rank_order[:, None]).astype(jnp.int32)
-    before_count = jnp.dot(earlier, jnp.sum(chosen_hot, axis=1))
-    slot_index = jnp.sum(before_count[:, None, :] * chosen_hot, axis=2)
-    kept_pair = slot_index < CAP
-    target = jnp.where(kept_pair, chosen_ids * CAP + slot_index, EXPERTS * CAP).reshape(-1)
-    reading = jnp.minimum(target, EXPERTS * CAP - 1)
-    owners = lax.axis_size("experts")
-    local_experts = w_gateup.shape[0]
-    outgoing = (
-        jnp.zeros((EXPERTS * CAP, width), jnp.bfloat16)
-        .at[target]
-        .set(jnp.repeat(moe_low, TOPK, axis=0), mode="drop")
-    )
-    received = lax.all_to_all(
-        outgoing.reshape(owners, local_experts, CAP, width),
-        "experts",
-        split_axis=0,
-        concat_axis=0,
-        tiled=True,
-    )
-    both = jnp.einsum("nesd,edf->nesf", received, w_gateup, preferred_element_type=jnp.float32)
-    hidden = (jax.nn.silu(both[..., :FF]) * both[..., FF:]).astype(jnp.bfloat16)
-    result = jnp.einsum(
-        "nesf,efd->nesd", hidden, w_down, preferred_element_type=jnp.float32
-    ).astype(jnp.bfloat16)
-    returned = lax.all_to_all(result, "experts", split_axis=0, concat_axis=0, tiled=True).reshape(
-        EXPERTS * CAP, width
-    )
-    picked = jnp.take(returned, reading, axis=0).reshape(length, TOPK, width)
-    gate_kept = jnp.where(kept_pair, gates, 0.0)
-    mixed = jnp.einsum("tk,tkd->td", gate_kept, picked, preferred_element_type=jnp.float32)
-    layer_output = (residual_middle + mixed).astype(jnp.bfloat16)[None]
-    upstream = cotangent[0].astype(jnp.float32)
-    grad_gates = jnp.where(
-        kept_pair,
-        jnp.einsum("td,tkd->tk", upstream, picked, preferred_element_type=jnp.float32),
-        0.0,
-    )
-    pair_grads = (
-        (gate_kept[:, :, None] * upstream[:, None, :])
-        .astype(jnp.bfloat16)
-        .reshape(length * TOPK, width)
-    )
-    grad_slots = (
-        jnp.zeros((EXPERTS * CAP, width), jnp.bfloat16).at[target].set(pair_grads, mode="drop")
-    )
-    grad_arrived = lax.all_to_all(
-        grad_slots.reshape(owners, local_experts, CAP, width),
-        "experts",
-        split_axis=0,
-        concat_axis=0,
-        tiled=True,
-    )
-    gate_pre = both[..., :FF]
-    up_pre = both[..., FF:]
-    sigmoid = jax.nn.sigmoid(gate_pre)
-    activated = gate_pre * sigmoid
-    hidden = (activated * up_pre).astype(jnp.bfloat16)
-    grad_hidden = jnp.einsum(
-        "nesd,efd->nesf", grad_arrived, w_down, preferred_element_type=jnp.float32
-    )
-    down_local = jnp.einsum(
-        "nesf,nesd->efd", hidden, grad_arrived, preferred_element_type=jnp.float32
-    )
-    grad_both = jnp.concatenate(
-        [
-            grad_hidden * up_pre * sigmoid * (1.0 + gate_pre * (1.0 - sigmoid)),
-            grad_hidden * activated,
-        ],
-        axis=-1,
-    ).astype(jnp.bfloat16)
-    gateup_local = jnp.einsum(
-        "nesd,nesf->edf", received, grad_both, preferred_element_type=jnp.float32
-    )
-    grad_rows = jnp.einsum(
-        "nesf,edf->nesd", grad_both, w_gateup, preferred_element_type=jnp.float32
-    ).astype(jnp.bfloat16)
-    rows_back = lax.all_to_all(
-        grad_rows, "experts", split_axis=0, concat_axis=0, tiled=True
-    ).reshape(EXPERTS * CAP, width)
-    back_pairs = jnp.take(rows_back, reading, axis=0).reshape(length, TOPK, width)
-    grad_moe_rows = jnp.einsum(
-        "tk,tkd->td", kept_pair.astype(jnp.float32), back_pairs, preferred_element_type=jnp.float32
-    )
-    grad_selected = gates * (grad_gates - jnp.sum(gates * grad_gates, axis=1, keepdims=True))
-    grad_logits = jnp.sum(grad_selected[:, :, None] * chosen_float, axis=1).astype(jnp.bfloat16)
-    router_local = jnp.einsum("td,te->de", moe_low, grad_logits, preferred_element_type=jnp.float32)
-    grad_moe_rows = grad_moe_rows + jnp.einsum(
-        "te,de->td", grad_logits, w_router, preferred_element_type=jnp.float32
+    logits = lax.dot_general(
+        w_router, moe_low, (((0,), (1,)), ((), ())), preferred_element_type=jnp.float32
+    )
+    top_logit = jnp.max(jnp.where(chosen, logits, MASKED), axis=0, keepdims=True)
+    raised = jnp.where(chosen, jnp.exp(logits - top_logit), 0.0)
+    gates = raised / jnp.sum(raised, axis=0, keepdims=True)
+
+    moe_groups = gather_groups(
+        moe_low[:half],
+        jnp.concatenate([moe_low[half:], packed_rows(gates, width).astype(BF16)], axis=0),
+    )
+    extra_rows = EXPERTS * length // width
+    first_expert = y_place * local_experts + dp_place * own_experts
+    place = jnp.stack([first_expert]).astype(jnp.int32)
+    pairs = len(moe_groups)
+    state = None
+    for pair in range(pairs):
+        state = dispatch(
+            place, pair, pairs, own_experts, moe_groups[pair], upstream_groups[pair], state
+        )
+    slots, slot_grads, table = state
+    total = slots.shape[1] * CAP
+    slots = slots.reshape(own_experts, total, width)
+    slot_grads = slot_grads.reshape(own_experts, total, width)
+    work_place = jnp.stack([dp_place * own_experts, z_place, dp_place]).astype(jnp.int32)
+    outs, rows, terms, finals = [], [], [], []
+    for number in range(own_experts):
+        out, row, term, sent, keep = experts_work(
+            work_place, number, slots, slot_grads, w_gateup, w_down, contexts, spans
+        )
+        outs.append(out)
+        rows.append(row)
+        terms.append(term)
+        arrived = hop(sent, "context", 1)
+        near = add_low(keep[0], arrived[0])
+        far = add_low(keep[1], arrived[1])
+        finals.append(add_low(near, hop(far, "context", 2)))
+    mixtures, sums = [None] * pairs, [None] * pairs
+    for pair in reversed(range(pairs)):
+        mixtures[pair], sums[pair] = combine(
+            place, pair, 2, table, outs, rows, terms, extra_rows
+        )
+    row_total = return_groups(sums)
+    grad_gate_terms = unpacked_rows(row_total[1][half:], length)
+    grad_moe_rows = jnp.concatenate([row_total[0], row_total[1][:half]], axis=0)
+    grad_selected = grad_gate_terms - gates * jnp.sum(grad_gate_terms, axis=0, keepdims=True)
+    grad_logits = grad_selected.astype(BF16)
+    router_local = lax.dot_general(
+        moe_low, grad_logits, (((0,), (1,)), ((), ())), preferred_element_type=jnp.float32
+    )
+    grad_moe_rows = grad_moe_rows + lax.dot_general(
+        grad_logits, w_router, (((0,), (1,)), ((), ())), preferred_element_type=jnp.float32
     )
     grad_middle, gain_moe_local = norm_backward(
         residual_middle, inverse_moe, gain_moe, grad_moe_rows
     )
     grad_middle = grad_middle + upstream
+    mixed = jnp.concatenate(return_groups(mixtures), axis=0)
+    layer_output = (residual_middle + mixed).astype(jnp.bfloat16)[None]
+
     grad_attn = grad_middle.astype(jnp.bfloat16)
     out_local = jnp.einsum("tf,td->fd", attn_low, grad_attn, preferred_element_type=jnp.float32)
     grad_heads = (
@@ -247,7 +624,6 @@
         jnp.sum(grad_heads.astype(jnp.float32) * attention_output, axis=-1), (1, 2, 0)
     )
     grad_queries = jnp.zeros((length, KVH, grouped, HD), jnp.float32)
-    blocks = lax.all_gather(keyval, "context", axis=0, tiled=True).reshape(-1, BLOCK, kv_width)
 
     def back_step(grad_now, block_item):
         block_rows, number = block_item
@@ -280,7 +656,6 @@
         back_step, grad_queries, (blocks, jnp.arange(blocks.shape[0]))
     )
     grad_keyvals = block_grads.reshape(-1, kv_width)
-    grad_queries, grad_keyvals = (grad_queries, grad_keyvals)
     grad_keyval_own = lax.psum_scatter(
         grad_keyvals.astype(jnp.bfloat16), "context", scatter_dimension=0, tiled=True
     ).astype(jnp.float32)
@@ -309,44 +684,48 @@
     )
     grad_inputs, gain_attn_local = norm_backward(inputs, inverse_attn, gain_attn, grad_normed)
     grad_input = (grad_inputs + grad_middle).astype(jnp.bfloat16)[None]
-    dense_sums = (
-        lax.psum_scatter(
-            gain_attn_local, ("experts", "context", "dp"), scatter_dimension=0, tiled=True
-        ),
-        lax.psum_scatter(
-            query_local, ("experts", "context", "dp"), scatter_dimension=0, tiled=True
-        ),
-        lax.psum_scatter(
-            keyval_local, ("experts", "context", "dp"), scatter_dimension=0, tiled=True
-        ),
-        lax.psum_scatter(out_local, ("experts", "context", "dp"), scatter_dimension=0, tiled=True),
-        lax.psum_scatter(
-            gain_moe_local, ("experts", "context", "dp"), scatter_dimension=0, tiled=True
-        ),
-        lax.psum_scatter(
-            router_local, ("experts", "context", "dp"), scatter_dimension=0, tiled=True
-        ),
-    )
-    expert_sums = (
-        lax.psum_scatter(
-            gateup_local.astype(jnp.bfloat16), ("context", "dp"), scatter_dimension=1, tiled=True
-        ).astype(jnp.float32),
-        lax.psum_scatter(
-            down_local.astype(jnp.bfloat16), ("context", "dp"), scatter_dimension=2, tiled=True
-        ).astype(jnp.float32),
-    )
-    summed = tuple(dense_sums) + tuple(expert_sums)
+
+    column = lambda vector, filled: jnp.pad(vector[:, None], ((0, 0), (0, filled - 1)))
+    early = summed_rows(
+        jnp.concatenate([out_local, router_local, column(gain_moe_local, 128 - EXPERTS)], axis=1)
+    )
+    late = summed_rows(
+        jnp.concatenate([query_local, keyval_local, column(gain_attn_local, 128)], axis=1)
+    )
+    grad_out = early[:, :width]
+    grad_router = early[:, width : width + EXPERTS]
+    grad_gain_moe = early[:, width + EXPERTS]
+    grad_query = late[:, : query_local.shape[1]]
+    grad_keyval = late[:, query_local.shape[1] : -128]
+    grad_gain_attn = late[:, -128]
+
+    stacked = jnp.stack(finals)
+    part = stacked.shape[1] // spans
+    across = x_hop(stacked[:, 2 * part :])
+    beside = core_hop(jnp.concatenate([stacked[:, part : 2 * part], across[:, part:]], axis=1))
+    near_blocks = jnp.stack(
+        [stacked[:, :part], beside[:, :part], across[:, :part], beside[:, part:]]
+    )
+    arranged = jnp.concatenate(
+        [
+            lax.dynamic_index_in_dim(near_blocks, jnp.bitwise_xor(dp_place, b), 0, keepdims=False)
+            for b in range(spans)
+        ],
+        axis=0,
+    ).astype(F32)
+    grad_gateup = arranged[:, :, : w_gateup.shape[2]]
+    grad_down = jnp.transpose(arranged[:, :, w_gateup.shape[2] :], (0, 2, 1))
     return (
         layer_output,
         grad_input,
-        summed[0],
-        summed[1],
-        summed[2],
-        summed[3],
-        summed[4],
-        summed[5],
-        summed[6],
-        summed[7],
+        grad_gain_attn,
+        grad_query,
+        grad_keyval,
+        grad_out,
+        grad_gain_moe,
+        grad_router,
+        grad_gateup,
+        grad_down,
     )
 
 

time: 2240 us -> 1050 us (0.47)
  waiting for transfers between devices: 1300 us -> 386 us
  blocking collectives: 297 us -> 0 us
  Pallas kernels: 0 us -> 142 us
  local copies, waits for them, and re-layouts: 219 us -> 126 us
  matrix products: 280 us -> 219 us
  starting transfers between devices: 16.2 us -> 55.1 us
    reduce_scatter x6 -> x0, waiting for transfers between devices: 1000 us -> none  [the longest x1 334 us: on_device(): lax.psum_scatter(gateup_local.astype(jnp.bfloat16), ('context', 'dp'), sc...]
    ppermute x0 -> x76, waiting for transfers between devices: none -> 318 us  [the longest x64 268 us: hop(): return lax.ppermute(value, axis, [(i, i ^ stride) for i in range(count)])]
    all_to_all x2 -> x0, blocking collectives: 254 us -> none  [the longest x1 128 us: on_device(): lax.all_to_all(outgoing.reshape(owners, local_experts, CAP, width), 'expe...]
    all_to_all x2 -> x0, waiting for transfers between devices: 212 us -> none  [the longest x1 109 us: on_device(): lax.all_to_all(result, 'experts', split_axis=0, concat_axis=0, tiled=True)]
    dot_general x13 -> x4, matrix products: 155 us -> 3.84 us  [the longest x1 2.77 us: on_device(): lax.dot_general(grad_logits, w_router, (((0,), (1,)), ((), ())), preferre...]
    pallas_call x0 -> x12, Pallas kernels: none -> 142 us  [the longest x4 81.5 us: experts_work(): pl.pallas_call(functools.partial(experts_kernel, chunks, spans), out_shap...]
    ppermute x0 -> x76, starting transfers between devices: none -> 55 us  [the longest x64 42.2 us: hop(): return lax.ppermute(value, axis, [(i, i ^ stride) for i in range(count)])]
    gather x2 -> x0, local copies, waits for them, and re-layouts: 53.1 us -> none  [the longest x1 26.6 us: on_device(): jnp.take(rows_back, reading, axis=0).reshape(length, TOPK, width)]
  transfers between devices with their start and end apart: 10 -> 78, of which waited for: 10 -> 31; matrix products, arithmetic and copies ran while one was open for 5% -> 38% of each run, Pallas kernels for 0% -> 4%
where the time goes in v1:
time: 1050 us; the launch traced here: 1040 us
  waiting for transfers between devices  386 us (37%)
  matrix products  219 us (21%)
  Pallas kernels  142 us (14%)
  local copies, waits for them, and re-layouts  126 us (12%)
  other arithmetic  82.4 us (8%)
  starting transfers between devices  55.1 us (5%)
  between operations  16 us (2%)
  loops' own time  12.3 us (1%)
    ppermute x64, waiting for transfers between devices, hop(): return lax.ppermute(value, axis, [(i, i ^ stride) for i in range(count)])  268 us
    pallas_call x4, Pallas kernels, experts_work(): pl.pallas_call(functools.partial(experts_kernel, chunks, spans), out_shap...  81.5 us
    all_gather x1, waiting for transfers between devices, on_device(): lax.all_gather(keyval, 'context', axis=0, tiled=True)  68.3 us
    dot_general x8, matrix products, attend_step(): jnp.einsum('hgqk,khd->qhgd', weights.astype(jnp.bfloat16), values_part, p...  58.8 us
    ppermute x12, waiting for transfers between devices, turn(): lax.ppermute(value, axis, [(i, (i + step) % count) for i in range(count)])  50 us
    dot_general x16, matrix products, block_scores(): jnp.einsum('qhgd,khd->hgqk', queries, keys_part, preferred_element_type=j...  48 us
    ppermute x64, starting transfers between devices, hop(): return lax.ppermute(value, axis, [(i, i ^ stride) for i in range(count)])  42.2 us
    dot_general x8, matrix products, back_step(): jnp.einsum('hgqk,khd->qhgd', grad_scores, keys_part, preferred_element_ty...  39.4 us
  transfers between devices with their start and end apart: 78, of which 31 were waited for; matrix products, arithmetic and copies ran while one was open for 38% of the time, Pallas kernels for 4%

profile of v1, /device:TPU:0, one launch (start us, length us, event | category | flops | bytes accessed | tf_op | source)
XLA Modules:
  0.0 1039.8 jit_solution(17600729979375705508)
XLA Ops:
  35.4 68.3 %all-gather.2.cloned.1.call-done = bf16[2048,1024]{1,0:T(8,128)(2,1)} async-done(((bf16[512,1024]{1,0:T(8,128)(2,1)}), bf16[2048,1024]{1,0:T(8,128)(2,1)}) %all-gather.2.cloned.1.call-update) | async-done | bytes 4194320 | tf_op jit(solution)/shard_map/all_gather | solution.py:528
  110.1 133.4 %while.36 = (s32[]{:T(128)}, f32[8,2,512]{2,1,0:T(2,128)S(1)}, f32[8,2,512]{2,1,0:T(2,128)S(1)}, f32[512,8,2,64]{0,3,2,1:T(8,128)}, s32[8]{0:T(128)S(1)}, /*inde...) while((s32[]{:T(128)}, f32[8,2,512]{2,1,0:T(2,128)S(1)}, ...), condition=%wide.region_4.5_spmd.clone, body=%wide.region_1.4_spmd.clone.sunk | while | flops 565764608 | bytes 67111272 | solution.py:547
  252.0 10.6 %collective-permute-done.13.refs_3_ = bf16[272,1024]{1,0:T(8,128)(2,1)S(1)} collective-permute-done((bf16[272,1024]{1,0:T(8,128)(2,1)}, bf16[272,1024]{1,0:T(8,128)(2,1)S(1)}, u32[]{:S(2)}, u32[]{:S(2)}) %collective-permute-start.13) | collective-permute-done | bytes 557088 | tf_op jit(solution)/shard_map/ppermute | solution.py:68
  280.8 11.0 %collective-permute-done.2.refs_1_ = bf16[272,1024]{1,0:T(8,128)(2,1)} collective-permute-done((bf16[272,1024]{1,0:T(8,128)(2,1)S(1)}, bf16[272,1024]{1,0:T(8,128)(2,1)}, u32[]{:S(2)}, u32[]{:S(2)}) %collective-permute-start.2) | collective-permute-done | bytes 557088 | tf_op jit(solution)/shard_map/ppermute | solution.py:63
  291.9 8.4 collective-permute-done.refs_0_
  305.4 11.0 %collective-permute-done.1.refs_0_ = bf16[256,1024]{1,0:T(8,128)(2,1)} collective-permute-done((bf16[256,1024]{1,0:T(8,128)(2,1)}, bf16[256,1024]{1,0:T(8,128)(2,1)}, u32[]{:S(2)}, u32[]{:S(2)}) %collective-permute-start.1) | collective-permute-done | bytes 524320 | tf_op jit(solution)/shard_map/ppermute | solution.py:63
  332.8 7.9 dispatch.6
  349.4 20.4 %experts.4 = (bf16[1280,1024]{1,0:T(8,128)(2,1)}, bf16[1280,1024]{1,0:T(8,128)(2,1)}, f32[1280,128]{1,0:T(8,128)}, bf16[2,256,1536]{2,1,0:T(8,128)(2,1)}, bf16[2,256,1536]{2,1,0:T(8,128)(2,1)}) custom-call(s32[3]{0:T(128)} %copy-done.90, bf16[4,1280,1024]{2,1,0:T(8,128)(2,1)} %bitcast.373, bf16[4,1280,1024]{2,1,0:T(8,128)(2,1)} %bitcast.377, ...), custom_call_target="tpu_custom_call" | custom-call | flops 12079595520 | bytes 16777216 | tf_op jit(solution)/shard_map/experts/pallas_call | solution.py:302
  369.8 20.3 %experts.5 = (bf16[1280,1024]{1,0:T(8,128)(2,1)}, bf16[1280,1024]{1,0:T(8,128)(2,1)}, f32[1280,128]{1,0:T(8,128)}, bf16[2,256,1536]{2,1,0:T(8,128)(2,1)}, bf16[2,256,1536]{2,1,0:T(8,128)(2,1)}) custom-call(s32[3]{0:T(128)} %copy-done.93, bf16[4,1280,1024]{2,1,0:T(8,128)(2,1)} %bitcast.374, bf16[4,1280,1024]{2,1,0:T(8,128)(2,1)} %bitcast.378, ...), custom_call_target="tpu_custom_call" | custom-call | flops 12079595520 | bytes 16777216 | tf_op jit(solution)/shard_map/experts/pallas_call | solution.py:302
  390.1 20.4 %experts.6 = (bf16[1280,1024]{1,0:T(8,128)(2,1)}, bf16[1280,1024]{1,0:T(8,128)(2,1)}, f32[1280,128]{1,0:T(8,128)}, bf16[2,256,1536]{2,1,0:T(8,128)(2,1)}, bf16[2,256,1536]{2,1,0:T(8,128)(2,1)}) custom-call(s32[3]{0:T(128)} %copy-done.92, bf16[4,1280,1024]{2,1,0:T(8,128)(2,1)} %bitcast.375, bf16[4,1280,1024]{2,1,0:T(8,128)(2,1)} %bitcast.379, ...), custom_call_target="tpu_custom_call" | custom-call | flops 12079595520 | bytes 16777216 | tf_op jit(solution)/shard_map/experts/pallas_call | solution.py:302
  410.5 20.5 %experts.7 = (bf16[1280,1024]{1,0:T(8,128)(2,1)}, bf16[1280,1024]{1,0:T(8,128)(2,1)}, f32[1280,128]{1,0:T(8,128)}, bf16[2,256,1536]{2,1,0:T(8,128)(2,1)}, bf16[2,256,1536]{2,1,0:T(8,128)(2,1)}) custom-call(s32[3]{0:T(128)} %copy-done.91, bf16[4,1280,1024]{2,1,0:T(8,128)(2,1)} %bitcast.376, bf16[4,1280,1024]{2,1,0:T(8,128)(2,1)} %bitcast.380, ...), custom_call_target="tpu_custom_call" | custom-call | flops 12079595520 | bytes 16777216 | tf_op jit(solution)/shard_map/experts/pallas_call | solution.py:302
  446.6 7.7 combine.6
  473.0 11.0 %collective-permute-done.33 = bf16[256,1024]{1,0:T(8,128)(2,1)S(1)} collective-permute-done((bf16[256,1024]{1,0:T(8,128)(2,1)S(1)}, bf16[256,1024]{1,0:T(8,128)(2,1)S(1)}, u32[]{:S(2)}, u32[]{:S(2)}) %collective-permute-start.33) | collective-permute-done | bytes 524320 | tf_op jit(solution)/shard_map/ppermute | solution.py:63
  486.8 8.5 collective-permute-done.47
  512.1 9.2 collective-permute-done.41
  535.0 8.2 collective-permute-done.55
  556.6 161.2 %while.37 = (s32[]{:T(128)}, f32[512,8,2,64]{0,3,2,1:T(8,128)}, bf16[8,256,1024]{2,1,0:T(8,128)(2,1)}, bf16[8,256,1024]{1,2,0:T(8,128)(2,1)}, s32[8]{0:T(128)S(1...) while((s32[]{:T(128)}, f32[512,8,2,64]{0,3,2,1:T(8,128)}, ...), condition=%wide.region_14.15_spmd.clone, body=%wide.region_13.14_spmd.clone.sunk | while | flops 1370235392 | bytes 73763216 | solution.py:655
  753.7 105.6 %collective-permute-done.67 = bf16[256,1536]{1,0:T(8,128)(2,1)} collective-permute-done((bf16[256,1536]{1,0:T(8,128)(2,1)}, bf16[256,1536]{1,0:T(8,128)(2,1)}, u32[]{:S(2)}, u32[]{:S(2)}) %collective-permute-start.67) | collective-permute-done | bytes 786464 | tf_op jit(solution)/shard_map/ppermute | solution.py:63
  861.0 32.0 %collective-permute-done.69 = bf16[256,1536]{1,0:T(8,128)(2,1)} collective-permute-done((bf16[256,1536]{1,0:T(8,128)(2,1)}, bf16[256,1536]{1,0:T(8,128)(2,1)}, u32[]{:S(2)}, u32[]{:S(2)}) %collective-permute-start.69) | collective-permute-done | bytes 786464 | tf_op jit(solution)/shard_map/ppermute | solution.py:63
  894.7 15.2 %collective-permute-done.71 = bf16[256,1536]{1,0:T(8,128)(2,1)} collective-permute-done((bf16[256,1536]{1,0:T(8,128)(2,1)}, bf16[256,1536]{1,0:T(8,128)(2,1)}, u32[]{:S(2)}, u32[]{:S(2)}) %collective-permute-start.71) | collective-permute-done | bytes 786464 | tf_op jit(solution)/shard_map/ppermute | solution.py:63
  913.6 11.9 %collective-permute-done.73 = bf16[256,1536]{1,0:T(8,128)(2,1)} collective-permute-done((bf16[256,1536]{1,0:T(8,128)(2,1)}, bf16[256,1536]{1,0:T(8,128)(2,1)}, u32[]{:S(2)}, u32[]{:S(2)}) %collective-permute-start.73) | collective-permute-done | bytes 786464 | tf_op jit(solution)/shard_map/ppermute | solution.py:63
  951.6 9.3 copy.80
  980.2 21.8 %collective-permute-done.57 = bf16[8,1,32,2176]{3,2,1,0:T(8,128)(2,1)S(1)} collective-permute-done((bf16[8,1,32,2176]{3,2,1,0:T(8,128)(2,1)S(1)}, bf16[8,1,32,2176]{3,2,1,0:T(8,128)(2,1)S(1)}, u32[]{:S(2)}, u32[]{:S(2)}) %collective-permute-start.57) | collective-permute-done | bytes 1114144 | tf_op jit(solution)/shard_map/ppermute | solution.py:63
  1004.7 11.1 %collective-permute-done.58 = bf16[128,2176]{1,0:T(8,128)(2,1)S(1)} collective-permute-done((bf16[128,2176]{1,0:T(8,128)(2,1)S(1)}, bf16[128,2176]{1,0:T(8,128)(2,1)S(1)}, u32[]{:S(2)}, u32[]{:S(2)}) %collective-permute-start.58) | collective-permute-done | bytes 557088 | tf_op jit(solution)/shard_map/ppermute | solution.py:63
  (729 shorter events, 561.4 us)
Async XLA Ops:
  7.2 96.5 %all-gather.2.cloned.1.call-start = ((), (), s32[]{:S(2)}) async-start(), calls=%async_computation.1 | async-start | bytes 5242880 | tf_op jit(solution)/shard_map/all_gather | solution.py:528
  20.1 912.4 %reduce-scatter.2.cloned.1.call-start = ((), (), s32[]{:S(2)}) async-start(), calls=%async_computation.2 | async-start | bytes 5242880 | tf_op jit(solution)/shard_map/reduce_scatter | solution.py:659
  22.4 227.8 %collective-permute-start.27 = (bf16[272,1024]{1,0:T(8,128)(2,1)}, bf16[272,1024]{1,0:T(8,128)(2,1)}, u32[]{:S(2)}, u32[]{:S(2)}) collective-permute-start(bf16[272,1024]{1,0:T(8,128)(2,1)} %pad_maximum_fusion.10.refs_3_), channel_id=1, source_target_pairs={{0,1},{1,0},{2,3},{3,2},{4,5},{5,4},{6,7},{7,6},{8,9},{9,8},{10,11... | collective-permute-start | bytes 1671176 | tf_op jit(solution)/shard_map/ppermute | solution.py:63
  22.9 229.0 %collective-permute-start.6 = (bf16[272,1024]{1,0:T(8,128)(2,1)}, bf16[272,1024]{1,0:T(8,128)(2,1)}, u32[]{:S(2)}, u32[]{:S(2)}) collective-permute-start(bf16[272,1024]{1,0:T(8,128)(2,1)} %pad_maximum_fusion.10.refs_3_), channel_id=1, source_target_pairs={{0,2},{1,3},{2,0},{3,1},{4,6},{5,7},{6,4},{7,5},{8,10},{9,11},{10,... | collective-permute-start | bytes 1671176 | tf_op jit(solution)/shard_map/ppermute | solution.py:63
  25.4 222.5 %collective-permute-start.26 = (bf16[256,1024]{1,0:T(8,128)(2,1)}, bf16[256,1024]{1,0:T(8,128)(2,1)}, u32[]{:S(2)}, u32[]{:S(2)}) collective-permute-start(bf16[256,1024]{1,0:T(8,128)(2,1)} %get-tuple-element.613.refs_2_), channel_id=1, source_target_pairs={{0,1},{1,0},{2,3},{3,2},{4,5},{5,4},{6,7},{7,6},{8,9},{9,8},{10,11... | collective-permute-start | bytes 1572872 | tf_op jit(solution)/shard_map/ppermute | solution.py:63
  25.6 223.9 %collective-permute-start.19 = (bf16[256,1024]{1,0:T(8,128)(2,1)}, bf16[256,1024]{1,0:T(8,128)(2,1)}, u32[]{:S(2)}, u32[]{:S(2)}) collective-permute-start(bf16[256,1024]{1,0:T(8,128)(2,1)} %get-tuple-element.613.refs_2_), channel_id=1, source_target_pairs={{0,2},{1,3},{2,0},{3,1},{4,6},{5,7},{6,4},{7,5},{8,10},{9,11},{10,... | collective-permute-start | bytes 1572872 | tf_op jit(solution)/shard_map/ppermute | solution.py:63
  25.9 223.6 %collective-permute-start.4 = (bf16[256,1024]{1,0:T(8,128)(2,1)}, bf16[256,1024]{1,0:T(8,128)(2,1)}, u32[]{:S(2)}, u32[]{:S(2)}) collective-permute-start(bf16[256,1024]{1,0:T(8,128)(2,1)} %get-tuple-element.613.refs_2_), channel_id=1, source_target_pairs={{0,16},{16,0},{1,17},{17,1},{2,18},{18,2},{3,19},{19,3},{4,20},{20... | collective-permute-start | bytes 1572872 | tf_op jit(solution)/shard_map/ppermute | solution.py:68
  269.1 32.6 %collective-permute-start.25 = (bf16[272,1024]{1,0:T(8,128)(2,1)S(1)}, bf16[272,1024]{1,0:T(8,128)(2,1)S(1)}, u32[]{:S(2)}, u32[]{:S(2)}) collective-permute-start(bf16[272,1024]{1,0:T(8,128)(2,1)S(1)} %pad_maximum_fusion.9.refs_1_), channel_id=1, source_target_pairs={{0,1},{1,0},{2,3},{3,2},{4,5},{5,4},{6,7},{7,6},{8,9},{9,8},{10,11... | collective-permute-start | bytes 1671176 | tf_op jit(solution)/shard_map/ppermute | solution.py:63
  276.4 25.3 %collective-permute-start.12 = (bf16[272,1024]{1,0:T(8,128)(2,1)S(1)}, bf16[272,1024]{1,0:T(8,128)(2,1)}, u32[]{:S(2)}, u32[]{:S(2)}) collective-permute-start(bf16[272,1024]{1,0:T(8,128)(2,1)S(1)} %pad_maximum_fusion.9.refs_1_), channel_id=1, source_target_pairs={{0,16},{16,0},{1,17},{17,1},{2,18},{18,2},{3,19},{19,3},{4,20},{20... | collective-permute-start | bytes 1671176 | tf_op jit(solution)/shard_map/ppermute | solution.py:68
  304.2 27.7 %collective-permute-start.15 = (bf16[272,1024]{1,0:T(8,128)(2,1)}, bf16[272,1024]{1,0:T(8,128)(2,1)S(1)}, u32[]{:S(2)}, u32[]{:S(2)}) collective-permute-start(bf16[272,1024]{1,0:T(8,128)(2,1)} %collective-permute-done.12.refs_1_), channel_id=1, source_target_pairs={{0,1},{1,0},{2,3},{3,2},{4,5},{5,4},{6,7},{7,6},{8,9},{9,8},{10,11... | collective-permute-start | bytes 1671176 | tf_op jit(solution)/shard_map/ppermute | solution.py:63
  304.9 35.7 %collective-permute-start.10 = (bf16[256,1024]{1,0:T(8,128)(2,1)}, bf16[256,1024]{1,0:T(8,128)(2,1)S(1)}, u32[]{:S(2)}, u32[]{:S(2)}) collective-permute-start(bf16[256,1024]{1,0:T(8,128)(2,1)} %copy-done.63), channel_id=1, source_target_pairs={{0,1},{1,0},{2,3},{3,2},{4,5},{5,4},{6,7},{7,6},{8,9},{9,8},{10,11... | collective-permute-start | bytes 1572872 | tf_op jit(solution)/shard_map/ppermute | solution.py:63
  496.2 25.1 %collective-permute-start.41 = (bf16[256,1024]{1,0:T(8,128)(2,1)S(1)}, bf16[256,1024]{1,0:T(8,128)(2,1)S(1)}, u32[]{:S(2)}, u32[]{:S(2)}) collective-permute-start(bf16[256,1024]{1,0:T(8,128)(2,1)S(1)} %add_convert_fusion.18), channel_id=1, source_target_pairs={{0,16},{16,0},{1,17},{17,1},{2,18},{18,2},{3,19},{19,3},{4,20},{20... | collective-permute-start | bytes 1572872 | tf_op jit(solution)/shard_map/ppermute | solution.py:68
  528.9 188.9 %collective-permute-start.66 = (bf16[2,256,1536]{2,1,0:T(8,128)(2,1)}, bf16[2,256,1536]{2,1,0:T(8,128)(2,1)}, u32[]{:S(2)}, u32[]{:S(2)}) collective-permute-start(bf16[2,256,1536]{2,1,0:T(8,128)(2,1)} %get-tuple-element.415), channel_id=1, source_target_pairs={{0,4},{4,0},{8,12},{12,8},{1,5},{5,1},{9,13},{13,9},{2,6},{6,2},{1... | collective-permute-start | bytes 4718600 | tf_op jit(solution)/shard_map/ppermute | solution.py:63
  532.6 190.1 %collective-permute-start.68 = (bf16[2,256,1536]{2,1,0:T(8,128)(2,1)}, bf16[2,256,1536]{2,1,0:T(8,128)(2,1)}, u32[]{:S(2)}, u32[]{:S(2)}) collective-permute-start(bf16[2,256,1536]{2,1,0:T(8,128)(2,1)} %get-tuple-element.417), channel_id=1, source_target_pairs={{0,4},{4,0},{8,12},{12,8},{1,5},{5,1},{9,13},{13,9},{2,6},{6,2},{1... | collective-permute-start | bytes 4718600 | tf_op jit(solution)/shard_map/ppermute | solution.py:63
  532.9 192.9 %collective-permute-start.70 = (bf16[2,256,1536]{2,1,0:T(8,128)(2,1)}, bf16[2,256,1536]{2,1,0:T(8,128)(2,1)}, u32[]{:S(2)}, u32[]{:S(2)}) collective-permute-start(bf16[2,256,1536]{2,1,0:T(8,128)(2,1)} %get-tuple-element.419), channel_id=1, source_target_pairs={{0,4},{4,0},{8,12},{12,8},{1,5},{5,1},{9,13},{13,9},{2,6},{6,2},{1... | collective-permute-start | bytes 4718600 | tf_op jit(solution)/shard_map/ppermute | solution.py:63
  543.2 187.3 %collective-permute-start.72 = (bf16[2,256,1536]{2,1,0:T(8,128)(2,1)}, bf16[2,256,1536]{2,1,0:T(8,128)(2,1)}, u32[]{:S(2)}, u32[]{:S(2)}) collective-permute-start(bf16[2,256,1536]{2,1,0:T(8,128)(2,1)} %get-tuple-element.421), channel_id=1, source_target_pairs={{0,4},{4,0},{8,12},{12,8},{1,5},{5,1},{9,13},{13,9},{2,6},{6,2},{1... | collective-permute-start | bytes 4718600 | tf_op jit(solution)/shard_map/ppermute | solution.py:63
  720.5 138.8 %collective-permute-start.67 = (bf16[256,1536]{1,0:T(8,128)(2,1)}, bf16[256,1536]{1,0:T(8,128)(2,1)}, u32[]{:S(2)}, u32[]{:S(2)}) collective-permute-start(bf16[256,1536]{1,0:T(8,128)(2,1)} %fusion.84), channel_id=1, source_target_pairs={{0,8},{4,12},{8,0},{12,4},{1,9},{5,13},{9,1},{13,5},{2,10},{6,14},... | collective-permute-start | bytes 2359304 | tf_op jit(solution)/shard_map/ppermute | solution.py:63
  725.2 167.8 %collective-permute-start.69 = (bf16[256,1536]{1,0:T(8,128)(2,1)}, bf16[256,1536]{1,0:T(8,128)(2,1)}, u32[]{:S(2)}, u32[]{:S(2)}) collective-permute-start(bf16[256,1536]{1,0:T(8,128)(2,1)} %fusion.86), channel_id=1, source_target_pairs={{0,8},{4,12},{8,0},{12,4},{1,9},{5,13},{9,1},{13,5},{2,10},{6,14},... | collective-permute-start | bytes 2359304 | tf_op jit(solution)/shard_map/ppermute | solution.py:63
  728.1 181.8 %collective-permute-start.71 = (bf16[256,1536]{1,0:T(8,128)(2,1)}, bf16[256,1536]{1,0:T(8,128)(2,1)}, u32[]{:S(2)}, u32[]{:S(2)}) collective-permute-start(bf16[256,1536]{1,0:T(8,128)(2,1)} %fusion.88), channel_id=1, source_target_pairs={{0,8},{4,12},{8,0},{12,4},{1,9},{5,13},{9,1},{13,5},{2,10},{6,14},... | collective-permute-start | bytes 2359304 | tf_op jit(solution)/shard_map/ppermute | solution.py:63
  732.7 192.8 %collective-permute-start.73 = (bf16[256,1536]{1,0:T(8,128)(2,1)}, bf16[256,1536]{1,0:T(8,128)(2,1)}, u32[]{:S(2)}, u32[]{:S(2)}) collective-permute-start(bf16[256,1536]{1,0:T(8,128)(2,1)} %fusion.90), channel_id=1, source_target_pairs={{0,8},{4,12},{8,0},{12,4},{1,9},{5,13},{9,1},{13,5},{2,10},{6,14},... | collective-permute-start | bytes 2359304 | tf_op jit(solution)/shard_map/ppermute | solution.py:63
  746.2 165.4 %collective-permute-start.61 = (bf16[8,2,32,1152]{3,2,1,0:T(8,128)(2,1)S(1)}, bf16[8,2,32,1152]{3,2,1,0:T(8,128)(2,1)S(1)}, u32[]{:S(2)}, u32[]{:S(2)}) collective-permute-start(bf16[8,2,32,1152]{3,2,1,0:T(8,128)(2,1)S(1)} %fusion.73), channel_id=1, source_target_pairs={{0,1},{1,0},{2,3},{3,2},{4,5},{5,4},{6,7},{7,6},{8,9},{9,8},{10,11... | collective-permute-start | bytes 3538952 | tf_op jit(solution)/shard_map/ppermute | solution.py:63
  928.5 43.7 %collective-permute-start.74 = (bf16[4,128,1536]{2,1,0:T(8,128)(2,1)}, bf16[4,128,1536]{2,1,0:T(8,128)(2,1)}, u32[]{:S(2)}, u32[]{:S(2)}) collective-permute-start(bf16[4,128,1536]{2,1,0:T(8,128)(2,1)} %pad_maximum_fusion.1), channel_id=1, source_target_pairs={{0,2},{1,3},{2,0},{3,1},{4,6},{5,7},{6,4},{7,5},{8,10},{9,11},{10,... | collective-permute-start | bytes 4718600 | tf_op jit(solution)/shard_map/ppermute | solution.py:63
  932.0 31.8 %collective-permute-start.63 = (bf16[128,1152]{1,0:T(8,128)(2,1)}, bf16[128,1152]{1,0:T(8,128)(2,1)}, u32[]{:S(2)}, u32[]{:S(2)}) collective-permute-start(bf16[128,1152]{1,0:T(8,128)(2,1)} %fusion.108), channel_id=1, source_target_pairs={{0,16},{16,0},{1,17},{17,1},{2,18},{18,2},{3,19},{19,3},{4,20},{20... | collective-permute-start | bytes 884744 | tf_op jit(solution)/shard_map/ppermute | solution.py:63
  975.7 26.3 %collective-permute-start.57 = (bf16[8,1,32,2176]{3,2,1,0:T(8,128)(2,1)S(1)}, bf16[8,1,32,2176]{3,2,1,0:T(8,128)(2,1)S(1)}, u32[]{:S(2)}, u32[]{:S(2)}) collective-permute-start(bf16[8,1,32,2176]{3,2,1,0:T(8,128)(2,1)S(1)} %dynamic-slice_convert_fusion.2), channel_id=1, source_target_pairs={{0,2},{1,3},{2,0},{3,1},{4,6},{5,7},{6,4},{7,5},{8,10},{9,11},{10,... | collective-permute-start | bytes 3342344 | tf_op jit(solution)/shard_map/ppermute | solution.py:63
  (185 other events, 2385.0 us)
Sparse Core Ops, SparseCore 0:
  20.2 83.4 all-gather.1
  717.9 161.3 reduce-scatter.1

commit v2 on v0

v2 whole, which is shorter than its diff:
```python
import functools

import jax
import jax.numpy as jnp
from jax import lax
from jax.experimental import pallas as pl
from jax.experimental.pallas import tpu as pltpu
from jax.sharding import PartitionSpec as P

KVH = 8
HD = 64
FF = 512
EXPERTS = 32
TOPK = 8
BLOCK = 256
CAP = 160


EPSILON = 1e-06
MASKED = -1e30
VMEM_LIMIT = 56 * 1024 * 1024
SMALL = pl.CostEstimate(flops=1, bytes_accessed=1, transcendentals=0)
F32 = jnp.float32
BF16 = jnp.bfloat16


def rotary_tables(offset, length, head_size):
    half_size = head_size // 2
    places = (offset + jnp.arange(length)).astype(jnp.float32)
    frequency = 10000.0 ** (-jnp.arange(half_size).astype(jnp.float32) * 2.0 / head_size)
    angles = places[:, None] * frequency[None, :]
    return (jnp.cos(angles)[:, None, :], jnp.sin(angles)[:, None, :])


def rotate(tensor, cos_table, sin_table):
    half_size = tensor.shape[-1] // 2
    first_half = tensor[..., :half_size]
    second_half = tensor[..., half_size:]
    return jnp.concatenate(
        [
            first_half * cos_table - second_half * sin_table,
            second_half * cos_table + first_half * sin_table,
        ],
        axis=-1,
    )


def norm_forward(tensor, gain):
    inverse = lax.rsqrt(jnp.mean(tensor * tensor, axis=-1, keepdims=True) + EPSILON)
    return (tensor * inverse * gain, inverse)


def norm_backward(tensor, inverse, gain, upstream):
    scaled = gain * upstream
    grad_gain = upstream * tensor * inverse
    grad_tensor = inverse * scaled - tensor * inverse**3 * jnp.mean(
        tensor * scaled, axis=-1, keepdims=True
    )
    return (grad_tensor, grad_gain)


def hop(value, axis, stride):
    count = lax.axis_size(axis)
    return lax.ppermute(value, axis, [(i, i ^ stride) for i in range(count)])


def turn(value, axis, step):
    count = lax.axis_size(axis)
    return lax.ppermute(value, axis, [(i, (i + step) % count) for i in range(count)])


def core_hop(value):
    return hop(value, "dp", 1)


def x_hop(value):
    return hop(value, "dp", lax.axis_size("dp") // 2)


def add_low(*terms):
    total = terms[0].astype(F32)
    for term in terms[1:]:
        total = total + term.astype(F32)
    return total.astype(BF16)


def packed_rows(table, width):
    experts, tokens = table.shape
    parts = width // tokens
    return jnp.transpose(
        table.reshape(parts, experts // parts, tokens), (1, 0, 2)
    ).reshape(experts // parts, width)


def unpacked_rows(rows, tokens):
    count, width = rows.shape
    parts = width // tokens
    return jnp.transpose(rows.reshape(count, parts, tokens), (1, 0, 2)).reshape(
        count * parts, tokens
    )


def after(value, *others):
    return lax.optimization_barrier((value, others))[0]


def gather_near(whole):
    owners = lax.axis_size("experts")
    return [x_hop(whole)] + [turn(whole, "experts", k) for k in range(1, owners)]


def gather_far(near, half):
    owners = lax.axis_size("experts")
    return [(x_hop(near[k][:half]), turn(near[0][half:], "experts", k)) for k in range(1, owners)]


def return_far(sums):
    owners = lax.axis_size("experts")
    return [
        (x_hop(sums[owners + k][0]), turn(sums[owners + k][1], "experts", -k)) for k in range(1, owners)
    ]


def far_parts(far, group):
    if group == 1:
        return [(1, pieces[1]) for pieces in far]
    return [(0, far[group - 2][0])]


def return_near(sums):
    owners = lax.axis_size("experts")
    return [x_hop(sums[1])] + [turn(sums[1 + k], "experts", -k) for k in range(1, owners)]


def return_total(own, arrivals):
    total = own.astype(F32)
    for piece in arrivals:
        total = total + piece.astype(F32)
    return total


def picked_row(block, expert, tokens):
    rows = block.shape[0]
    part, row = lax.div(expert, rows), lax.rem(expert, rows)
    chosen = block[:, :tokens]
    for number in range(1, block.shape[1] // tokens):
        chosen = jnp.where(part == number, block[:, number * tokens : (number + 1) * tokens], chosen)
    places = lax.broadcasted_iota(jnp.int32, chosen.shape, 0)
    return jnp.sum(jnp.where(places == row, chosen, 0.0), axis=0, keepdims=True)


def expert_of(place_ref, number, pair_experts):
    own = pair_experts // 2
    return place_ref[0] + number if number < own else place_ref[1] + number - own


def one_hot(slot_row):
    places = lax.broadcasted_iota(jnp.int32, (CAP, slot_row.shape[1]), 0).astype(F32)
    return places == slot_row


def dispatch_kernel(pair_experts, half, pieces, with_gates, place_ref, *refs):
    if pieces == 1:
        first, second = refs[0].at[:half], refs[0].at[half:]
    else:
        first, second = refs[:2]
    if with_gates:
        slots_ref = refs[pieces]
        out_ref, gate_ref, table_ref = refs[-3:]
    else:
        out_ref, table_ref = refs[-2:]
    tokens = 2 * half
    extra = second[half:, :].astype(F32)
    picks = []
    for e in range(pair_experts):
        row = picked_row(extra, expert_of(place_ref, e, pair_experts), tokens)
        table_ref[0, e : e + 1, :] = row
        if with_gates:
            match = one_hot(slots_ref[0, e : e + 1, :])
            gates = jnp.sum(jnp.where(match, row, 0.0), axis=1, keepdims=True)
            gate_ref[e, 0] = jnp.broadcast_to(gates, gate_ref.shape[2:])
        else:
            match = one_hot(row)
        picks.append(jnp.where(match, 1.0, 0.0).astype(BF16))
    pick = jnp.concatenate(picks, axis=0)
    rows = jnp.dot(pick[:, :half], first[...], preferred_element_type=F32) + jnp.dot(
        pick[:, half:], second[:half, :], preferred_element_type=F32
    )
    for e in range(pair_experts):
        out_ref[e, 0] = rows[e * CAP : (e + 1) * CAP].astype(BF16)


def dispatch(place, group, groups, pair_experts, half, pieces, slots, earlier):
    width = pieces[0].shape[1]
    tokens = 2 * half
    whole = lambda array: pl.BlockSpec(array.shape, lambda i, s: (0, 0))
    operands = list(pieces)
    in_specs = [whole(array) for array in operands]
    slots_shape = (pair_experts, groups, CAP, width)
    gate_shape = (pair_experts, groups, CAP, 128)
    table_shape = (groups, pair_experts, tokens)
    table_spec = pl.BlockSpec((1, pair_experts, tokens), lambda i, s: (group, 0, 0))
    out_specs = [pl.BlockSpec((pair_experts, 1, CAP, width), lambda i, s: (0, group, 0, 0))]
    out_shape = [jax.ShapeDtypeStruct(slots_shape, BF16)]
    if slots is not None:
        operands.append(slots)
        in_specs.append(table_spec)
        out_specs.append(pl.BlockSpec((pair_experts, 1, CAP, 128), lambda i, s: (0, group, 0, 0)))
        out_shape.append(jax.ShapeDtypeStruct(gate_shape, F32))
    out_specs.append(table_spec)
    out_shape.append(jax.ShapeDtypeStruct(table_shape, F32))
    aliases = {}
    if earlier is not None:
        aliases = {1 + len(operands) + i: i for i in range(len(earlier))}
        in_specs += [pl.BlockSpec(memory_space=pl.ANY)] * len(earlier)
        operands = operands + list(earlier)
    return pl.pallas_call(
        functools.partial(dispatch_kernel, pair_experts, half, len(pieces), slots is not None),
        out_shape=out_shape,
        grid_spec=pltpu.PrefetchScalarGridSpec(
            num_scalar_prefetch=1, grid=(1,), in_specs=in_specs, out_specs=out_specs
        ),
        input_output_aliases=aliases,
        compiler_params=pltpu.CompilerParams(vmem_limit_bytes=VMEM_LIMIT),
        cost_estimate=SMALL,
        name="dispatch",
    )(place, *operands)


def experts_kernel(slot, chunk, spans, own, place_ref, *refs):
    xs_ref, us_ref, gates_ref, up_ref, down_ref = refs[:5]
    refs = refs[5:]
    arrived_refs = ()
    if own:
        arrived_refs, refs = refs[:2], refs[2:]
    outs_ref, rows_ref, terms_ref = refs[:3]
    pieces_refs = refs[3:5]
    refs = refs[5:]
    x_all, gu_all, gate_all, up_all, down_all, out_all, row_all, term_all, grad_all, hidden_all = refs[:10]
    piece, pieces_all, *arrived_all, load_sems, store_sems = refs[10:]
    total = x_all.shape[0]
    ff = down_all.shape[0]
    sources = [
        (xs_ref.at[slot], x_all),
        (up_ref.at[place_ref[0]], up_all),
        (us_ref.at[slot], gu_all),
        (gates_ref.at[slot], gate_all),
        (down_ref.at[place_ref[0]], down_all),
    ]
    for i, arrived_ref in enumerate(arrived_refs):
        count = arrived_ref.shape[0]
        sources.append((arrived_ref, arrived_all[0].at[pl.ds(i * count, count)]))
    loads = [
        pltpu.make_async_copy(source, target, load_sems.at[i]) for i, (source, target) in enumerate(sources)
    ]
    for load in loads:
        load.start()
    stores = []

    def store(source, target):
        stores.append(pltpu.make_async_copy(source, target, store_sems.at[len(stores)]))
        stores[-1].start()

    loads[0].wait()
    loads[1].wait()
    for number in range(total // chunk):
        span = slice(number * chunk, (number + 1) * chunk)
        at = pl.ds(number * chunk, chunk)
        both = jnp.dot(x_all[span], up_all[...], preferred_element_type=F32)
        if number == 0:
            for load in loads[2:5]:
                load.wait()
        gate_pre, up_pre = both[:, :ff], both[:, ff:]
        gu = (gu_all[span].astype(F32) * gate_all[span, 0:1]).astype(BF16)
        gu_all[span] = gu
        sigmoid = jax.nn.sigmoid(gate_pre)
        activated = gate_pre * sigmoid
        hidden = (activated * up_pre).astype(BF16)
        hidden_all[span] = hidden
        grad_hidden = lax.dot_general(gu, down_all[...], NT, preferred_element_type=F32)
        out_all[span] = jnp.dot(hidden, down_all[...], preferred_element_type=F32).astype(BF16)
        store(out_all.at[at], outs_ref.at[at])
        terms = jnp.sum(grad_hidden * hidden.astype(F32), axis=1, keepdims=True)
        term_all[span] = jnp.broadcast_to(terms, (chunk, term_all.shape[1]))
        store(term_all.at[at], terms_ref.at[at])
        grad_gate = grad_hidden * up_pre * sigmoid * (1.0 + gate_pre * (1.0 - sigmoid))
        grad_both = jnp.concatenate(
            [grad_gate.astype(BF16), (grad_hidden * activated).astype(BF16)], axis=1
        )
        grad_all[span] = grad_both
        row_all[span] = lax.dot_general(
            grad_both, up_all[...], NT, preferred_element_type=F32
        ).astype(BF16)
        store(row_all.at[at], rows_ref.at[at])
    for load in loads[5:]:
        load.wait()
    contexts = pieces_all.shape[0]
    half = contexts // 2
    rows = piece.shape[0]
    part = rows // spans
    over_rows = (((0,), (0,)), ((), ()))
    width = grad_all.shape[1]
    for number in range(contexts):
        relative = (number % half) * 2 + (1 if number < half else 0)
        owner = lax.bitwise_xor(place_ref[1], relative)
        columns = pl.ds(pl.multiple_of(owner * rows, rows), rows)
        piece[:, :width] = lax.dot_general(
            x_all[:, columns], grad_all[...], over_rows, preferred_element_type=F32
        )
        piece[:, width:] = lax.dot_general(
            gu_all[:, columns], hidden_all[...], over_rows, preferred_element_type=F32
        )
        for near in range(spans):
            wanted = lax.bitwise_xor(place_ref[2], near)
            value = piece[pl.ds(pl.multiple_of(wanted * part, part), part), :]
            to = slice(near * part, (near + 1) * part)
            if own:
                value = value + arrived_all[0][number, to, :].astype(F32)
            pieces_all[number, to, :] = value.astype(BF16)
        store(pieces_all.at[number], pieces_refs[number // half].at[number % half])
    for copy in stores:
        copy.wait()


def experts_work(place, slot, slots, slot_grads, slot_gates, w_gateup, w_down, contexts, spans, arrived):
    total, width = slots.shape[1:]
    ff = w_down.shape[1]
    chunk = 2 * CAP
    rows = width // contexts
    half = contexts // 2
    own = arrived is not None
    piece_width = w_gateup.shape[2] + ff
    piece_shape = lambda count: jax.ShapeDtypeStruct((count, rows, piece_width), BF16)
    operands = [slots, slot_grads, slot_gates, w_gateup, w_down]
    out_shape = [
        jax.ShapeDtypeStruct((total, width), BF16),
        jax.ShapeDtypeStruct((total, width), BF16),
        jax.ShapeDtypeStruct((total, 128), F32),
    ]
    scratch = [
        pltpu.VMEM((total, width), BF16),
        pltpu.VMEM((total, width), BF16),
        pltpu.VMEM((total, 128), F32),
        pltpu.VMEM(w_gateup.shape[1:], BF16),
        pltpu.VMEM(w_down.shape[1:], BF16),
        pltpu.VMEM((total, width), BF16),
        pltpu.VMEM((total, width), BF16),
        pltpu.VMEM((total, 128), F32),
        pltpu.VMEM((total, 2 * ff), BF16),
        pltpu.VMEM((total, ff), BF16),
        pltpu.VMEM((rows, piece_width), F32),
        pltpu.VMEM((contexts, rows, piece_width), BF16),
    ]
    out_shape += [piece_shape(half), piece_shape(half)]
    if own:
        operands += list(arrived)
        scratch.append(pltpu.VMEM((contexts, rows, piece_width), BF16))
    scratch.append(pltpu.SemaphoreType.DMA((7,)))
    scratch.append(pltpu.SemaphoreType.DMA((3 * (total // chunk) + contexts,)))
    return pl.pallas_call(
        functools.partial(experts_kernel, slot, chunk, spans, own),
        out_shape=out_shape,
        grid_spec=pltpu.PrefetchScalarGridSpec(
            num_scalar_prefetch=1,
            grid=(1,),
            in_specs=[pl.BlockSpec(memory_space=pl.ANY)] * len(operands),
            out_specs=[pl.BlockSpec(memory_space=pl.ANY)] * len(out_shape),
            scratch_shapes=scratch,
        ),
        compiler_params=pltpu.CompilerParams(vmem_limit_bytes=VMEM_LIMIT),
        cost_estimate=SMALL,
        name="experts",
    )(place, *operands)


def combine_kernel(pair_experts, half, extra_rows, added, results, with_terms, place_ref, slots_ref, *refs):
    scale_ref, terms = None, ()
    if with_terms:
        values = refs[:pair_experts]
        terms = refs[pair_experts : 2 * pair_experts]
        refs = refs[2 * pair_experts :]
    else:
        scale_ref = refs[0]
        values = refs[1 : 1 + pair_experts]
        refs = refs[1 + pair_experts :]
    added_refs = refs[: len(added)]
    if results == 1:
        first, second = refs[-1].at[:half], refs[-1].at[half:]
    else:
        first, second = refs[-2:]
    tokens = 2 * half
    extra_places = lax.broadcasted_iota(jnp.int32, (max(extra_rows, 8), tokens), 0)
    picks = []
    extras = [jnp.zeros(extra_places.shape, F32) for _ in range(first.shape[1] // tokens)]
    for e in range(pair_experts):
        match = one_hot(slots_ref[0, e : e + 1, :])
        if with_terms:
            picks.append(jnp.where(match, 1.0, 0.0).astype(BF16))
            term_row = jnp.sum(jnp.where(match, terms[e][:, 0:1], 0.0), axis=0, keepdims=True)
            expert = expert_of(place_ref, e, pair_experts)
            part, row = lax.div(expert, extra_rows), lax.rem(expert, extra_rows)
            for k in range(len(extras)):
                extras[k] = jnp.where(
                    jnp.logical_and(extra_places == row, part == k), term_row, extras[k]
                )
        else:
            picks.append(jnp.where(match, scale_ref[0, e : e + 1, :], 0.0).astype(BF16))
    pick = jnp.concatenate(picks, axis=0)
    block = jnp.concatenate([ref[...] for ref in values], axis=0)
    summed = lax.dot_general(pick, block, (((0,), (0,)), ((), ())), preferred_element_type=F32)
    halves = [summed[:half], summed[half:]]
    for piece, ref in zip(added, added_refs):
        halves[piece] = halves[piece] + ref[:half, :].astype(F32)
        if with_terms and piece == 1:
            extras = [
                extra + ref[half:, k * tokens : (k + 1) * tokens].astype(F32) for k, extra in enumerate(extras)
            ]
    first[...] = halves[0].astype(BF16)
    second[:half, :] = halves[1].astype(BF16)
    if with_terms:
        for k, extra in enumerate(extras):
            second[half:, k * tokens : (k + 1) * tokens] = extra.astype(BF16)


def combine(place, group, results, slot_table, scales, values, terms, extra_rows, parts=()):
    pair_experts = len(values)
    tokens = slot_table.shape[2]
    width = values[0].shape[1]
    half = tokens // 2
    table_spec = pl.BlockSpec((1,) + slot_table.shape[1:], lambda i, s: (group, 0, 0))
    whole = lambda array: pl.BlockSpec(array.shape, lambda i, s: (0, 0))
    in_specs = [table_spec]
    operands = [slot_table]
    if terms is None:
        in_specs.append(table_spec)
        operands.append(scales)
        extra_rows = 0
    in_specs += [pl.BlockSpec((CAP, width), lambda i, s: (group, 0))] * pair_experts
    operands += values
    if terms is not None:
        in_specs += [pl.BlockSpec((CAP, 128), lambda i, s: (group, 0))] * pair_experts
        operands += terms
    in_specs += [whole(array) for _, array in parts]
    operands += [array for _, array in parts]
    counts = [tokens + extra_rows] if results == 1 else [half, half + extra_rows]
    out_shape = [jax.ShapeDtypeStruct((count, width), BF16) for count in counts]
    result = pl.pallas_call(
        functools.partial(
            combine_kernel,
            pair_experts,
            half,
            extra_rows,
            [piece for piece, _ in parts],
            results,
            terms is not None,
        ),
        out_shape=out_shape,
        grid_spec=pltpu.PrefetchScalarGridSpec(
            num_scalar_prefetch=1,
            grid=(1,),
            in_specs=in_specs,
            out_specs=[whole(shape) for shape in out_shape],
        ),
        compiler_params=pltpu.CompilerParams(vmem_limit_bytes=VMEM_LIMIT),
        cost_estimate=SMALL,
        name="combine",
    )(place, *operands)
    return result[0] if results == 1 else result


NT = (((1,), (1,)), ((), ()))


def attend_kernel(first, last, distance, place_ref, q_ref, k_ref, v_ref, *refs):
    if first:
        state_in, stat_in = None, None
    else:
        state_in, stat_in = refs[:2]
        refs = refs[2:]
    state_ref, stat_ref = refs[:2]
    keys_count = k_ref.shape[0]
    length = q_ref.shape[0]
    heads = q_ref.shape[1] // HD
    grouped = heads // (k_ref.shape[1] // HD)

    def pieces():
        if first:
            return [(slice(b * BLOCK, (b + 1) * BLOCK), slice(0, (b + 1) * BLOCK)) for b in range(length // BLOCK)]
        return [(slice(0, length), slice(0, keys_count))]

    def work():
        turned_values = jnp.transpose(v_ref[...])
        for head in range(heads):
            kv_head = head // grouped
            own = slice(head * HD, (head + 1) * HD)
            shared = slice(kv_head * HD, (kv_head + 1) * HD)
            for q_span, k_span in pieces():
                scores = lax.dot_general(
                    k_ref[k_span, shared], q_ref[q_span, own], NT, preferred_element_type=F32
                )
                top = jnp.max(scores, axis=0, keepdims=True)
                if not first:
                    before = stat_in[0, head : head + 1, q_span]
                    top = jnp.maximum(top, before)
                weights = jnp.exp(scores - top)
                total = jnp.sum(weights, axis=0, keepdims=True)
                update = jnp.dot(
                    turned_values[shared, k_span], weights.astype(BF16), preferred_element_type=F32
                )
                if not first:
                    factor = jnp.exp(before - top)
                    total = total + factor * stat_in[0, heads + head : heads + head + 1, q_span]
                    update = update + factor * state_in[own, q_span]
                stat_ref[0, head : head + 1, q_span] = top
                stat_ref[0, heads + head : heads + head + 1, q_span] = total
                state_ref[own, q_span] = update

    if first:
        work()
    else:
        pl.when(place_ref[0] >= distance)(work)

        @pl.when(place_ref[0] < distance)
        def _():
            state_ref[...] = state_in[...]
            stat_ref[...] = stat_in[...]

    if last:
        low_ref = refs[2]
        for head in range(heads):
            own = slice(head * HD, (head + 1) * HD)
            total = stat_ref[0, heads + head : heads + head + 1, :]
            state_ref[own, :] = state_ref[own, :] / total
            stat_ref[0, head : head + 1, :] = stat_ref[0, head : head + 1, :] + jnp.log(total)
        low_ref[...] = jnp.transpose(state_ref[...]).astype(BF16)


def attend_chunk(place, distance, last, queries, keyval, state):
    length, width = queries.shape
    kv_half = keyval.shape[1] // 2
    pairs = kv_half // 128
    q_columns = width // pairs
    heads = q_columns // HD
    first = state is None
    q_spec = pl.BlockSpec((length, q_columns), lambda i, s: (0, i))
    state_spec = pl.BlockSpec((q_columns, length), lambda i, s: (i, 0))
    stat_spec = pl.BlockSpec((1, 2 * heads, length), lambda i, s: (i, 0, 0))
    in_specs = [
        q_spec,
        pl.BlockSpec((keyval.shape[0], 128), lambda i, s: (0, i)),
        pl.BlockSpec((keyval.shape[0], 128), lambda i, s: (0, pairs + i)),
    ]
    operands = [queries, keyval, keyval]
    out_specs = [state_spec, stat_spec]
    out_shape = [
        jax.ShapeDtypeStruct((width, length), F32),
        jax.ShapeDtypeStruct((pairs, 2 * heads, length), F32),
    ]
    if not first:
        in_specs += [state_spec, stat_spec]
        operands += list(state)
    if last:
        out_specs.append(q_spec)
        out_shape.append(jax.ShapeDtypeStruct((length, width), BF16))
    work = length * keyval.shape[0] * width
    return pl.pallas_call(
        functools.partial(attend_kernel, first, last, distance),
        out_shape=out_shape,
        grid_spec=pltpu.PrefetchScalarGridSpec(
            num_scalar_prefetch=1, grid=(pairs,), in_specs=in_specs, out_specs=out_specs
        ),
        compiler_params=pltpu.CompilerParams(vmem_limit_bytes=VMEM_LIMIT),
        cost_estimate=SMALL,
        name="attend",
    )(place, *operands)


def back_kernel(first, own_chunk, distance, arrives, place_ref, q_ref, k_ref, v_ref, grad_ref, state_ref, stat_ref, *refs):
    arrived_ref = None
    if arrives:
        arrived_ref, refs = refs[0], refs[1:]
    dq_in = None
    if not first:
        dq_in, refs = refs[0], refs[1:]
    dkv_ref, dq_ref = refs
    length = q_ref.shape[0]
    keys_count = k_ref.shape[0]
    heads = q_ref.shape[1] // HD
    kv_heads = k_ref.shape[1] // HD
    grouped = heads // kv_heads

    def work():
        turned_keys = jnp.transpose(k_ref[...])
        turned_grads = jnp.transpose(grad_ref[...].astype(F32))
        if own_chunk:
            pieces = [
                (slice(b * BLOCK, (b + 1) * BLOCK), slice(0, (b + 1) * BLOCK)) for b in range(length // BLOCK)
            ]
        else:
            pieces = [(slice(0, length), slice(0, keys_count))]
        for kv_head in range(kv_heads):
            shared = slice(kv_head * HD, (kv_head + 1) * HD)
            sums = {}
            for head in range(kv_head * grouped, (kv_head + 1) * grouped):
                own = slice(head * HD, (head + 1) * HD)
                row_term = jnp.sum(turned_grads[own, :] * state_ref[own, :], axis=0, keepdims=True)
                for q_span, k_span in pieces:
                    q = q_ref[q_span, own]
                    grad = grad_ref[q_span, own]
                    scores = lax.dot_general(k_ref[k_span, shared], q, NT, preferred_element_type=F32)
                    probs = jnp.exp(scores - stat_ref[0, head : head + 1, q_span])
                    grad_probs = lax.dot_general(v_ref[k_span, shared], grad, NT, preferred_element_type=F32)
                    grad_scores = (probs * (grad_probs - row_term[:, q_span])).astype(BF16)
                    grad_values = jnp.dot(probs.astype(BF16), grad, preferred_element_type=F32)
                    grad_keys = jnp.dot(grad_scores, q, preferred_element_type=F32)
                    blocks = grad_keys.shape[0] // BLOCK
                    for b in range(blocks):
                        part = slice(b * BLOCK, (b + 1) * BLOCK)
                        if b in sums:
                            sums[b] = (sums[b][0] + grad_keys[part], sums[b][1] + grad_values[part])
                        else:
                            sums[b] = (grad_keys[part], grad_values[part])
                    grad_q = jnp.dot(turned_keys[shared, k_span], grad_scores, preferred_element_type=F32)
                    if first:
                        dq_ref[own, q_span] = grad_q
                    else:
                        dq_ref[own, q_span] = dq_in[own, q_span] + grad_q
            for b, pair in sums.items():
                part = slice(b * BLOCK, (b + 1) * BLOCK)
                for i in range(2):
                    value = pair[i]
                    if arrives:
                        value = value + arrived_ref[i, part, shared].astype(F32)
                    dkv_ref[i, part, shared] = value.astype(BF16)

    if own_chunk:
        work()
    else:
        pl.when(place_ref[0] >= distance)(work)

        @pl.when(place_ref[0] < distance)
        def _():
            dkv_ref[...] = jnp.zeros_like(dkv_ref)
            dq_ref[...] = jnp.zeros_like(dq_ref) if first else dq_in[...]


def back_chunk(place, distance, queries, keyval, grad_heads, state, stats, arrived, dq):
    length, width = queries.shape
    kv_half = keyval.shape[1] // 2
    pairs = kv_half // 128
    q_columns = width // pairs
    heads = q_columns // HD
    q_spec = pl.BlockSpec((length, q_columns), lambda i, s: (0, i))
    state_spec = pl.BlockSpec((q_columns, length), lambda i, s: (i, 0))
    stat_spec = pl.BlockSpec((1, 2 * heads, length), lambda i, s: (i, 0, 0))
    dkv_spec = pl.BlockSpec((2, keyval.shape[0], 128), lambda i, s: (0, 0, i))
    in_specs = [
        q_spec,
        pl.BlockSpec((keyval.shape[0], 128), lambda i, s: (0, i)),
        pl.BlockSpec((keyval.shape[0], 128), lambda i, s: (0, pairs + i)),
        q_spec,
        state_spec,
        stat_spec,
    ]
    operands = [queries, keyval, keyval, grad_heads, state, stats]
    if arrived is not None:
        in_specs.append(dkv_spec)
        operands.append(arrived)
    if dq is not None:
        in_specs.append(state_spec)
        operands.append(dq)
    work = length * keyval.shape[0] * width
    return pl.pallas_call(
        functools.partial(back_kernel, dq is None, distance == 0, distance, arrived is not None),
        out_shape=[
            jax.ShapeDtypeStruct((2, keyval.shape[0], kv_half), BF16),
            jax.ShapeDtypeStruct((width, length), F32),
        ],
        grid_spec=pltpu.PrefetchScalarGridSpec(
            num_scalar_prefetch=1, grid=(pairs,), in_specs=in_specs, out_specs=[dkv_spec, state_spec]
        ),
        compiler_params=pltpu.CompilerParams(vmem_limit_bytes=VMEM_LIMIT),
        cost_estimate=SMALL,
        name="back",
    )(place, *operands)


TN = (((0,), (0,)), ((), ()))


def sum_hops():
    owners, contexts, spans = (lax.axis_size(a) for a in ("experts", "context", "dp"))
    hops = []
    for axis, count in (("dp", spans), ("experts", owners), ("context", contexts)):
        bit = 1
        while bit < count:
            hops.append((axis, bit))
            bit *= 2
    return hops


def put_arranged(value, columns, place_ref, plan, plain, arranged, keep_ref, send_ref):
    contexts, spans, masks = plan
    part = value.shape[0] // len(masks)
    half = value.shape[0] // 2
    width = value.shape[1]
    plain[:, :width] = value
    for number, (owner_mask, context_mask, span_mask) in enumerate(masks):
        block = (
            lax.bitwise_xor(place_ref[0], owner_mask) * contexts
            + lax.bitwise_xor(place_ref[1], context_mask)
        ) * spans + lax.bitwise_xor(place_ref[2], span_mask)
        source = pl.ds(pl.multiple_of(block * part, part), part)
        arranged[number * part : (number + 1) * part, :width] = plain[source, :width]
    keep_ref[:, columns] = arranged[:half, :width].astype(BF16)
    send_ref[:, columns] = arranged[half:, :width].astype(BF16)


def sum_plan():
    contexts, spans = lax.axis_size("context"), lax.axis_size("dp")
    hops = sum_hops()
    masks = []
    for number in range(2 ** len(hops)):
        mask = {"experts": 0, "context": 0, "dp": 0}
        for i, (axis, bit) in enumerate(hops):
            if (number >> (len(hops) - 1 - i)) & 1:
                mask[axis] |= bit
        masks.append((mask["experts"], mask["context"], mask["dp"]))
    return contexts, spans, masks


def summed(pair):
    keep, send = pair
    for i, (axis, bit) in enumerate(sum_hops()):
        total = keep.astype(F32) + hop(send, axis, bit).astype(F32)
        rows = total.shape[0] // 2
        if i + 1 == len(sum_hops()):
            return total
        keep, send = total[:rows], total[rows:].astype(BF16)


def turned_back(rows, cos, sin):
    parts = []
    for head in range(rows.shape[0] // HD):
        first = rows[head * HD : head * HD + HD // 2]
        second = rows[head * HD + HD // 2 : (head + 1) * HD]
        parts += [first * cos + second * sin, second * cos - first * sin]
    return jnp.concatenate(parts, axis=0)


STEP = 256


def step_columns():
    step = pl.program_id(0)
    return step, pl.ds(pl.multiple_of(step * STEP, STEP), STEP)


def out_grad_kernel(plan, steps, place_ref, low_ref, grad_ref, moe_ref, logits_ref, gain_ref, keep_ref, send_ref,
                    plain, arranged):
    step, columns = step_columns()

    @pl.when(step < steps)
    def _():
        value = lax.dot_general(low_ref[...], grad_ref[...], TN, preferred_element_type=F32)
        put_arranged(value, columns, place_ref, plan, plain, arranged, keep_ref, send_ref)

    @pl.when(step == steps)
    def _():
        lanes = lax.broadcasted_iota(jnp.int32, logits_ref.shape, 1)
        ones = jnp.where(lanes == EXPERTS, 1.0, 0.0).astype(BF16)
        value = lax.dot_general(moe_ref[...], logits_ref[...], TN, preferred_element_type=F32)
        value = value + lax.dot_general(gain_ref[...], ones, TN, preferred_element_type=F32)
        put_arranged(value, slice(steps * STEP, steps * STEP + 128), place_ref, plan, plain, arranged, keep_ref, send_ref)


def out_grad(place, attn_low, grad_attn, moe_low, grad_logits, gain_terms):
    length, rows = attn_low.shape
    width = grad_attn.shape[1]
    steps = width // STEP
    whole = lambda array: pl.BlockSpec(array.shape, lambda i, s: (0, 0))
    shape = jax.ShapeDtypeStruct((rows // 2, width + 128), BF16)
    return pl.pallas_call(
        functools.partial(out_grad_kernel, sum_plan(), steps),
        out_shape=[shape, shape],
        grid_spec=pltpu.PrefetchScalarGridSpec(
            num_scalar_prefetch=1,
            grid=(steps + 1,),
            in_specs=[
                whole(attn_low),
                pl.BlockSpec((length, STEP), lambda i, s: (0, jnp.minimum(i, steps - 1))),
                whole(moe_low),
                whole(grad_logits),
                whole(gain_terms),
            ],
            out_specs=[whole(shape), whole(shape)],
            scratch_shapes=[pltpu.VMEM((rows, STEP), F32)] * 2,
        ),
        compiler_params=pltpu.CompilerParams(vmem_limit_bytes=VMEM_LIMIT),
        cost_estimate=SMALL,
        name="out_grad",
    )(place, attn_low, grad_attn, moe_low, grad_logits, gain_terms)


def query_grad_kernel(plan, scale, place_ref, dq_ref, cos_ref, sin_ref, low_ref, weight_ref, keep_ref, send_ref,
                      normed_ref, plain, arranged):
    step, columns = step_columns()
    turned = turned_back(dq_ref[...] * scale, cos_ref[...], sin_ref[...])
    low = jnp.transpose(turned).astype(BF16)
    value = lax.dot_general(low_ref[...], low, TN, preferred_element_type=F32)
    put_arranged(value, columns, place_ref, plan, plain, arranged, keep_ref, send_ref)
    part = lax.dot_general(low, weight_ref[...], NT, preferred_element_type=F32)

    @pl.when(step == 0)
    def _():
        normed_ref[...] = part

    @pl.when(step > 0)
    def _():
        normed_ref[...] = normed_ref[...] + part


def query_grad(place, grad_queries, cos, sin, normed_low, query_weight, scale):
    columns, length = grad_queries.shape
    rows = normed_low.shape[1]
    whole = lambda array: pl.BlockSpec(array.shape, lambda i, s: (0, 0))
    shape = jax.ShapeDtypeStruct((rows // 2, columns), BF16)
    normed = jax.ShapeDtypeStruct((length, rows), F32)
    return pl.pallas_call(
        functools.partial(query_grad_kernel, sum_plan(), scale),
        out_shape=[shape, shape, normed],
        grid_spec=pltpu.PrefetchScalarGridSpec(
            num_scalar_prefetch=1,
            grid=(columns // STEP,),
            in_specs=[
                pl.BlockSpec((STEP, length), lambda i, s: (i, 0)),
                whole(cos),
                whole(sin),
                whole(normed_low),
                pl.BlockSpec((rows, STEP), lambda i, s: (0, i)),
            ],
            out_specs=[whole(shape), whole(shape), whole(normed)],
            scratch_shapes=[pltpu.VMEM((rows, STEP), F32)] * 2,
        ),
        compiler_params=pltpu.CompilerParams(vmem_limit_bytes=VMEM_LIMIT),
        cost_estimate=SMALL,
        name="query_grad",
    )(place, grad_queries, cos, sin, normed_low, query_weight)


def keyval_grad_kernel(plan, steps, place_ref, own_ref, arrived_ref, cos_ref, sin_ref, low_ref, weight_ref, part_ref,
                       input_ref, inverse_ref, gain_ref, middle_ref, keep_ref, send_ref, result_ref, total,
                       plain, arranged):
    step, columns = step_columns()

    def take(low):
        value = lax.dot_general(low_ref[...], low, TN, preferred_element_type=F32)
        put_arranged(value, columns, place_ref, plan, plain, arranged, keep_ref, send_ref)
        part = lax.dot_general(low, weight_ref[...], NT, preferred_element_type=F32)

        @pl.when(step == 0)
        def _():
            total[...] = part_ref[...] + part

        @pl.when(step > 0)
        def _():
            total[...] = total[...] + part

    def sum_block():
        return own_ref[0].astype(F32) + arrived_ref[0].astype(F32)

    @pl.when(step < steps // 2)
    def _():
        turned = turned_back(jnp.transpose(sum_block()), cos_ref[...], sin_ref[...])
        take(jnp.transpose(turned).astype(BF16))

    @pl.when(jnp.logical_and(step >= steps // 2, step < steps))
    def _():
        take(sum_block().astype(BF16))

    @pl.when(step == steps)
    def _():
        grad = total[...]
        inputs = input_ref[...].astype(F32)
        inverse = inverse_ref[...][:, 0:1]
        scaled = gain_ref[...] * grad
        mean = jnp.mean(inputs * scaled, axis=1, keepdims=True)
        result = inverse * scaled - inputs * (inverse * inverse * inverse * mean) + middle_ref[...]
        result_ref[...] = result.astype(BF16)
        terms = (grad * inputs * inverse).astype(BF16)
        ones = jnp.ones((terms.shape[0], 128), BF16)
        value = lax.dot_general(terms, ones, TN, preferred_element_type=F32)
        put_arranged(value, slice(steps * STEP, steps * STEP + 128), place_ref, plan, plain, arranged, keep_ref, send_ref)


def keyval_grad(place, own, arrived, cos, sin, normed_low, keyval_weight, part, inputs, inverse, gain, grad_middle):
    length, rows = normed_low.shape
    width = keyval_weight.shape[1]
    steps = width // STEP
    half = steps // 2
    whole = lambda array: pl.BlockSpec(array.shape, lambda i, s: (0,) * len(array.shape))
    shape = jax.ShapeDtypeStruct((rows // 2, width + 128), BF16)
    result = jax.ShapeDtypeStruct((length, rows), BF16)
    at = lambda i: jnp.minimum(i, steps - 1)
    chunk = pl.BlockSpec((1, length, STEP), lambda i, s: (at(i) // half, 0, at(i) % half))
    return pl.pallas_call(
        functools.partial(keyval_grad_kernel, sum_plan(), steps),
        out_shape=[shape, shape, result],
        grid_spec=pltpu.PrefetchScalarGridSpec(
            num_scalar_prefetch=1,
            grid=(steps + 1,),
            in_specs=[
                chunk,
                chunk,
                whole(cos),
                whole(sin),
                whole(normed_low),
                pl.BlockSpec((rows, STEP), lambda i, s: (0, at(i))),
                whole(part),
                whole(inputs),
                whole(inverse),
                whole(gain),
                whole(grad_middle),
            ],
            out_specs=[whole(shape), whole(shape), whole(result)],
            scratch_shapes=[pltpu.VMEM((length, rows), F32)] + [pltpu.VMEM((rows, STEP), F32)] * 2,
        ),
        compiler_params=pltpu.CompilerParams(vmem_limit_bytes=VMEM_LIMIT),
        cost_estimate=SMALL,
        name="keyval_grad",
    )(place, own, arrived, cos, sin, normed_low, keyval_weight, part, inputs, inverse, gain, grad_middle)


def on_device(
    decoder_input,
    gain_attn,
    query_weight,
    keyval_weight,
    output_weight,
    gain_moe,
    w_router,
    w_gateup,
    w_down,
    top_idx,
    slot_order,
    cotangent,
):
    owners, contexts, spans = (lax.axis_size(a) for a in ("experts", "context", "dp"))
    inputs = decoder_input[0].astype(jnp.float32)
    length = inputs.shape[0]
    width = inputs.shape[1]
    half = length // 2
    heads = query_weight.shape[1] // HD
    kv_width = keyval_weight.shape[1]
    kv_half = kv_width // 2
    scale = HD ** (-0.5)
    local_experts = w_gateup.shape[0]
    own_experts = local_experts // spans
    y_place, z_place, dp_place = (lax.axis_index(a) for a in ("experts", "context", "dp"))

    ids = top_idx[0].T
    chosen = jnp.any(ids[None, :, :] == jnp.arange(EXPERTS)[:, None, None], axis=1)
    rank_order = slot_order[0, 0]
    earlier = (rank_order[:, None] < rank_order[None, :]).astype(BF16)
    before = jnp.dot(chosen.astype(BF16), earlier, preferred_element_type=F32)
    kept = jnp.logical_and(chosen, before < CAP)
    slot_table = jnp.where(kept, before, -1.0)
    upstream_low = cotangent[0]
    upstream = upstream_low.astype(jnp.float32)
    pair_experts = 2 * own_experts
    other_core = jnp.bitwise_xor(dp_place, 1)
    expert_place = jnp.stack(
        [
            y_place * local_experts + dp_place * own_experts,
            y_place * local_experts + other_core * own_experts,
        ]
    ).astype(jnp.int32)
    own_upstream = jnp.concatenate([upstream_low, packed_rows(slot_table, width).astype(BF16)], axis=0)

    offset = z_place * length
    cos_table, sin_table = rotary_tables(offset, length, HD)
    cos_rows, sin_rows = (jnp.transpose(table[:, 0]) for table in (cos_table, sin_table))
    sum_place = jnp.stack([y_place, z_place, dp_place]).astype(jnp.int32)
    normed_rows, inverse_attn = norm_forward(inputs, gain_attn)
    normed_low = normed_rows.astype(jnp.bfloat16)
    query_unrotated = jnp.dot(normed_low, query_weight, preferred_element_type=jnp.float32)
    keyval_unrotated = jnp.dot(normed_low, keyval_weight, preferred_element_type=jnp.float32)
    queries = (
        rotate(query_unrotated.reshape(length, heads, HD), cos_table, sin_table)
        .astype(jnp.bfloat16)
        .reshape(length, heads * HD)
    ) * jnp.asarray(scale, BF16)
    keys_turned = rotate(
        keyval_unrotated[:, :kv_half].reshape(length, KVH, HD), cos_table, sin_table
    ).reshape(length, kv_half)
    keyval = jnp.concatenate([keys_turned, keyval_unrotated[:, kv_half:]], axis=1).astype(
        jnp.bfloat16
    )
    z_index = jnp.stack([z_place]).astype(jnp.int32)
    near_upstream = gather_near(own_upstream)
    groups = 2 * owners
    upstream_groups = [(rows,) for rows in [own_upstream] + near_upstream]
    attended, grad_state = None, None
    chunk = keyval
    chunks = [keyval]
    for distance in range(contexts):
        arriving = None
        if distance < contexts - 1:
            upward = [(i, i + 1) for i in range(distance, contexts - 1)]
            arriving = lax.ppermute(chunk, "context", upward)
        attended = attend_chunk(
            z_index,
            distance,
            distance == contexts - 1,
            queries,
            chunk,
            None if attended is None else attended[:2],
        )
        if arriving is not None:
            if distance == 1 or contexts < 3:
                near_upstream = after(near_upstream, attended[1])
                upstream_groups = upstream_groups[:groups] + gather_far(near_upstream, half)
            for group in range(groups):
                if group * (contexts - 1) // groups == distance:
                    pieces = after(upstream_groups[group], attended[1])
                    grad_state = dispatch(
                        expert_place, group, groups, pair_experts, half, pieces, None, grad_state
                    )
            chunk, attended, grad_state = lax.optimization_barrier((arriving, attended, grad_state))
            chunks.append(chunk)
    attention_output, attention_stats, attn_low = attended
    slot_grads, slot_rows = grad_state
    residual_middle = inputs + jnp.dot(attn_low, output_weight, preferred_element_type=jnp.float32)
    normed_moe, inverse_moe = norm_forward(residual_middle, gain_moe)
    moe_low = normed_moe.astype(jnp.bfloat16)
    logits = lax.dot_general(
        w_router, moe_low, (((0,), (1,)), ((), ())), preferred_element_type=jnp.float32
    )
    top_logit = jnp.max(jnp.where(chosen, logits, MASKED), axis=0, keepdims=True)
    raised = jnp.where(chosen, jnp.exp(logits - top_logit), 0.0)
    gates = raised / jnp.sum(raised, axis=0, keepdims=True)

    own_rows = jnp.concatenate([moe_low, packed_rows(gates, width).astype(BF16)], axis=0)
    near_rows = gather_near(own_rows)

    def place_rows(group, pieces, row_state):
        return dispatch(
            expert_place, group, groups, pair_experts, half, pieces, slot_rows, row_state
        )

    row_state = place_rows(0, (own_rows,), None)
    near_rows, row_state = lax.optimization_barrier((near_rows, row_state))
    far_rows = gather_far(near_rows, half)
    for group, rows in enumerate(near_rows):
        row_state = place_rows(1 + group, (rows,), row_state)
    far_rows, row_state = lax.optimization_barrier((far_rows, row_state))
    for group, pieces in enumerate(far_rows):
        row_state = place_rows(1 + owners + group, pieces, row_state)
    slots, slot_gates, gate_rows = row_state
    extra_rows = EXPERTS * length // width
    total = groups * CAP
    slots = slots.reshape(pair_experts, total, width)
    slot_gates = slot_gates.reshape(pair_experts, total, 128)
    slot_grads = slot_grads.reshape(pair_experts, total, width)

    def work(number, own, gate, arrived):
        owner = dp_place if own else other_core
        work_place = jnp.stack([owner * own_experts + number, z_place, owner]).astype(jnp.int32)
        slot = number if own else own_experts + number
        return experts_work(
            work_place,
            slot,
            after(slots, gate),
            slot_grads,
            slot_gates,
            w_gateup,
            w_down,
            contexts,
            spans,
            arrived,
        )

    outs, rows, terms = ([None] * pair_experts for _ in range(3))
    crossing, sent, kept_sums, near_sums, crossed, finals = ([None] * own_experts for _ in range(6))

    def arrive_near(number, gate):
        arrived = after(sent[number], gate)
        near_sums[number] = add_low(kept_sums[number][0], arrived[0])
        crossed[number] = add_low(kept_sums[number][1], arrived[1])
        return crossed[number]

    def cross(number, gate):
        crossed[number] = hop(after(crossed[number], gate), "context", 2)

    def fold_near(number, gate):
        far = arrive_near(number, gate)
        cross(number, far)
        return far

    def exchanged(numbers):
        stacked = jnp.stack([finals[number] for number in numbers])
        part = stacked.shape[1] // spans
        across = x_hop(stacked[:, 2 * part :])
        beside = core_hop(jnp.concatenate([stacked[:, part : 2 * part], across[:, part:]], axis=1))
        return jnp.stack([stacked[:, :part], beside[:, :part], across[:, :part], beside[:, part:]])

    def fold_far(number, gate):
        finals[number] = add_low(near_sums[number], after(crossed[number], gate))
        return finals[number]

    order = [(0, False)]
    for number in range(own_experts):
        if number + 1 < own_experts:
            order.append((number + 1, False))
        order.append((number, True))
    gate = slot_gates
    for number, own in order:
        if own and number == 2:
            gate = fold_near(0, gate)
        slot = number if own else own_experts + number
        result = work(number, own, gate, crossing[number] if own else None)
        outs[slot], rows[slot], terms[slot] = result[:3]
        gate = result[2]
        if own:
            kept_sums[number] = result[4]
            sent[number] = hop(result[3], "context", 1)
        else:
            crossing[number] = (core_hop(result[3]), core_hop(result[4]))

    def near_then(number, value):
        return after(value, fold_near(number, value)) if number < own_experts else value

    def far_then(number, value):
        return after(value, fold_far(number, value)) if number < own_experts else value

    def row_part(group, parts=()):
        results = 2 if group > owners else 1
        return combine(expert_place, group, results, slot_rows, None, rows, terms, extra_rows, parts)

    def mixture_part(group, gate, parts=()):
        results = 2 if group > owners else 1
        return combine(
            expert_place, group, results, after(slot_rows, gate), gate_rows, outs, None, 0, parts
        )

    row_sums, mixtures = [None] * groups, [None] * groups
    far_groups = range(1 + owners, groups)
    near_groups = range(1, 1 + owners)
    for group in far_groups:
        row_sums[group] = row_part(group)
    far_sums = return_far(row_sums)
    row_sums[0] = row_part(0)
    gate = row_sums[0]
    for group in far_groups:
        mixtures[group] = mixture_part(group, gate)
        gate = mixtures[group]
    if own_experts < 3:
        gate = near_then(0, gate)
    gate = near_then(1, gate)
    far_sums = after(far_sums, gate)
    for group in near_groups:
        row_sums[group] = row_part(group, far_parts(far_sums, group))
    arrivals = return_near(row_sums)
    mixtures[0] = mixture_part(0, row_sums[near_groups[-1]])
    arrivals = after(arrivals, mixtures[0])
    arrivals = far_then(0, near_then(2, arrivals))
    row_total = return_total(row_sums[0], arrivals)
    row_total = far_then(1, row_total)
    grad_gate_terms = unpacked_rows(row_total[length:], length)
    grad_moe_rows = row_total[:length]
    grad_selected = grad_gate_terms - gates * jnp.sum(grad_gate_terms, axis=0, keepdims=True)
    grad_logits = grad_selected.astype(BF16)
    grad_moe_rows = grad_moe_rows + lax.dot_general(
        grad_logits, w_router, (((0,), (1,)), ((), ())), preferred_element_type=jnp.float32
    )
    grad_middle, gain_moe_terms = norm_backward(
        residual_middle, inverse_moe, gain_moe, grad_moe_rows
    )
    grad_middle = grad_middle + upstream
    grad_attn = grad_middle.astype(jnp.bfloat16)
    grad_heads = (
        jnp.einsum("td,fd->tf", grad_attn, output_weight, preferred_element_type=jnp.float32)
        .astype(jnp.bfloat16)
    )
    grad_heads = near_then(3, grad_heads)

    def back(distance, grad_heads, arrived, grad_queries):
        return back_chunk(
            z_index,
            distance,
            queries,
            chunks[distance],
            grad_heads,
            attention_output,
            attention_stats,
            arrived,
            grad_queries,
        )

    def down(distance, grad_chunk):
        pairs = [(i, i - 1) for i in range(distance, contexts)]
        return lax.ppermute(grad_chunk, "context", pairs)

    grad_chunk, grad_queries = back(contexts - 1, grad_heads, None, None)
    arrived = down(contexts - 1, grad_chunk)
    for group in far_groups:
        mixtures[group] = after(mixtures[group], grad_chunk)
    far_mixtures = return_far(mixtures)
    own_chunk, grad_queries = back(0, after(grad_heads, grad_chunk), None, grad_queries)
    grad_queries = far_then(2, grad_queries)
    for distance in reversed(range(1, contexts - 1)):
        arrived = after(arrived, grad_queries)
        grad_chunk, grad_queries = back(distance, grad_heads, arrived, grad_queries)
        arrived = down(distance, grad_chunk)
        if distance == contexts - 2:
            for group in near_groups:
                mixtures[group] = mixture_part(group, grad_chunk, far_parts(far_mixtures, group))
            mixture_arrivals = return_near(mixtures)
            grad_queries = far_then(3, grad_queries)
    for number in range(4, own_experts):
        grad_queries = far_then(number, near_then(number, grad_queries))
    arrived = after(arrived, grad_queries)
    mixed = return_total(mixtures[0], mixture_arrivals)
    layer_output = (residual_middle + mixed).astype(jnp.bfloat16)[None]
    early = summed(
        out_grad(
            sum_place,
            attn_low,
            after(grad_attn, own_chunk),
            moe_low,
            jnp.pad(grad_logits.T, ((0, 0), (0, 128 - EXPERTS))),
            gain_moe_terms.astype(BF16),
        )
    )
    *query_sums, grad_normed = query_grad(
        sum_place, grad_queries, cos_rows, sin_rows, normed_low, query_weight, scale
    )
    grad_query = summed(query_sums)
    *keyval_sums, grad_input = keyval_grad(
        sum_place,
        own_chunk,
        arrived,
        cos_rows,
        sin_rows,
        normed_low,
        keyval_weight,
        grad_normed,
        decoder_input[0],
        jnp.broadcast_to(inverse_attn, (length, 128)),
        gain_attn[None, :],
        grad_middle,
    )
    grad_input = grad_input[None]
    late = summed(keyval_sums)
    grad_out = early[:, :width]
    grad_router = early[:, width : width + EXPERTS]
    grad_gain_moe = early[:, width + EXPERTS]
    grad_keyval = late[:, :kv_width]
    grad_gain_attn = late[:, kv_width]

    near_blocks = exchanged(range(own_experts))
    arranged = jnp.concatenate(
        [
            lax.dynamic_index_in_dim(near_blocks, jnp.bitwise_xor(dp_place, b), 0, keepdims=False)
            for b in range(spans)
        ],
        axis=0,
    ).astype(F32)
    grad_gateup = arranged[:, :, : w_gateup.shape[2]]
    grad_down = jnp.transpose(arranged[:, :, w_gateup.shape[2] :], (0, 2, 1))
    return (
        layer_output,
        grad_input,
        grad_gain_attn,
        grad_query,
        grad_keyval,
        grad_out,
        grad_gain_moe,
        grad_router,
        grad_gateup,
        grad_down,
    )


def solution(mesh):
    in_specs = (
        P(("experts", "dp"), "context", None),
        P(),
        P(),
        P(),
        P(),
        P(),
        P(),
        P("experts", None, None),
        P("experts", None, None),
        P(("experts", "dp"), "context", None),
        P(("experts", "dp"), "context", None),
        P(("experts", "dp"), "context", None),
    )
    out_specs = (
        P(("experts", "dp"), "context", None),
        P(("experts", "dp"), "context", None),
        P(("experts", "context", "dp")),
        P(("experts", "context", "dp"), None),
        P(("experts", "context", "dp"), None),
        P(("experts", "context", "dp"), None),
        P(("experts", "context", "dp")),
        P(("experts", "context", "dp"), None),
        P("experts", ("context", "dp"), None),
        P("experts", None, ("context", "dp")),
    )
    return jax.shard_map(
        on_device, mesh=mesh, in_specs=in_specs, out_specs=out_specs, check_vma=False
    )
```

time: 2240 us -> 657 us (0.29)
  waiting for transfers between devices: 1300 us -> 192 us
  blocking collectives: 297 us -> 0 us
  matrix products: 280 us -> 13.9 us
  Pallas kernels: 0 us -> 261 us
  local copies, waits for them, and re-layouts: 219 us -> 33.3 us
  starting transfers between devices: 16.2 us -> 95.9 us
  other arithmetic: 98.6 us -> 48.9 us
    reduce_scatter x7 -> x0, waiting for transfers between devices: 1020 us -> none  [the longest x1 334 us: on_device(): lax.psum_scatter(gateup_local.astype(jnp.bfloat16), ('context', 'dp'), sc...]
    dot_general x74 -> x3, matrix products: 269 us -> 4.51 us  [the longest x1 2.91 us: on_device(): lax.dot_general(grad_logits, w_router, (((0,), (1,)), ((), ())), preferre...]
    pallas_call x0 -> x35, Pallas kernels: none -> 261 us  [the longest x8 95.5 us: experts_work(): pl.pallas_call(functools.partial(experts_kernel, slot, chunk, spans, own)...]
    all_to_all x2 -> x0, blocking collectives: 254 us -> none  [the longest x1 128 us: on_device(): lax.all_to_all(outgoing.reshape(owners, local_experts, CAP, width), 'expe...]
    all_to_all x2 -> x0, waiting for transfers between devices: 212 us -> none  [the longest x1 109 us: on_device(): lax.all_to_all(result, 'experts', split_axis=0, concat_axis=0, tiled=True)]
    ppermute x0 -> x55, waiting for transfers between devices: none -> 192 us  [the longest x41 190 us: hop(): return lax.ppermute(value, axis, [(i, i ^ stride) for i in range(count)])]
    ppermute x0 -> x55, starting transfers between devices: none -> 95.9 us  [the longest x41 74.6 us: hop(): return lax.ppermute(value, axis, [(i, i ^ stride) for i in range(count)])]
    all_gather x1 -> x0, waiting for transfers between devices: 67.6 us -> none  [on_device(): lax.all_gather(keyval, 'context', axis=0, tiled=True)]
  transfers between devices with their start and end apart: 10 -> 55, of which waited for: 10 -> 17; matrix products, arithmetic and copies ran while one was open for 5% -> 11% of each run, Pallas kernels for 0% -> 33%
where the time goes in v2:
time: 657 us; the launch traced here: 647 us
  Pallas kernels  261 us (40%)
  waiting for transfers between devices  192 us (29%)
  starting transfers between devices  95.9 us (15%)
  other arithmetic  48.9 us (7%)
  local copies, waits for them, and re-layouts  33.3 us (5%)
  matrix products  13.9 us (2%)
    ppermute x41, waiting for transfers between devices, hop(): return lax.ppermute(value, axis, [(i, i ^ stride) for i in range(count)])  190 us
    pallas_call x8, Pallas kernels, experts_work(): pl.pallas_call(functools.partial(experts_kernel, slot, chunk, spans, own)...  95.5 us
    ppermute x41, starting transfers between devices, hop(): return lax.ppermute(value, axis, [(i, i ^ stride) for i in range(count)])  74.6 us
    pallas_call x8, Pallas kernels, combine(): pl.pallas_call(functools.partial(combine_kernel, pair_experts, half, extr...  41.3 us
    pallas_call x8, Pallas kernels, dispatch(): pl.pallas_call(functools.partial(dispatch_kernel, pair_experts, half, len...  40.7 us
    pallas_call x4, Pallas kernels, back_chunk(): pl.pallas_call(functools.partial(back_kernel, dq is None, distance == 0,...  29.1 us
    pallas_call x4, Pallas kernels, attend_chunk(): pl.pallas_call(functools.partial(attend_kernel, first, last, distance), o...  24.8 us
    convert_element_type x8, other arithmetic, add_low(): return total.astype(BF16)  14.1 us
  transfers between devices with their start and end apart: 55, of which 17 were waited for; matrix products, arithmetic and copies ran while one was open for 11% of the time, Pallas kernels for 33%

profile of v2, /device:TPU:0, one launch (start us, length us, event | category | flops | bytes accessed | tf_op | source)
XLA Modules:
  0.0 647.2 jit_solution(14254594810964706678)
XLA Ops:
  34.0 11.7 %attend.4 = (f32[1024,512]{1,0:T(8,128)}, f32[4,8,512]{2,1,0:T(8,128)}) custom-call(s32[1]{0:T(128)} %bitcast.1.place_ref, bf16[512,1024]{1,0:T(8,128)(2,1)} %copy.93.q_ref, bf16[512,1024]{1,0:T(8,128)(2,1)} %copy-done.4, bf16[512,1024]{1,0:T(8,128)(2,1)} %copy-done.4), custom_call_target="tpu_custom_call" | custom-call | flops 1 | bytes 1 | tf_op jit(solution)/shard_map/attend/pallas_call | solution.py:566
  107.5 15.6 %collective-permute-done.7.refs_0_ = bf16[528,1024]{1,0:T(8,128)(2,1)S(1)} collective-permute-done((bf16[528,1024]{1,0:T(8,128)(2,1)S(1)}, bf16[528,1024]{1,0:T(8,128)(2,1)S(1)}, u32[]{:S(2)}, u32[]{:S(2)}) %collective-permute-start.7) | collective-permute-done | bytes 1081376 | tf_op jit(solution)/shard_map/ppermute | solution.py:64
  145.1 11.7 %experts.8 = (bf16[640,1024]{1,0:T(8,128)(2,1)}, bf16[640,1024]{1,0:T(8,128)(2,1)}, f32[640,128]{1,0:T(8,128)}, bf16[2,256,1536]{2,1,0:T(8,128)(2,1)}, bf16[2,256,1536]{2,1,0:T(8,128)(2,1)}) custom-call(s32[3]{0:T(128)} %get-tuple-element.364.place_ref, bf16[8,640,1024]{2,1,0:T(8,128)(2,1)} %bitcast.124, bf16[8,640,1024]{2,1,0:T(8,128)(2,1)} %bitcast.132, ...), custom_call_target="tpu_custom_call" | custom-call | flops 1 | bytes 1 | tf_op jit(solution)/shard_map/experts/pallas_call | solution.py:360
  157.4 11.5 %experts.9 = (bf16[640,1024]{1,0:T(8,128)(2,1)}, bf16[640,1024]{1,0:T(8,128)(2,1)}, f32[640,128]{1,0:T(8,128)}, bf16[2,256,1536]{2,1,0:T(8,128)(2,1)}, bf16[2,256,1536]{2,1,0:T(8,128)(2,1)}) custom-call(s32[3]{0:T(128)} %get-tuple-element.363.place_ref, bf16[8,640,1024]{2,1,0:T(8,128)(2,1)} %bitcast.125, bf16[8,640,1024]{2,1,0:T(8,128)(2,1)} %bitcast.133, ...), custom_call_target="tpu_custom_call" | custom-call | flops 1 | bytes 1 | tf_op jit(solution)/shard_map/experts/pallas_call | solution.py:360
  172.4 12.4 %experts.10 = (bf16[640,1024]{1,0:T(8,128)(2,1)}, bf16[640,1024]{1,0:T(8,128)(2,1)}, f32[640,128]{1,0:T(8,128)}, bf16[2,256,1536]{2,1,0:T(8,128)(2,1)}, bf16[2,256,1536]{2,1,0:T(8,128)(2,1)}) custom-call(s32[3]{0:T(128)} %add_add_fusion.place_ref, bf16[8,640,1024]{2,1,0:T(8,128)(2,1)} %bitcast.126, bf16[8,640,1024]{2,1,0:T(8,128)(2,1)} %bitcast.134, ...), custom_call_target="tpu_custom_call" | custom-call | flops 1 | bytes 1 | tf_op jit(solution)/shard_map/experts/pallas_call | solution.py:360
  184.8 14.2 %collective-permute-start.15 = (bf16[2,256,1536]{2,1,0:T(8,128)(2,1)}, bf16[2,256,1536]{2,1,0:T(8,128)(2,1)}, u32[]{:S(2)}, u32[]{:S(2)}) collective-permute-start(bf16[2,256,1536]{2,1,0:T(8,128)(2,1)} %get-tuple-element.246), channel_id=1, source_target_pairs={{0,4},{4,0},{8,12},{12,8},{1,5},{5,1},{9,13},{13,9},{2,6},{6,2},{1... | collective-permute-start | bytes 4718600 | tf_op jit(solution)/shard_map/ppermute | solution.py:64
  200.2 11.5 %experts.11 = (bf16[640,1024]{1,0:T(8,128)(2,1)}, bf16[640,1024]{1,0:T(8,128)(2,1)}, f32[640,128]{1,0:T(8,128)}, bf16[2,256,1536]{2,1,0:T(8,128)(2,1)}, bf16[2,256,1536]{2,1,0:T(8,128)(2,1)}) custom-call(s32[3]{0:T(128)} %get-tuple-element.365.place_ref, bf16[8,640,1024]{2,1,0:T(8,128)(2,1)} %bitcast.127, bf16[8,640,1024]{2,1,0:T(8,128)(2,1)} %bitcast.135, ...), custom_call_target="tpu_custom_call" | custom-call | flops 1 | bytes 1 | tf_op jit(solution)/shard_map/experts/pallas_call | solution.py:360
  211.7 12.2 %experts.12 = (bf16[640,1024]{1,0:T(8,128)(2,1)}, bf16[640,1024]{1,0:T(8,128)(2,1)}, f32[640,128]{1,0:T(8,128)}, bf16[2,256,1536]{2,1,0:T(8,128)(2,1)}, bf16[2,256,1536]{2,1,0:T(8,128)(2,1)}) custom-call(s32[3]{0:T(128)} %add_add_fusion.3.place_ref, bf16[8,640,1024]{2,1,0:T(8,128)(2,1)} %bitcast.128, bf16[8,640,1024]{2,1,0:T(8,128)(2,1)} %bitcast.136, ...), custom_call_target="tpu_custom_call" | custom-call | flops 1 | bytes 1 | tf_op jit(solution)/shard_map/experts/pallas_call | solution.py:360
  224.5 11.7 %experts.13 = (bf16[640,1024]{1,0:T(8,128)(2,1)}, bf16[640,1024]{1,0:T(8,128)(2,1)}, f32[640,128]{1,0:T(8,128)}, bf16[2,256,1536]{2,1,0:T(8,128)(2,1)}, bf16[2,256,1536]{2,1,0:T(8,128)(2,1)}) custom-call(s32[3]{0:T(128)} %get-tuple-element.366.place_ref, bf16[8,640,1024]{2,1,0:T(8,128)(2,1)} %bitcast.129, bf16[8,640,1024]{2,1,0:T(8,128)(2,1)} %bitcast.137, ...), custom_call_target="tpu_custom_call" | custom-call | flops 1 | bytes 1 | tf_op jit(solution)/shard_map/experts/pallas_call | solution.py:360
  240.7 12.0 %experts.14 = (bf16[640,1024]{1,0:T(8,128)(2,1)}, bf16[640,1024]{1,0:T(8,128)(2,1)}, f32[640,128]{1,0:T(8,128)}, bf16[2,256,1536]{2,1,0:T(8,128)(2,1)}, bf16[2,256,1536]{2,1,0:T(8,128)(2,1)}) custom-call(s32[3]{0:T(128)} %add_add_fusion.5.place_ref, bf16[8,640,1024]{2,1,0:T(8,128)(2,1)} %bitcast.130, bf16[8,640,1024]{2,1,0:T(8,128)(2,1)} %bitcast.138, ...), custom_call_target="tpu_custom_call" | custom-call | flops 1 | bytes 1 | tf_op jit(solution)/shard_map/experts/pallas_call | solution.py:360
  252.7 12.5 %experts.15 = (bf16[640,1024]{1,0:T(8,128)(2,1)}, bf16[640,1024]{1,0:T(8,128)(2,1)}, f32[640,128]{1,0:T(8,128)}, bf16[2,256,1536]{2,1,0:T(8,128)(2,1)}, bf16[2,256,1536]{2,1,0:T(8,128)(2,1)}) custom-call(s32[3]{0:T(128)} %add_add_fusion.7.place_ref, bf16[8,640,1024]{2,1,0:T(8,128)(2,1)} %bitcast.131, bf16[8,640,1024]{2,1,0:T(8,128)(2,1)} %bitcast.139, ...), custom_call_target="tpu_custom_call" | custom-call | flops 1 | bytes 1 | tf_op jit(solution)/shard_map/experts/pallas_call | solution.py:360
  273.9 10.6 %collective-permute-done.20.refs_16_ = bf16[256,1024]{1,0:T(8,128)(2,1)S(1)} collective-permute-done((bf16[256,1024]{1,0:T(8,128)(2,1)}, bf16[256,1024]{1,0:T(8,128)(2,1)S(1)}, u32[]{:S(2)}, u32[]{:S(2)}) %collective-permute-start.20) | collective-permute-done | bytes 524320 | tf_op jit(solution)/shard_map/ppermute | solution.py:64
  309.4 13.3 %collective-permute-start.25 = (bf16[256,1536]{1,0:T(8,128)(2,1)}, bf16[256,1536]{1,0:T(8,128)(2,1)}, u32[]{:S(2)}, u32[]{:S(2)}) collective-permute-start(bf16[256,1536]{1,0:T(8,128)(2,1)} %fusion.23), channel_id=1, source_target_pairs={{0,8},{4,12},{8,0},{12,4},{1,9},{5,13},{9,1},{13,5},{2,10},{6,14},... | collective-permute-start | bytes 2359304 | tf_op jit(solution)/shard_map/ppermute | solution.py:64
  332.3 41.6 %collective-permute-done.25 = bf16[256,1536]{1,0:T(8,128)(2,1)} collective-permute-done((bf16[256,1536]{1,0:T(8,128)(2,1)}, bf16[256,1536]{1,0:T(8,128)(2,1)}, u32[]{:S(2)}, u32[]{:S(2)}) %collective-permute-start.25) | collective-permute-done | bytes 786464 | tf_op jit(solution)/shard_map/ppermute | solution.py:64
  377.8 12.0 %collective-permute-done.27 = bf16[256,1536]{1,0:T(8,128)(2,1)} collective-permute-done((bf16[256,1536]{1,0:T(8,128)(2,1)}, bf16[256,1536]{1,0:T(8,128)(2,1)}, u32[]{:S(2)}, u32[]{:S(2)}) %collective-permute-start.27) | collective-permute-done | bytes 786464 | tf_op jit(solution)/shard_map/ppermute | solution.py:64
  407.5 13.0 %back.5 = (bf16[2,512,512]{2,1,0:T(8,128)(2,1)}, f32[1024,512]{1,0:T(8,128)}) custom-call(s32[1]{0:T(128)} %bitcast.1.place_ref, bf16[512,1024]{1,0:T(8,128)(2,1)} %copy.93.q_ref, bf16[512,1024]{1,0:T(8,128)(2,1)} %copy-done.4, bf16[512,1024]{1,0:T(8,128)(2,1)} %copy-done.4, bf16[512,1024]{1,0:T(8,128)(2,1)} %convolution_convert_fusion.grad_ref, ...), custom_call_target="tpu_custom_call" | custom-call | flops 1 | bytes 1 | tf_op jit(solution)/shard_map/back/pallas_call | solution.py:673
  421.2 8.2 %out_grad.1 = (bf16[512,1152]{1,0:T(8,128)(2,1)}, bf16[512,1152]{1,0:T(8,128)(2,1)}) custom-call(s32[3]{0:T(128)} %add_add_fusion.8.place_ref, bf16[512,1024]{1,0:T(8,128)(2,1)} %get-tuple-element.206.low_ref, bf16[512,1024]{1,0:T(8,128)(2,1)} %copy-done.15, bf16[512,1024]{1,0:T(8,128)(2,1)} %copy-done.5, bf16[512,128]{1,0:T(8,128)(2,1)} %pad.4.logits_ref, ...), custom_call_target="tpu_custom_call" | custom-call | flops 1 | bytes 1 | tf_op jit(solution)/shard_map/out_grad/pallas_call | solution.py:783
  436.2 31.7 %collective-permute-done.30 = bf16[256,1536]{1,0:T(8,128)(2,1)} collective-permute-done((bf16[256,1536]{1,0:T(8,128)(2,1)}, bf16[256,1536]{1,0:T(8,128)(2,1)}, u32[]{:S(2)}, u32[]{:S(2)}) %collective-permute-start.30) | collective-permute-done | bytes 786464 | tf_op jit(solution)/shard_map/ppermute | solution.py:64
  479.1 22.0 %collective-permute-done.36 = bf16[256,1536]{1,0:T(8,128)(2,1)S(1)} collective-permute-done((bf16[256,1536]{1,0:T(8,128)(2,1)}, bf16[256,1536]{1,0:T(8,128)(2,1)S(1)}, u32[]{:S(2)}, u32[]{:S(2)}) %collective-permute-start.36) | collective-permute-done | bytes 786464 | tf_op jit(solution)/shard_map/ppermute | solution.py:64
  528.0 8.8 %query_grad.1 = (bf16[512,1024]{1,0:T(8,128)(2,1)}, bf16[512,1024]{1,0:T(8,128)(2,1)}, f32[512,1024]{1,0:T(8,128)}) custom-call(s32[3]{0:T(128)} %add_add_fusion.8.place_ref, f32[1024,512]{1,0:T(8,128)} %get-tuple-element.323.dq_ref, f32[32,512]{1,0:T(8,128)} %get-tuple-element.352.cos_ref, f32[32,512]{1,0:T(8,128)} %get-tuple-element.351.sin_ref, ...), custom_call_target="tpu_custom_call" | custom-call | flops 1 | bytes 1 | tf_op jit(solution)/shard_map/query_grad/pallas_call | solution.py:829
  537.9 8.9 %collective-permute-done.50 = bf16[128,1152]{1,0:T(8,128)(2,1)S(1)} collective-permute-done((bf16[128,1152]{1,0:T(8,128)(2,1)S(1)}, bf16[128,1152]{1,0:T(8,128)(2,1)S(1)}, u32[]{:S(2)}, u32[]{:S(2)}) %collective-permute-start.50) | collective-permute-done | bytes 294944 | tf_op jit(solution)/shard_map/ppermute | solution.py:64
  572.0 7.5 %collective-permute-done.44 = bf16[256,1024]{1,0:T(8,128)(2,1)S(1)} collective-permute-done((bf16[256,1024]{1,0:T(8,128)(2,1)S(1)}, bf16[256,1024]{1,0:T(8,128)(2,1)S(1)}, u32[]{:S(2)}, u32[]{:S(2)}) %collective-permute-start.44) | collective-permute-done | bytes 524320 | tf_op jit(solution)/shard_map/ppermute | solution.py:64
  584.3 12.5 %keyval_grad.1 = (bf16[512,1152]{1,0:T(8,128)(2,1)}, bf16[512,1152]{1,0:T(8,128)(2,1)}, bf16[512,1024]{1,0:T(8,128)(2,1)}) custom-call(s32[3]{0:T(128)} %add_add_fusion.8.place_ref, bf16[2,512,512]{2,1,0:T(8,128)(2,1)} %get-tuple-element.316.own_ref, bf16[2,512,512]{2,1,0:T(8,128)(2,1)} %copy-done.46, f32[32,512]{1,0:T(8,128)} %get-tuple-element.352.cos_ref, ...), custom_call_target="tpu_custom_call" | custom-call | flops 1 | bytes 1 | tf_op jit(solution)/shard_map/keyval_grad/pallas_call | solution.py:906
  612.9 11.0 %collective-permute-done.39 = bf16[256,1152]{1,0:T(8,128)(2,1)S(1)} collective-permute-done((bf16[256,1152]{1,0:T(8,128)(2,1)S(1)}, bf16[256,1152]{1,0:T(8,128)(2,1)S(1)}, u32[]{:S(2)}, u32[]{:S(2)}) %collective-permute-start.39) | collective-permute-done | bytes 589856 | tf_op jit(solution)/shard_map/ppermute | solution.py:64
  (371 shorter events, 306.8 us)
Async XLA Ops:
  5.2 45.5 %collective-permute-start.1 = (bf16[528,1024]{1,0:T(8,128)(2,1)}, bf16[528,1024]{1,0:T(8,128)(2,1)}, u32[]{:S(2)}, u32[]{:S(2)}) collective-permute-start(bf16[528,1024]{1,0:T(8,128)(2,1)} %pad_maximum_fusion.4.refs_0_), channel_id=1, source_target_pairs={{0,2},{1,3},{2,0},{3,1},{4,6},{5,7},{6,4},{7,5},{8,10},{9,11},{10,... | collective-permute-start | bytes 3244040 | tf_op jit(solution)/shard_map/ppermute | solution.py:64
  16.4 39.3 %collective-permute-start = (bf16[512,1024]{1,0:T(8,128)(2,1)S(1)}, bf16[512,1024]{1,0:T(8,128)(2,1)}, u32[]{:S(2)}, u32[]{:S(2)}) collective-permute-start(bf16[512,1024]{1,0:T(8,128)(2,1)S(1)} %pad_maximum_fusion.6.k_ref.v_ref), channel_id=1, source_target_pairs={{0,4},{4,8},{8,12},{1,5},{5,9},{9,13},{2,6},{6,10},{10,14},{3,7},{... | collective-permute-start | bytes 3145736 | tf_op jit(solution)/shard_map/ppermute | solution.py:1010
  20.9 40.3 %collective-permute-start.3 = (bf16[528,1024]{1,0:T(8,128)(2,1)}, bf16[528,1024]{1,0:T(8,128)(2,1)}, u32[]{:S(2)}, u32[]{:S(2)}) collective-permute-start(bf16[528,1024]{1,0:T(8,128)(2,1)} %pad_maximum_fusion.4.refs_0_), channel_id=1, source_target_pairs={{0,16},{16,0},{1,17},{17,1},{2,18},{18,2},{3,19},{19,3},{4,20},{20... | collective-permute-start | bytes 3244040 | tf_op jit(solution)/shard_map/ppermute | solution.py:69
  168.9 42.8 %collective-permute-start.13 = (bf16[2,256,1536]{2,1,0:T(8,128)(2,1)}, bf16[2,256,1536]{2,1,0:T(8,128)(2,1)}, u32[]{:S(2)}, u32[]{:S(2)}) collective-permute-start(bf16[2,256,1536]{2,1,0:T(8,128)(2,1)} %get-tuple-element.242), channel_id=1, source_target_pairs={{0,1},{1,0},{2,3},{3,2},{4,5},{5,4},{6,7},{7,6},{8,9},{9,8},{10,11... | collective-permute-start | bytes 4718600 | tf_op jit(solution)/shard_map/ppermute | solution.py:64
  169.0 42.7 %collective-permute-start.14 = (bf16[2,256,1536]{2,1,0:T(8,128)(2,1)}, bf16[2,256,1536]{2,1,0:T(8,128)(2,1)}, u32[]{:S(2)}, u32[]{:S(2)}) collective-permute-start(bf16[2,256,1536]{2,1,0:T(8,128)(2,1)} %get-tuple-element.243), channel_id=1, source_target_pairs={{0,1},{1,0},{2,3},{3,2},{4,5},{5,4},{6,7},{7,6},{8,9},{9,8},{10,11... | collective-permute-start | bytes 4718600 | tf_op jit(solution)/shard_map/ppermute | solution.py:64
  184.8 53.3 %collective-permute-start.15 = (bf16[2,256,1536]{2,1,0:T(8,128)(2,1)}, bf16[2,256,1536]{2,1,0:T(8,128)(2,1)}, u32[]{:S(2)}, u32[]{:S(2)}) collective-permute-start(bf16[2,256,1536]{2,1,0:T(8,128)(2,1)} %get-tuple-element.246), channel_id=1, source_target_pairs={{0,4},{4,0},{8,12},{12,8},{1,5},{5,1},{9,13},{13,9},{2,6},{6,2},{1... | collective-permute-start | bytes 4718600 | tf_op jit(solution)/shard_map/ppermute | solution.py:64
  238.1 71.3 %collective-permute-start.26 = (bf16[2,256,1536]{2,1,0:T(8,128)(2,1)}, bf16[2,256,1536]{2,1,0:T(8,128)(2,1)S(1)}, u32[]{:S(2)}, u32[]{:S(2)}) collective-permute-start(bf16[2,256,1536]{2,1,0:T(8,128)(2,1)} %get-tuple-element.291), channel_id=1, source_target_pairs={{0,4},{4,0},{8,12},{12,8},{1,5},{5,1},{9,13},{13,9},{2,6},{6,2},{1... | collective-permute-start | bytes 4718600 | tf_op jit(solution)/shard_map/ppermute | solution.py:64
  271.8 59.2 %collective-permute-start.24 = (bf16[2,256,1536]{2,1,0:T(8,128)(2,1)}, bf16[2,256,1536]{2,1,0:T(8,128)(2,1)S(1)}, u32[]{:S(2)}, u32[]{:S(2)}) collective-permute-start(bf16[2,256,1536]{2,1,0:T(8,128)(2,1)} %get-tuple-element.282), channel_id=1, source_target_pairs={{0,4},{4,0},{8,12},{12,8},{1,5},{5,1},{9,13},{13,9},{2,6},{6,2},{1... | collective-permute-start | bytes 4718600 | tf_op jit(solution)/shard_map/ppermute | solution.py:64
  290.6 38.7 %collective-permute-start.23 = (bf16[528,1024]{1,0:T(8,128)(2,1)}, bf16[528,1024]{1,0:T(8,128)(2,1)S(1)}, u32[]{:S(2)}, u32[]{:S(2)}) collective-permute-start(bf16[528,1024]{1,0:T(8,128)(2,1)} %combine.9), channel_id=1, source_target_pairs={{0,16},{16,0},{1,17},{17,1},{2,18},{18,2},{3,19},{19,3},{4,20},{20... | collective-permute-start | bytes 3244040 | tf_op jit(solution)/shard_map/ppermute | solution.py:69
  297.6 33.5 %collective-permute-start.22 = (bf16[528,1024]{1,0:T(8,128)(2,1)}, bf16[528,1024]{1,0:T(8,128)(2,1)}, u32[]{:S(2)}, u32[]{:S(2)}) collective-permute-start(bf16[528,1024]{1,0:T(8,128)(2,1)} %combine.12), channel_id=1, source_target_pairs={{0,2},{1,3},{2,0},{3,1},{4,6},{5,7},{6,4},{7,5},{8,10},{9,11},{10,... | collective-permute-start | bytes 3244040 | tf_op jit(solution)/shard_map/ppermute | solution.py:64
  309.4 64.5 %collective-permute-start.25 = (bf16[256,1536]{1,0:T(8,128)(2,1)}, bf16[256,1536]{1,0:T(8,128)(2,1)}, u32[]{:S(2)}, u32[]{:S(2)}) collective-permute-start(bf16[256,1536]{1,0:T(8,128)(2,1)} %fusion.23), channel_id=1, source_target_pairs={{0,8},{4,12},{8,0},{12,4},{1,9},{5,13},{9,1},{13,5},{2,10},{6,14},... | collective-permute-start | bytes 2359304 | tf_op jit(solution)/shard_map/ppermute | solution.py:64
  323.8 66.0 %collective-permute-start.27 = (bf16[256,1536]{1,0:T(8,128)(2,1)}, bf16[256,1536]{1,0:T(8,128)(2,1)}, u32[]{:S(2)}, u32[]{:S(2)}) collective-permute-start(bf16[256,1536]{1,0:T(8,128)(2,1)} %fusion.27), channel_id=1, source_target_pairs={{0,8},{4,12},{8,0},{12,4},{1,9},{5,13},{9,1},{13,5},{2,10},{6,14},... | collective-permute-start | bytes 2359304 | tf_op jit(solution)/shard_map/ppermute | solution.py:64
  329.3 71.3 %collective-permute-start.28 = (bf16[2,256,1536]{2,1,0:T(8,128)(2,1)}, bf16[2,256,1536]{2,1,0:T(8,128)(2,1)}, u32[]{:S(2)}, u32[]{:S(2)}) collective-permute-start(bf16[2,256,1536]{2,1,0:T(8,128)(2,1)} %get-tuple-element.299), channel_id=1, source_target_pairs={{0,4},{4,0},{8,12},{12,8},{1,5},{5,1},{9,13},{13,9},{2,6},{6,2},{1... | collective-permute-start | bytes 4718600 | tf_op jit(solution)/shard_map/ppermute | solution.py:64
  429.5 39.6 %collective-permute-start.48 = (bf16[512,1152]{1,0:T(8,128)(2,1)}, bf16[512,1152]{1,0:T(8,128)(2,1)}, u32[]{:S(2)}, u32[]{:S(2)}) collective-permute-start(bf16[512,1152]{1,0:T(8,128)(2,1)} %get-tuple-element.333), channel_id=1, source_target_pairs={{0,1},{1,0},{2,3},{3,2},{4,5},{5,4},{6,7},{7,6},{8,9},{9,8},{10,11... | collective-permute-start | bytes 3538952 | tf_op jit(solution)/shard_map/ppermute | solution.py:64
  429.5 38.4 %collective-permute-start.30 = (bf16[256,1536]{1,0:T(8,128)(2,1)}, bf16[256,1536]{1,0:T(8,128)(2,1)}, u32[]{:S(2)}, u32[]{:S(2)}) collective-permute-start(bf16[256,1536]{1,0:T(8,128)(2,1)} %fusion.24), channel_id=1, source_target_pairs={{0,8},{4,12},{8,0},{12,4},{1,9},{5,13},{9,1},{13,5},{2,10},{6,14},... | collective-permute-start | bytes 2359304 | tf_op jit(solution)/shard_map/ppermute | solution.py:64
  430.5 43.0 %collective-permute-start.29 = (bf16[2,512,512]{2,1,0:T(8,128)(2,1)}, bf16[2,512,512]{2,1,0:T(8,128)(2,1)}, u32[]{:S(2)}, u32[]{:S(2)}) collective-permute-start(bf16[2,512,512]{2,1,0:T(8,128)(2,1)} %get-tuple-element.304), channel_id=1, source_target_pairs={{12,8},{13,9},{14,10},{15,11},{28,24},{29,25},{30,26},{31,27}} | collective-permute-start | bytes 3145736 | tf_op jit(solution)/shard_map/ppermute | solution.py:1202
  432.1 69.0 %collective-permute-start.36 = (bf16[256,1536]{1,0:T(8,128)(2,1)}, bf16[256,1536]{1,0:T(8,128)(2,1)S(1)}, u32[]{:S(2)}, u32[]{:S(2)}) collective-permute-start(bf16[256,1536]{1,0:T(8,128)(2,1)} %fusion.28), channel_id=1, source_target_pairs={{0,8},{4,12},{8,0},{12,4},{1,9},{5,13},{9,1},{13,5},{2,10},{6,14},... | collective-permute-start | bytes 2359304 | tf_op jit(solution)/shard_map/ppermute | solution.py:64
  434.7 69.7 %collective-permute-start.31 = (bf16[256,1024]{1,0:T(8,128)(2,1)}, bf16[256,1024]{1,0:T(8,128)(2,1)}, u32[]{:S(2)}, u32[]{:S(2)}) collective-permute-start(bf16[256,1024]{1,0:T(8,128)(2,1)} %get-tuple-element.314), channel_id=1, source_target_pairs={{0,16},{16,0},{1,17},{17,1},{2,18},{18,2},{3,19},{19,3},{4,20},{20... | collective-permute-start | bytes 1572872 | tf_op jit(solution)/shard_map/ppermute | solution.py:69
  467.9 42.8 %collective-permute-start.33 = (bf16[256,1024]{1,0:T(8,128)(2,1)}, bf16[256,1024]{1,0:T(8,128)(2,1)}, u32[]{:S(2)}, u32[]{:S(2)}) collective-permute-start(bf16[256,1024]{1,0:T(8,128)(2,1)} %get-tuple-element.315), channel_id=1, source_target_pairs={{0,2},{1,3},{2,0},{3,1},{4,6},{5,7},{6,4},{7,5},{8,10},{9,11},{10,... | collective-permute-start | bytes 1572872 | tf_op jit(solution)/shard_map/ppermute | solution.py:64
  471.2 46.1 %collective-permute-start.49 = (bf16[256,1152]{1,0:T(8,128)(2,1)S(1)}, bf16[256,1152]{1,0:T(8,128)(2,1)}, u32[]{:S(2)}, u32[]{:S(2)}) collective-permute-start(bf16[256,1152]{1,0:T(8,128)(2,1)S(1)} %slice.373), channel_id=1, source_target_pairs={{0,2},{1,3},{2,0},{3,1},{4,6},{5,7},{6,4},{7,5},{8,10},{9,11},{10,... | collective-permute-start | bytes 1769480 | tf_op jit(solution)/shard_map/ppermute | solution.py:64
  509.5 42.6 %collective-permute-start.32 = (bf16[512,1024]{1,0:T(8,128)(2,1)}, bf16[512,1024]{1,0:T(8,128)(2,1)}, u32[]{:S(2)}, u32[]{:S(2)}) collective-permute-start(bf16[512,1024]{1,0:T(8,128)(2,1)} %combine.14), channel_id=1, source_target_pairs={{0,2},{1,3},{2,0},{3,1},{4,6},{5,7},{6,4},{7,5},{8,10},{9,11},{10,... | collective-permute-start | bytes 3145736 | tf_op jit(solution)/shard_map/ppermute | solution.py:64
  515.7 37.7 %collective-permute-start.34 = (bf16[512,1024]{1,0:T(8,128)(2,1)}, bf16[512,1024]{1,0:T(8,128)(2,1)}, u32[]{:S(2)}, u32[]{:S(2)}) collective-permute-start(bf16[512,1024]{1,0:T(8,128)(2,1)} %combine.15), channel_id=1, source_target_pairs={{0,16},{16,0},{1,17},{17,1},{2,18},{18,2},{3,19},{19,3},{4,20},{20... | collective-permute-start | bytes 3145736 | tf_op jit(solution)/shard_map/ppermute | solution.py:69
  521.4 48.1 %collective-permute-start.53 = (bf16[4,128,1536]{2,1,0:T(8,128)(2,1)}, bf16[4,128,1536]{2,1,0:T(8,128)(2,1)}, u32[]{:S(2)}, u32[]{:S(2)}) collective-permute-start(bf16[4,128,1536]{2,1,0:T(8,128)(2,1)} %pad_maximum_fusion.1), channel_id=1, source_target_pairs={{0,2},{1,3},{2,0},{3,1},{4,6},{5,7},{6,4},{7,5},{8,10},{9,11},{10,... | collective-permute-start | bytes 4718600 | tf_op jit(solution)/shard_map/ppermute | solution.py:64
  558.6 38.6 %collective-permute-start.52 = (bf16[32,1152]{1,0:T(8,128)(2,1)S(1)}, bf16[32,1152]{1,0:T(8,128)(2,1)}, u32[]{:S(2)}, u32[]{:S(2)}) collective-permute-start(bf16[32,1152]{1,0:T(8,128)(2,1)S(1)} %slice.383), channel_id=1, source_target_pairs={{0,8},{4,12},{8,0},{12,4},{1,9},{5,13},{9,1},{13,5},{2,10},{6,14},... | collective-permute-start | bytes 221192 | tf_op jit(solution)/shard_map/ppermute | solution.py:64
  (101 other events, 1149.0 us)

commit v3 on v2

--- a/solution.py
+++ b/solution.py
@@ -21,6 +21,8 @@
 VMEM_LIMIT = 56 * 1024 * 1024
 SMALL = pl.CostEstimate(flops=1, bytes_accessed=1, transcendentals=0)
 F32 = jnp.float32
+NT = (((1,), (1,)), ((), ()))
+TN = (((0,), (0,)), ((), ()))
 BF16 = jnp.bfloat16
 
 
@@ -227,138 +229,142 @@
     )(place, *operands)
 
 
-def experts_kernel(slot, chunk, spans, own, place_ref, *refs):
+def experts_kernel(first_slot, count, chunk, spans, arrived_at, place_ref, *refs):
+    own = arrived_at is not None
     xs_ref, us_ref, gates_ref, up_ref, down_ref = refs[:5]
-    refs = refs[5:]
-    arrived_refs = ()
-    if own:
-        arrived_refs, refs = refs[:2], refs[2:]
-    outs_ref, rows_ref, terms_ref = refs[:3]
-    pieces_refs = refs[3:5]
-    refs = refs[5:]
-    x_all, gu_all, gate_all, up_all, down_all, out_all, row_all, term_all, grad_all, hidden_all = refs[:10]
-    piece, pieces_all, *arrived_all, load_sems, store_sems = refs[10:]
-    total = x_all.shape[0]
-    ff = down_all.shape[0]
-    sources = [
-        (xs_ref.at[slot], x_all),
-        (up_ref.at[place_ref[0]], up_all),
-        (us_ref.at[slot], gu_all),
-        (gates_ref.at[slot], gate_all),
-        (down_ref.at[place_ref[0]], down_all),
-    ]
-    for i, arrived_ref in enumerate(arrived_refs):
-        count = arrived_ref.shape[0]
-        sources.append((arrived_ref, arrived_all[0].at[pl.ds(i * count, count)]))
-    loads = [
-        pltpu.make_async_copy(source, target, load_sems.at[i]) for i, (source, target) in enumerate(sources)
-    ]
-    for load in loads:
-        load.start()
+    arrived_ref, refs = (refs[5], refs[6:]) if own else (None, refs[5:])
+    results, refs = refs[: 3 * count], refs[3 * count :]
+    pieces_ref, refs = refs[0], refs[1:]
+    x_all, gu_all, gate_all, up_all, down_all, out_all, row_all, term_all, pieces_all = refs[:9]
+    grad_all, hidden_all, piece, *arrived_all, load_sems, store_sems = refs[9:]
+    total = x_all.shape[1]
+    ff = down_all.shape[1]
+    contexts = pieces_all.shape[1]
+    rows = piece.shape[0]
+    part = rows // spans
+    width = grad_all.shape[1]
+
+    def loads_of(e):
+        slot, weights = first_slot + e, place_ref[0] + e
+        sources = [
+            (xs_ref.at[slot], x_all.at[e]),
+            (up_ref.at[weights], up_all.at[e]),
+            (us_ref.at[slot], gu_all.at[e]),
+            (gates_ref.at[slot], gate_all.at[e]),
+            (down_ref.at[weights], down_all.at[e]),
+        ]
+        if own:
+            sources.append((arrived_ref.at[pl.ds(0, contexts), arrived_at + e], arrived_all[0].at[e]))
+        return [
+            pltpu.make_async_copy(source, target, load_sems.at[e, i])
+            for i, (source, target) in enumerate(sources)
+        ]
+
     stores = []
 
     def store(source, target):
         stores.append(pltpu.make_async_copy(source, target, store_sems.at[len(stores)]))
         stores[-1].start()
 
-    loads[0].wait()
-    loads[1].wait()
-    for number in range(total // chunk):
-        span = slice(number * chunk, (number + 1) * chunk)
-        at = pl.ds(number * chunk, chunk)
-        both = jnp.dot(x_all[span], up_all[...], preferred_element_type=F32)
-        if number == 0:
-            for load in loads[2:5]:
-                load.wait()
-        gate_pre, up_pre = both[:, :ff], both[:, ff:]
-        gu = (gu_all[span].astype(F32) * gate_all[span, 0:1]).astype(BF16)
-        gu_all[span] = gu
-        sigmoid = jax.nn.sigmoid(gate_pre)
-        activated = gate_pre * sigmoid
-        hidden = (activated * up_pre).astype(BF16)
-        hidden_all[span] = hidden
-        grad_hidden = lax.dot_general(gu, down_all[...], NT, preferred_element_type=F32)
-        out_all[span] = jnp.dot(hidden, down_all[...], preferred_element_type=F32).astype(BF16)
-        store(out_all.at[at], outs_ref.at[at])
-        terms = jnp.sum(grad_hidden * hidden.astype(F32), axis=1, keepdims=True)
-        term_all[span] = jnp.broadcast_to(terms, (chunk, term_all.shape[1]))
-        store(term_all.at[at], terms_ref.at[at])
-        grad_gate = grad_hidden * up_pre * sigmoid * (1.0 + gate_pre * (1.0 - sigmoid))
-        grad_both = jnp.concatenate(
-            [grad_gate.astype(BF16), (grad_hidden * activated).astype(BF16)], axis=1
-        )
-        grad_all[span] = grad_both
-        row_all[span] = lax.dot_general(
-            grad_both, up_all[...], NT, preferred_element_type=F32
-        ).astype(BF16)
-        store(row_all.at[at], rows_ref.at[at])
-    for load in loads[5:]:
-        load.wait()
-    contexts = pieces_all.shape[0]
-    half = contexts // 2
-    rows = piece.shape[0]
-    part = rows // spans
-    over_rows = (((0,), (0,)), ((), ()))
-    width = grad_all.shape[1]
-    for number in range(contexts):
-        relative = (number % half) * 2 + (1 if number < half else 0)
-        owner = lax.bitwise_xor(place_ref[1], relative)
-        columns = pl.ds(pl.multiple_of(owner * rows, rows), rows)
-        piece[:, :width] = lax.dot_general(
-            x_all[:, columns], grad_all[...], over_rows, preferred_element_type=F32
-        )
-        piece[:, width:] = lax.dot_general(
-            gu_all[:, columns], hidden_all[...], over_rows, preferred_element_type=F32
-        )
-        for near in range(spans):
-            wanted = lax.bitwise_xor(place_ref[2], near)
-            value = piece[pl.ds(pl.multiple_of(wanted * part, part), part), :]
-            to = slice(near * part, (near + 1) * part)
-            if own:
-                value = value + arrived_all[0][number, to, :].astype(F32)
-            pieces_all[number, to, :] = value.astype(BF16)
-        store(pieces_all.at[number], pieces_refs[number // half].at[number % half])
+    def start(loads):
+        for load in loads:
+            load.start()
+
+    loads = loads_of(0)
+    start(loads)
+    for e in range(count):
+        outs_ref, rows_ref, terms_ref = results[3 * e : 3 * e + 3]
+        following = loads_of(e + 1) if e + 1 < count else []
+        loads[0].wait()
+        loads[1].wait()
+        for number in range(total // chunk):
+            span = slice(number * chunk, (number + 1) * chunk)
+            at = pl.ds(number * chunk, chunk)
+            both = jnp.dot(x_all[e, span], up_all[e], preferred_element_type=F32)
+            if number == 0:
+                for load in loads[2:]:
+                    load.wait()
+                start(following)
+            gate_pre, up_pre = both[:, :ff], both[:, ff:]
+            gu = (gu_all[e, span].astype(F32) * gate_all[e, span, 0:1]).astype(BF16)
+            gu_all[e, span] = gu
+            sigmoid = jax.nn.sigmoid(gate_pre)
+            activated = gate_pre * sigmoid
+            hidden = (activated * up_pre).astype(BF16)
+            hidden_all[span] = hidden
+            grad_hidden = lax.dot_general(gu, down_all[e], NT, preferred_element_type=F32)
+            out_all[e, span] = jnp.dot(hidden, down_all[e], preferred_element_type=F32).astype(BF16)
+            store(out_all.at[e, at], outs_ref.at[at])
+            terms = jnp.sum(grad_hidden * hidden.astype(F32), axis=1, keepdims=True)
+            term_all[e, span] = jnp.broadcast_to(terms, (chunk, term_all.shape[2]))
+            store(term_all.at[e, at], terms_ref.at[at])
+            grad_gate = grad_hidden * up_pre * sigmoid * (1.0 + gate_pre * (1.0 - sigmoid))
+            grad_both = jnp.concatenate(
+                [grad_gate.astype(BF16), (grad_hidden * activated).astype(BF16)], axis=1
+            )
+            grad_all[span] = grad_both
+            row_all[e, span] = lax.dot_general(
+                grad_both, up_all[e], NT, preferred_element_type=F32
+            ).astype(BF16)
+            store(row_all.at[e, at], rows_ref.at[at])
+        for number in range(contexts):
+            columns = slice(number * rows, (number + 1) * rows)
+            piece[:, :width] = lax.dot_general(
+                x_all[e, :, columns], grad_all[...], TN, preferred_element_type=F32
+            )
+            piece[:, width:] = lax.dot_general(
+                gu_all[e, :, columns], hidden_all[...], TN, preferred_element_type=F32
+            )
+            for near in range(spans):
+                wanted = lax.bitwise_xor(place_ref[1], near)
+                value = piece[pl.ds(pl.multiple_of(wanted * part, part), part), :]
+                to = slice(near * part, (near + 1) * part)
+                if own:
+                    value = value + arrived_all[0][e, number, to, :].astype(F32)
+                pieces_all[e, number, to, :] = value.astype(BF16)
+            store(pieces_all.at[e, number], pieces_ref.at[number, e])
+        loads = following
     for copy in stores:
         copy.wait()
 
 
-def experts_work(place, slot, slots, slot_grads, slot_gates, w_gateup, w_down, contexts, spans, arrived):
+def experts_work(place, first_slot, count, slots, slot_grads, slot_gates, w_gateup, w_down, contexts, spans, arrived):
     total, width = slots.shape[1:]
     ff = w_down.shape[1]
     chunk = 2 * CAP
     rows = width // contexts
-    half = contexts // 2
     own = arrived is not None
     piece_width = w_gateup.shape[2] + ff
-    piece_shape = lambda count: jax.ShapeDtypeStruct((count, rows, piece_width), BF16)
     operands = [slots, slot_grads, slot_gates, w_gateup, w_down]
     out_shape = [
         jax.ShapeDtypeStruct((total, width), BF16),
         jax.ShapeDtypeStruct((total, width), BF16),
         jax.ShapeDtypeStruct((total, 128), F32),
-    ]
+    ] * count
+    out_shape.append(jax.ShapeDtypeStruct((contexts, count, rows, piece_width), BF16))
     scratch = [
-        pltpu.VMEM((total, width), BF16),
-        pltpu.VMEM((total, width), BF16),
-        pltpu.VMEM((total, 128), F32),
-        pltpu.VMEM(w_gateup.shape[1:], BF16),
-        pltpu.VMEM(w_down.shape[1:], BF16),
-        pltpu.VMEM((total, width), BF16),
-        pltpu.VMEM((total, width), BF16),
-        pltpu.VMEM((total, 128), F32),
+        pltpu.VMEM((count, total, width), BF16),
+        pltpu.VMEM((count, total, width), BF16),
+        pltpu.VMEM((count, total, 128), F32),
+        pltpu.VMEM((count,) + w_gateup.shape[1:], BF16),
+        pltpu.VMEM((count,) + w_down.shape[1:], BF16),
+        pltpu.VMEM((count, total, width), BF16),
+        pltpu.VMEM((count, total, width), BF16),
+        pltpu.VMEM((count, total, 128), F32),
+        pltpu.VMEM((count, contexts, rows, piece_width), BF16),
         pltpu.VMEM((total, 2 * ff), BF16),
         pltpu.VMEM((total, ff), BF16),
         pltpu.VMEM((rows, piece_width), F32),
-        pltpu.VMEM((contexts, rows, piece_width), BF16),
     ]
-    out_shape += [piece_shape(half), piece_shape(half)]
     if own:
-        operands += list(arrived)
-        scratch.append(pltpu.VMEM((contexts, rows, piece_width), BF16))
-    scratch.append(pltpu.SemaphoreType.DMA((7,)))
-    scratch.append(pltpu.SemaphoreType.DMA((3 * (total // chunk) + contexts,)))
-    return pl.pallas_call(
-        functools.partial(experts_kernel, slot, chunk, spans, own),
+        operands.append(arrived[0])
+        scratch.append(pltpu.VMEM((count, contexts, rows, piece_width), BF16))
+    scratch.append(pltpu.SemaphoreType.DMA((count, 7)))
+    scratch.append(pltpu.SemaphoreType.DMA((count * (3 * (total // chunk) + contexts),)))
+    results = pl.pallas_call(
+        functools.partial(
+            experts_kernel, first_slot, count, chunk, spans, arrived[1] if own else None
+        ),
         out_shape=out_shape,
         grid_spec=pltpu.PrefetchScalarGridSpec(
             num_scalar_prefetch=1,
@@ -371,6 +377,7 @@
         cost_estimate=SMALL,
         name="experts",
     )(place, *operands)
+    return [results[3 * e : 3 * e + 3] for e in range(count)], results[3 * count]
 
 
 def combine_kernel(pair_experts, half, extra_rows, added, results, with_terms, place_ref, slots_ref, *refs):
@@ -468,9 +475,6 @@
     return result[0] if results == 1 else result
 
 
-NT = (((1,), (1,)), ((), ()))
-
-
 def attend_kernel(first, last, distance, place_ref, q_ref, k_ref, v_ref, *refs):
     if first:
         state_in, stat_in = None, None
@@ -685,18 +689,17 @@
     )(place, *operands)
 
 
-TN = (((0,), (0,)), ((), ()))
-
-
-def sum_hops():
-    owners, contexts, spans = (lax.axis_size(a) for a in ("experts", "context", "dp"))
-    hops = []
-    for axis, count in (("dp", spans), ("experts", owners), ("context", contexts)):
+def sum_hops(experts_first=False):
+    hops = {}
+    for axis in ("dp", "experts", "context"):
         bit = 1
-        while bit < count:
-            hops.append((axis, bit))
+        hops[axis] = []
+        while bit < lax.axis_size(axis):
+            hops[axis].append((axis, bit))
             bit *= 2
-    return hops
+    core, along_x = hops["dp"][:1], hops["dp"][1:]
+    middle = hops["experts"] + along_x if experts_first else along_x + hops["experts"]
+    return core + middle + hops["context"]
 
 
 def put_arranged(value, columns, place_ref, plan, plain, arranged, keep_ref, send_ref):
@@ -716,9 +719,9 @@
     send_ref[:, columns] = arranged[half:, :width].astype(BF16)
 
 
-def sum_plan():
+def sum_plan(experts_first=False):
     contexts, spans = lax.axis_size("context"), lax.axis_size("dp")
-    hops = sum_hops()
+    hops = sum_hops(experts_first)
     masks = []
     for number in range(2 ** len(hops)):
         mask = {"experts": 0, "context": 0, "dp": 0}
@@ -729,14 +732,16 @@
     return contexts, spans, masks
 
 
-def summed(pair):
+def summed(pair, start=0, stop=None, experts_first=False):
     keep, send = pair
-    for i, (axis, bit) in enumerate(sum_hops()):
-        total = keep.astype(F32) + hop(send, axis, bit).astype(F32)
+    hops = sum_hops(experts_first)
+    for i in range(start, len(hops) if stop is None else stop):
+        total = keep.astype(F32) + hop(send, *hops[i]).astype(F32)
         rows = total.shape[0] // 2
-        if i + 1 == len(sum_hops()):
+        if i + 1 == len(hops):
             return total
         keep, send = total[:rows], total[rows:].astype(BF16)
+    return keep, send
 
 
 def turned_back(rows, cos, sin):
@@ -781,7 +786,7 @@
     whole = lambda array: pl.BlockSpec(array.shape, lambda i, s: (0, 0))
     shape = jax.ShapeDtypeStruct((rows // 2, width + 128), BF16)
     return pl.pallas_call(
-        functools.partial(out_grad_kernel, sum_plan(), steps),
+        functools.partial(out_grad_kernel, sum_plan(True), steps),
         out_shape=[shape, shape],
         grid_spec=pltpu.PrefetchScalarGridSpec(
             num_scalar_prefetch=1,
@@ -827,7 +832,7 @@
     shape = jax.ShapeDtypeStruct((rows // 2, columns), BF16)
     normed = jax.ShapeDtypeStruct((length, rows), F32)
     return pl.pallas_call(
-        functools.partial(query_grad_kernel, sum_plan(), scale),
+        functools.partial(query_grad_kernel, sum_plan(True), scale),
         out_shape=[shape, shape, normed],
         grid_spec=pltpu.PrefetchScalarGridSpec(
             num_scalar_prefetch=1,
@@ -1063,13 +1068,13 @@
     slot_gates = slot_gates.reshape(pair_experts, total, 128)
     slot_grads = slot_grads.reshape(pair_experts, total, width)
 
-    def work(number, own, gate, arrived):
+    def work(number, count, own, gate, arrived):
         owner = dp_place if own else other_core
-        work_place = jnp.stack([owner * own_experts + number, z_place, owner]).astype(jnp.int32)
-        slot = number if own else own_experts + number
+        work_place = jnp.stack([owner * own_experts + number, owner]).astype(jnp.int32)
         return experts_work(
             work_place,
-            slot,
+            number if own else own_experts + number,
+            count,
             after(slots, gate),
             slot_grads,
             slot_gates,
@@ -1081,57 +1086,32 @@
         )
 
     outs, rows, terms = ([None] * pair_experts for _ in range(3))
-    crossing, sent, kept_sums, near_sums, crossed, finals = ([None] * own_experts for _ in range(6))
-
-    def arrive_near(number, gate):
-        arrived = after(sent[number], gate)
-        near_sums[number] = add_low(kept_sums[number][0], arrived[0])
-        crossed[number] = add_low(kept_sums[number][1], arrived[1])
-        return crossed[number]
-
-    def cross(number, gate):
-        crossed[number] = hop(after(crossed[number], gate), "context", 2)
-
-    def fold_near(number, gate):
-        far = arrive_near(number, gate)
-        cross(number, far)
-        return far
-
-    def exchanged(numbers):
-        stacked = jnp.stack([finals[number] for number in numbers])
+    crossing, finals = [None] * own_experts, []
+
+    def exchange_x(stacked):
         part = stacked.shape[1] // spans
-        across = x_hop(stacked[:, 2 * part :])
+        return stacked, x_hop(stacked[:, 2 * part :])
+
+    def exchange_core(stacked, across):
+        part = stacked.shape[1] // spans
         beside = core_hop(jnp.concatenate([stacked[:, part : 2 * part], across[:, part:]], axis=1))
-        return jnp.stack([stacked[:, :part], beside[:, :part], across[:, :part], beside[:, part:]])
-
-    def fold_far(number, gate):
-        finals[number] = add_low(near_sums[number], after(crossed[number], gate))
-        return finals[number]
-
-    order = [(0, False)]
-    for number in range(own_experts):
-        if number + 1 < own_experts:
-            order.append((number + 1, False))
-        order.append((number, True))
+        return stacked[:, :part], beside[:, :part], across[:, :part], beside[:, part:]
+
     gate = slot_gates
-    for number, own in order:
-        if own and number == 2:
-            gate = fold_near(0, gate)
-        slot = number if own else own_experts + number
-        result = work(number, own, gate, crossing[number] if own else None)
-        outs[slot], rows[slot], terms[slot] = result[:3]
-        gate = result[2]
-        if own:
-            kept_sums[number] = result[4]
-            sent[number] = hop(result[3], "context", 1)
-        else:
-            crossing[number] = (core_hop(result[3]), core_hop(result[4]))
-
-    def near_then(number, value):
-        return after(value, fold_near(number, value)) if number < own_experts else value
-
-    def far_then(number, value):
-        return after(value, fold_far(number, value)) if number < own_experts else value
+    count = min(2, own_experts)
+    for own in (False, True):
+        for start in range(0, own_experts, count):
+            results, pieces = work(start, count, own, gate, crossing[start] if own else None)
+            for number in range(start, start + count):
+                slot = number if own else own_experts + number
+                outs[slot], rows[slot], terms[slot] = results[number - start]
+            gate = results[-1][2]
+            if own:
+                finals.append(lax.psum_scatter(pieces, "context", scatter_dimension=0, tiled=False))
+            else:
+                crossed_pieces = core_hop(pieces)
+                for number in range(start, start + count):
+                    crossing[number] = (crossed_pieces, number - start)
 
     def row_part(group, parts=()):
         results = 2 if group > owners else 1
@@ -1154,18 +1134,16 @@
     for group in far_groups:
         mixtures[group] = mixture_part(group, gate)
         gate = mixtures[group]
-    if own_experts < 3:
-        gate = near_then(0, gate)
-    gate = near_then(1, gate)
     far_sums = after(far_sums, gate)
     for group in near_groups:
         row_sums[group] = row_part(group, far_parts(far_sums, group))
     arrivals = return_near(row_sums)
     mixtures[0] = mixture_part(0, row_sums[near_groups[-1]])
     arrivals = after(arrivals, mixtures[0])
-    arrivals = far_then(0, near_then(2, arrivals))
     row_total = return_total(row_sums[0], arrivals)
-    row_total = far_then(1, row_total)
+    for group in far_groups:
+        mixtures[group] = after(mixtures[group], row_total)
+    far_mixtures = return_far(mixtures)
     grad_gate_terms = unpacked_rows(row_total[length:], length)
     grad_moe_rows = row_total[:length]
     grad_selected = grad_gate_terms - gates * jnp.sum(grad_gate_terms, axis=0, keepdims=True)
@@ -1182,8 +1160,6 @@
         jnp.einsum("td,fd->tf", grad_attn, output_weight, preferred_element_type=jnp.float32)
         .astype(jnp.bfloat16)
     )
-    grad_heads = near_then(3, grad_heads)
-
     def back(distance, grad_heads, arrived, grad_queries):
         return back_chunk(
             z_index,
@@ -1201,41 +1177,50 @@
         pairs = [(i, i - 1) for i in range(distance, contexts)]
         return lax.ppermute(grad_chunk, "context", pairs)
 
-    grad_chunk, grad_queries = back(contexts - 1, grad_heads, None, None)
-    arrived = down(contexts - 1, grad_chunk)
-    for group in far_groups:
-        mixtures[group] = after(mixtures[group], grad_chunk)
-    far_mixtures = return_far(mixtures)
-    own_chunk, grad_queries = back(0, after(grad_heads, grad_chunk), None, grad_queries)
-    grad_queries = far_then(2, grad_queries)
-    for distance in reversed(range(1, contexts - 1)):
-        arrived = after(arrived, grad_queries)
+    grad_queries, arrived = None, None
+    early_exchange = None
+    for distance in reversed(range(1, contexts)):
         grad_chunk, grad_queries = back(distance, grad_heads, arrived, grad_queries)
         arrived = down(distance, grad_chunk)
-        if distance == contexts - 2:
+        if distance == contexts - 1:
+            far_mixtures = after(far_mixtures, grad_chunk)
+            gate = grad_chunk
             for group in near_groups:
-                mixtures[group] = mixture_part(group, grad_chunk, far_parts(far_mixtures, group))
+                mixtures[group] = mixture_part(group, gate, far_parts(far_mixtures, group))
+                gate = mixtures[group]
             mixture_arrivals = return_near(mixtures)
-            grad_queries = far_then(3, grad_queries)
-    for number in range(4, own_experts):
-        grad_queries = far_then(number, near_then(number, grad_queries))
-    arrived = after(arrived, grad_queries)
-    mixed = return_total(mixtures[0], mixture_arrivals)
-    layer_output = (residual_middle + mixed).astype(jnp.bfloat16)[None]
-    early = summed(
-        out_grad(
-            sum_place,
-            attn_low,
-            after(grad_attn, own_chunk),
-            moe_low,
-            jnp.pad(grad_logits.T, ((0, 0), (0, 128 - EXPERTS))),
-            gain_moe_terms.astype(BF16),
-        )
-    )
+            own_chunk, grad_queries = back(0, after(grad_heads, gate), None, grad_queries)
+            arrived, grad_queries = lax.optimization_barrier((arrived, grad_queries))
+        elif distance == contexts - 2:
+            out_sums = out_grad(
+                sum_place,
+                attn_low,
+                after(grad_attn, grad_chunk),
+                moe_low,
+                jnp.pad(grad_logits.T, ((0, 0), (0, 128 - EXPERTS))),
+                gain_moe_terms.astype(BF16),
+            )
+            mixture_arrivals = after(mixture_arrivals, out_sums)
+            mixed = return_total(mixtures[0], mixture_arrivals)
+            layer_output = (residual_middle + mixed).astype(jnp.bfloat16)[None]
+            if len(finals) > 1:
+                early_exchange = exchange_x(after(finals[0], grad_chunk))
+            arrived, out_sums, layer_output, early_exchange = lax.optimization_barrier(
+                (arrived, out_sums, layer_output, early_exchange)
+            )
+    blocks = []
+    if early_exchange is not None:
+        early_exchange, grad_chunk = lax.optimization_barrier((early_exchange, grad_chunk))
+        blocks.append(exchange_core(*early_exchange))
+    out_sums = summed(after(out_sums, grad_chunk), 0, 1, True)
     *query_sums, grad_normed = query_grad(
         sum_place, grad_queries, cos_rows, sin_rows, normed_low, query_weight, scale
     )
-    grad_query = summed(query_sums)
+    arrived, grad_normed, out_sums, blocks, query_sums = lax.optimization_barrier(
+        (arrived, grad_normed, out_sums, blocks, query_sums)
+    )
+    query_sums = summed(query_sums, 0, 1, True)
+    out_sums = summed(out_sums, 1, 2, True)
     *keyval_sums, grad_input = keyval_grad(
         sum_place,
         own_chunk,
@@ -1251,14 +1236,32 @@
         grad_middle,
     )
     grad_input = grad_input[None]
-    late = summed(keyval_sums)
+    chains = [keyval_sums, query_sums, out_sums]
+    steps = [0, 1, 2]
+    order = [False, True, True]
+    stops = len(sum_hops())
+    chains = list(lax.optimization_barrier(tuple(chains)))
+    round_number = 0
+    last_exchange = exchange_x(after(finals[-1], chains[0]))
+    while min(steps) < stops:
+        for i in range(len(chains)):
+            if steps[i] < stops:
+                chains[i] = summed(chains[i], steps[i], steps[i] + 1, order[i])
+                steps[i] += 1
+        chains = list(lax.optimization_barrier(tuple(chains)))
+        if round_number == 2:
+            blocks.append(exchange_core(*after(last_exchange, chains[0])))
+        round_number += 1
+    late, grad_query, early = chains
     grad_out = early[:, :width]
     grad_router = early[:, width : width + EXPERTS]
     grad_gain_moe = early[:, width + EXPERTS]
     grad_keyval = late[:, :kv_width]
     grad_gain_attn = late[:, kv_width]
 
-    near_blocks = exchanged(range(own_experts))
+    near_blocks = jnp.stack(
+        [jnp.concatenate([block[place] for block in blocks], axis=0) for place in range(spans)]
+    )
     arranged = jnp.concatenate(
         [
             lax.dynamic_index_in_dim(near_blocks, jnp.bitwise_xor(dp_place, b), 0, keepdims=False)

time: 657 us -> 640 us (0.974)
  starting transfers between devices: 95.9 us -> 50.7 us
  waiting for transfers between devices: 192 us -> 234 us
  other arithmetic: 48.9 us -> 28 us
  between operations: 2.33 us -> 15.6 us
  Pallas kernels: 261 us -> 248 us
    ppermute x3, waiting for transfers between devices: 0.01 us -> 111 us  [down(): return lax.ppermute(grad_chunk, 'context', pairs)]
    ppermute x41 -> x29, waiting for transfers between devices: 190 us -> 92.6 us  [hop(): return lax.ppermute(value, axis, [(i, i ^ stride) for i in range(count)])]
    ppermute x41 -> x29, starting transfers between devices: 74.6 us -> 31.5 us  [hop(): return lax.ppermute(value, axis, [(i, i ^ stride) for i in range(count)])]
    ppermute x8, waiting for transfers between devices: 1.7 us -> 30 us  [turn(): lax.ppermute(value, axis, [(i, (i + step) % count) for i in range(count)])]
    convert_element_type x8 -> x0, other arithmetic: 14.1 us -> none  [add_low(): return total.astype(BF16)]
    pallas_call x10 -> x6, Pallas kernels: 112 us -> 100 us  [the longest x4 83.3 us: experts_work(): pl.pallas_call(functools.partial(experts_kernel, first_slot, count, chunk...]
    unnamed x141 -> x133, local copies, waits for them, and re-layouts: 12.4 us -> 14 us
  transfers between devices with their start and end apart: 55 -> 45, of which waited for: 17 -> 22; matrix products, arithmetic and copies ran while one was open for 11% -> 9% of each run, Pallas kernels for 33% -> 31%
where the time goes in v3:
time: 640 us; the launch traced here: 630 us
  Pallas kernels  248 us (39%)
  waiting for transfers between devices  234 us (37%)
  starting transfers between devices  50.7 us (8%)
  local copies, waits for them, and re-layouts  39.8 us (6%)
  other arithmetic  28 us (4%)
  between operations  15.6 us (2%)
  matrix products  14 us (2%)
    ppermute x3, waiting for transfers between devices, down(): return lax.ppermute(grad_chunk, 'context', pairs)  111 us
    ppermute x29, waiting for transfers between devices, hop(): return lax.ppermute(value, axis, [(i, i ^ stride) for i in range(count)])  92.6 us
    pallas_call x4, Pallas kernels, experts_work(): pl.pallas_call(functools.partial(experts_kernel, first_slot, count, chunk...  83.3 us
    pallas_call x8, Pallas kernels, combine(): pl.pallas_call(functools.partial(combine_kernel, pair_experts, half, extr...  41.2 us
    pallas_call x8, Pallas kernels, dispatch(): pl.pallas_call(functools.partial(dispatch_kernel, pair_experts, half, len...  40.6 us
    ppermute x29, starting transfers between devices, hop(): return lax.ppermute(value, axis, [(i, i ^ stride) for i in range(count)])  31.5 us
    ppermute x8, waiting for transfers between devices, turn(): lax.ppermute(value, axis, [(i, (i + step) % count) for i in range(count)])  30 us
    pallas_call x4, Pallas kernels, back_chunk(): pl.pallas_call(functools.partial(back_kernel, dq is None, distance == 0,...  29.2 us
  transfers between devices with their start and end apart: 45, of which 22 were waited for; matrix products, arithmetic and copies ran while one was open for 9% of the time, Pallas kernels for 31%

profile of v3, /device:TPU:0, one launch (start us, length us, event | category | flops | bytes accessed | tf_op | source)
XLA Modules:
  0.0 630.0 jit_solution(13533114781845164829)
XLA Ops:
  40.7 11.7 %attend.4 = (f32[1024,512]{1,0:T(8,128)}, f32[4,8,512]{2,1,0:T(8,128)}) custom-call(s32[1]{0:T(128)} %bitcast.place_ref, bf16[512,1024]{1,0:T(8,128)(2,1)} %copy.104.q_ref, bf16[512,1024]{1,0:T(8,128)(2,1)} %copy-done.4, bf16[512,1024]{1,0:T(8,128)(2,1)} %copy-done.4), custom_call_target="tpu_custom_call" | custom-call | flops 1 | bytes 1 | tf_op jit(solution)/shard_map/attend/pallas_call | solution.py:570
  81.2 7.3 %collective-permute-done.5.refs_0_ = bf16[256,1024]{1,0:T(8,128)(2,1)S(1)} collective-permute-done((bf16[256,1024]{1,0:T(8,128)(2,1)S(1)}, bf16[256,1024]{1,0:T(8,128)(2,1)S(1)}, u32[]{:S(2)}, u32[]{:S(2)}) %collective-permute-start.5) | collective-permute-done | bytes 524320 | tf_op jit(solution)/shard_map/ppermute | solution.py:66
  116.0 15.6 %collective-permute-done.8.refs_0_ = bf16[528,1024]{1,0:T(8,128)(2,1)S(1)} collective-permute-done((bf16[528,1024]{1,0:T(8,128)(2,1)S(1)}, bf16[528,1024]{1,0:T(8,128)(2,1)S(1)}, u32[]{:S(2)}, u32[]{:S(2)}) %collective-permute-start.8) | collective-permute-done | bytes 1081376 | tf_op jit(solution)/shard_map/ppermute | solution.py:71
  152.3 19.6 %experts.4 = (bf16[640,1024]{1,0:T(8,128)(2,1)}, bf16[640,1024]{1,0:T(8,128)(2,1)}, f32[640,128]{1,0:T(8,128)}, bf16[640,1024]{1,0:T(8,128)(2,1)}, bf16[640,1024...) custom-call(s32[2]{0:T(128)} %pad_add_fusion.3.place_ref, bf16[8,640,1024]{2,1,0:T(8,128)(2,1)} %bitcast.90, ...), custom_call_target="tpu_custom_call" | custom-call | flops 1 | bytes 1 | tf_op jit(solution)/shard_map/experts/pallas_call | solution.py:364
  172.6 19.7 %experts.5 = (bf16[640,1024]{1,0:T(8,128)(2,1)}, bf16[640,1024]{1,0:T(8,128)(2,1)}, f32[640,128]{1,0:T(8,128)}, bf16[640,1024]{1,0:T(8,128)(2,1)}, bf16[640,1024...) custom-call(s32[2]{0:T(128)} %get-tuple-element.418.place_ref, ...), custom_call_target="tpu_custom_call" | custom-call | flops 1 | bytes 1 | tf_op jit(solution)/shard_map/experts/pallas_call | solution.py:364
  192.3 22.1 %experts.6 = (bf16[640,1024]{1,0:T(8,128)(2,1)}, bf16[640,1024]{1,0:T(8,128)(2,1)}, f32[640,128]{1,0:T(8,128)}, bf16[640,1024]{1,0:T(8,128)(2,1)}, bf16[640,1024...) custom-call(s32[2]{0:T(128)} %pad_add_fusion.1.place_ref, bf16[8,640,1024]{2,1,0:T(8,128)(2,1)} %bitcast.92, ...), custom_call_target="tpu_custom_call" | custom-call | flops 1 | bytes 1 | tf_op jit(solution)/shard_map/experts/pallas_call | solution.py:364
  215.7 9.5 %collective-permute-done.12.refs_5_ = bf16[4,2,256,1536]{3,2,1,0:T(8,128)(2,1)} collective-permute-done((bf16[4,2,256,1536]{3,2,1,0:T(8,128)(2,1)}, bf16[4,2,256,1536]{3,2,1,0:T(8,128)(2,1)}, u32[]{:S(2)}, u32[]{:S(2)}) %collective-permute-start.12) | collective-permute-done | bytes 6291488 | tf_op jit(solution)/shard_map/ppermute | solution.py:66
  225.1 21.9 %experts.7 = (bf16[640,1024]{1,0:T(8,128)(2,1)}, bf16[640,1024]{1,0:T(8,128)(2,1)}, f32[640,128]{1,0:T(8,128)}, bf16[640,1024]{1,0:T(8,128)(2,1)}, bf16[640,1024...) custom-call(s32[2]{0:T(128)} %pad_add_fusion.4.place_ref, bf16[8,640,1024]{2,1,0:T(8,128)(2,1)} %bitcast.93, ...), custom_call_target="tpu_custom_call" | custom-call | flops 1 | bytes 1 | tf_op jit(solution)/shard_map/experts/pallas_call | solution.py:364
  268.6 5.3 combine.12
  274.5 5.4 combine.11
  285.6 13.8 %collective-permute-done.16 = bf16[528,1024]{1,0:T(8,128)(2,1)} collective-permute-done((bf16[528,1024]{1,0:T(8,128)(2,1)}, bf16[528,1024]{1,0:T(8,128)(2,1)}, u32[]{:S(2)}, u32[]{:S(2)}) %collective-permute-start.16) | collective-permute-done | bytes 1081376 | tf_op jit(solution)/shard_map/ppermute | solution.py:71
  299.4 5.6 collective-permute-done.15
  325.0 9.6 %collective-permute-done.18.refs_9_ = bf16[256,1024]{1,0:T(8,128)(2,1)S(1)} collective-permute-done((bf16[256,1024]{1,0:T(8,128)(2,1)S(1)}, bf16[256,1024]{1,0:T(8,128)(2,1)S(1)}, u32[]{:S(2)}, u32[]{:S(2)}) %collective-permute-start.18) | collective-permute-done | bytes 524320 | tf_op jit(solution)/shard_map/ppermute | solution.py:66
  348.9 13.1 %back.5 = (bf16[2,512,512]{2,1,0:T(8,128)(2,1)}, f32[1024,512]{1,0:T(8,128)}) custom-call(s32[1]{0:T(128)} %bitcast.place_ref, bf16[512,1024]{1,0:T(8,128)(2,1)} %copy.104.q_ref, bf16[512,1024]{1,0:T(8,128)(2,1)} %copy-done.4, bf16[512,1024]{1,0:T(8,128)(2,1)} %copy-done.4, bf16[512,1024]{1,0:T(8,128)(2,1)} %convolution_convert_fusion.grad_ref, ...), custom_call_target="tpu_custom_call" | custom-call | flops 1 | bytes 1 | tf_op jit(solution)/shard_map/back/pallas_call | solution.py:677
  363.0 5.6 back.6
  373.5 8.2 %out_grad.1 = (bf16[512,1152]{1,0:T(8,128)(2,1)}, bf16[512,1152]{1,0:T(8,128)(2,1)}) custom-call(s32[3]{0:T(128)} %pad_add_fusion.5.place_ref, bf16[512,1024]{1,0:T(8,128)(2,1)} %get-tuple-element.229.low_ref, bf16[512,1024]{1,0:T(8,128)(2,1)} %copy-done.15, bf16[512,1024]{1,0:T(8,128)(2,1)} %copy-done.5, bf16[512,128]{1,0:T(8,128)(2,1)} %pad.4.logits_ref, ...), custom_call_target="tpu_custom_call" | custom-call | flops 1 | bytes 1 | tf_op jit(solution)/shard_map/out_grad/pallas_call | solution.py:788
  387.6 5.7 back.7
  398.1 8.8 %query_grad.1 = (bf16[512,1024]{1,0:T(8,128)(2,1)}, bf16[512,1024]{1,0:T(8,128)(2,1)}, f32[512,1024]{1,0:T(8,128)}) custom-call(s32[3]{0:T(128)} %pad_add_fusion.5.place_ref, f32[1024,512]{1,0:T(8,128)} %get-tuple-element.321.dq_ref, f32[32,512]{1,0:T(8,128)} %get-tuple-element.406.cos_ref, f32[32,512]{1,0:T(8,128)} %get-tuple-element.405.sin_ref, ...), custom_call_target="tpu_custom_call" | custom-call | flops 1 | bytes 1 | tf_op jit(solution)/shard_map/query_grad/pallas_call | solution.py:834
  408.9 110.8 %collective-permute-done.24.arrived_ref = bf16[2,512,512]{2,1,0:T(8,128)(2,1)S(1)} collective-permute-done((bf16[2,512,512]{2,1,0:T(8,128)(2,1)}, bf16[2,512,512]{2,1,0:T(8,128)(2,1)S(1)}, u32[]{:S(2)}, u32[]{:S(2)}) %collective-permute-start.24) | collective-permute-done | bytes 1048608 | tf_op jit(solution)/shard_map/ppermute | solution.py:1178
  521.4 12.0 %keyval_grad.1 = (bf16[512,1152]{1,0:T(8,128)(2,1)}, bf16[512,1152]{1,0:T(8,128)(2,1)}, bf16[512,1024]{1,0:T(8,128)(2,1)}) custom-call(s32[3]{0:T(128)} %pad_add_fusion.5.place_ref, bf16[2,512,512]{2,1,0:T(8,128)(2,1)} %get-tuple-element.317.own_ref, bf16[2,512,512]{2,1,0:T(8,128)(2,1)} %copy-done.37, f32[32,512]{1,0:T(8,128)} %get-tuple-element.406.cos_ref, ...), custom_call_target="tpu_custom_call" | custom-call | flops 1 | bytes 1 | tf_op jit(solution)/shard_map/keyval_grad/pallas_call | solution.py:911
  539.2 7.5 %collective-permute-done.31 = bf16[128,1152]{1,0:T(8,128)(2,1)S(1)} collective-permute-done((bf16[128,1152]{1,0:T(8,128)(2,1)S(1)}, bf16[128,1152]{1,0:T(8,128)(2,1)S(1)}, u32[]{:S(2)}, u32[]{:S(2)}) %collective-permute-start.31) | collective-permute-done | bytes 294944 | tf_op jit(solution)/shard_map/ppermute | solution.py:66
  564.3 9.5 %collective-permute-done.32 = bf16[256,1152]{1,0:T(8,128)(2,1)S(1)} collective-permute-done((bf16[256,1152]{1,0:T(8,128)(2,1)S(1)}, bf16[256,1152]{1,0:T(8,128)(2,1)S(1)}, u32[]{:S(2)}, u32[]{:S(2)}) %collective-permute-start.32) | collective-permute-done | bytes 589856 | tf_op jit(solution)/shard_map/ppermute | solution.py:66
  574.8 8.9 %collective-permute-start.37 = (bf16[32,1152]{1,0:T(8,128)(2,1)}, bf16[32,1152]{1,0:T(8,128)(2,1)S(1)}, u32[]{:S(2)}, u32[]{:S(2)}) collective-permute-start(bf16[32,1152]{1,0:T(8,128)(2,1)} %slice.314), channel_id=1, source_target_pairs={{0,8},{4,12},{8,0},{12,4},{1,9},{5,13},{9,1},{13,5},{2,10},{6,14},... | collective-permute-start | bytes 221192 | tf_op jit(solution)/shard_map/ppermute | solution.py:66
  595.2 7.3 %collective-permute-done.41 = bf16[2,128,1536]{2,1,0:T(8,128)(2,1)S(1)} collective-permute-done((bf16[2,128,1536]{2,1,0:T(8,128)(2,1)S(1)}, bf16[2,128,1536]{2,1,0:T(8,128)(2,1)S(1)}, u32[]{:S(2)}, u32[]{:S(2)}) %collective-permute-start.41) | collective-permute-done | bytes 786464 | tf_op jit(solution)/shard_map/ppermute | solution.py:66
  (359 shorter events, 249.9 us)
Async XLA Ops:
  7.2 363.0 %reduce-scatter.3.cloned.1.call-start = ((), (), s32[]{:S(2)}) async-start(), calls=%async_computation.2 | async-start | bytes 7864320 | tf_op jit(solution)/shard_map/reduce_scatter | solution.py:1110
  11.7 45.7 %collective-permute-start.1 = (bf16[528,1024]{1,0:T(8,128)(2,1)}, bf16[528,1024]{1,0:T(8,128)(2,1)}, u32[]{:S(2)}, u32[]{:S(2)}) collective-permute-start(bf16[528,1024]{1,0:T(8,128)(2,1)} %pad_maximum_fusion.1.refs_0_), channel_id=1, source_target_pairs={{0,2},{1,3},{2,0},{3,1},{4,6},{5,7},{6,4},{7,5},{8,10},{9,11},{10,... | collective-permute-start | bytes 3244040 | tf_op jit(solution)/shard_map/ppermute | solution.py:66
  23.0 39.4 %collective-permute-start = (bf16[512,1024]{1,0:T(8,128)(2,1)S(1)}, bf16[512,1024]{1,0:T(8,128)(2,1)}, u32[]{:S(2)}, u32[]{:S(2)}) collective-permute-start(bf16[512,1024]{1,0:T(8,128)(2,1)S(1)} %pad_maximum_fusion.3.k_ref.v_ref), channel_id=1, source_target_pairs={{0,4},{4,8},{8,12},{1,5},{5,9},{9,13},{2,6},{6,10},{10,14},{3,7},{... | collective-permute-start | bytes 3145736 | tf_op jit(solution)/shard_map/ppermute | solution.py:1015
  27.5 40.0 %collective-permute-start.3 = (bf16[528,1024]{1,0:T(8,128)(2,1)}, bf16[528,1024]{1,0:T(8,128)(2,1)}, u32[]{:S(2)}, u32[]{:S(2)}) collective-permute-start(bf16[528,1024]{1,0:T(8,128)(2,1)} %pad_maximum_fusion.1.refs_0_), channel_id=1, source_target_pairs={{0,16},{16,0},{1,17},{17,1},{2,18},{18,2},{3,19},{19,3},{4,20},{20... | collective-permute-start | bytes 3244040 | tf_op jit(solution)/shard_map/ppermute | solution.py:71
  72.4 22.0 %collective-permute-start.4 = (bf16[512,1024]{1,0:T(8,128)(2,1)S(1)}, bf16[512,1024]{1,0:T(8,128)(2,1)S(1)}, u32[]{:S(2)}, u32[]{:S(2)}) collective-permute-start(bf16[512,1024]{1,0:T(8,128)(2,1)S(1)} %collective-permute-done.2.k_ref.v_ref), channel_id=1, source_target_pairs={{8,12},{9,13},{10,14},{11,15},{24,28},{25,29},{26,30},{27,31}} | collective-permute-start | bytes 3145736 | tf_op jit(solution)/shard_map/ppermute | solution.py:1015
  74.2 14.3 %collective-permute-start.6 = (bf16[272,1024]{1,0:T(8,128)(2,1)S(1)}, bf16[272,1024]{1,0:T(8,128)(2,1)S(1)}, u32[]{:S(2)}, u32[]{:S(2)}) collective-permute-start(bf16[272,1024]{1,0:T(8,128)(2,1)S(1)} %slice.191), channel_id=1, source_target_pairs={{0,16},{16,0},{1,17},{17,1},{2,18},{18,2},{3,19},{19,3},{4,20},{20... | collective-permute-start | bytes 1671176 | tf_op jit(solution)/shard_map/ppermute | solution.py:71
  108.0 23.6 %collective-permute-start.8 = (bf16[528,1024]{1,0:T(8,128)(2,1)S(1)}, bf16[528,1024]{1,0:T(8,128)(2,1)S(1)}, u32[]{:S(2)}, u32[]{:S(2)}) collective-permute-start(bf16[528,1024]{1,0:T(8,128)(2,1)S(1)} %pad_maximum_fusion.2.refs_0_), channel_id=1, source_target_pairs={{0,16},{16,0},{1,17},{17,1},{2,18},{18,2},{3,19},{19,3},{4,20},{20... | collective-permute-start | bytes 3244040 | tf_op jit(solution)/shard_map/ppermute | solution.py:71
  109.5 23.5 %collective-permute-start.7 = (bf16[528,1024]{1,0:T(8,128)(2,1)S(1)}, bf16[528,1024]{1,0:T(8,128)(2,1)S(1)}, u32[]{:S(2)}, u32[]{:S(2)}) collective-permute-start(bf16[528,1024]{1,0:T(8,128)(2,1)S(1)} %pad_maximum_fusion.2.refs_0_), channel_id=1, source_target_pairs={{0,2},{1,3},{2,0},{3,1},{4,6},{5,7},{6,4},{7,5},{8,10},{9,11},{10,... | collective-permute-start | bytes 3244040 | tf_op jit(solution)/shard_map/ppermute | solution.py:66
  171.9 20.3 %collective-permute-start.11 = (bf16[4,2,256,1536]{3,2,1,0:T(8,128)(2,1)}, bf16[4,2,256,1536]{3,2,1,0:T(8,128)(2,1)}, u32[]{:S(2)}, u32[]{:S(2)}) collective-permute-start(bf16[4,2,256,1536]{3,2,1,0:T(8,128)(2,1)} %get-tuple-element.258), channel_id=1, source_target_pairs={{0,1},{1,0},{2,3},{3,2},{4,5},{5,4},{6,7},{7,6},{8,9},{9,8},{10,11... | collective-permute-start | bytes 18874376 | tf_op jit(solution)/shard_map/ppermute | solution.py:66
  214.4 369.3 %reduce-scatter.5.cloned.1.call-start = ((), (), s32[]{:S(2)}) async-start(), calls=%async_computation.3 | async-start | bytes 7864320 | tf_op jit(solution)/shard_map/reduce_scatter | solution.py:1110
  252.1 15.7 %collective-permute-start.14 = (bf16[272,1024]{1,0:T(8,128)(2,1)}, bf16[272,1024]{1,0:T(8,128)(2,1)S(1)}, u32[]{:S(2)}, u32[]{:S(2)}) collective-permute-start(bf16[272,1024]{1,0:T(8,128)(2,1)} %get-tuple-element.276), channel_id=1, source_target_pairs={{0,16},{16,0},{1,17},{17,1},{2,18},{18,2},{3,19},{19,3},{4,20},{20... | collective-permute-start | bytes 1671176 | tf_op jit(solution)/shard_map/ppermute | solution.py:71
  273.9 25.5 %collective-permute-start.16 = (bf16[528,1024]{1,0:T(8,128)(2,1)}, bf16[528,1024]{1,0:T(8,128)(2,1)}, u32[]{:S(2)}, u32[]{:S(2)}) collective-permute-start(bf16[528,1024]{1,0:T(8,128)(2,1)} %combine.12), channel_id=1, source_target_pairs={{0,16},{16,0},{1,17},{17,1},{2,18},{18,2},{3,19},{19,3},{4,20},{20... | collective-permute-start | bytes 3244040 | tf_op jit(solution)/shard_map/ppermute | solution.py:71
  279.8 25.1 %collective-permute-start.15 = (bf16[528,1024]{1,0:T(8,128)(2,1)}, bf16[528,1024]{1,0:T(8,128)(2,1)}, u32[]{:S(2)}, u32[]{:S(2)}) collective-permute-start(bf16[528,1024]{1,0:T(8,128)(2,1)} %combine.11), channel_id=1, source_target_pairs={{0,2},{1,3},{2,0},{3,1},{4,6},{5,7},{6,4},{7,5},{8,10},{9,11},{10,... | collective-permute-start | bytes 3244040 | tf_op jit(solution)/shard_map/ppermute | solution.py:66
  321.8 40.3 %collective-permute-start.17 = (bf16[2,512,512]{2,1,0:T(8,128)(2,1)}, bf16[2,512,512]{2,1,0:T(8,128)(2,1)S(1)}, u32[]{:S(2)}, u32[]{:S(2)}) collective-permute-start(bf16[2,512,512]{2,1,0:T(8,128)(2,1)} %get-tuple-element.296), channel_id=1, source_target_pairs={{12,8},{13,9},{14,10},{15,11},{28,24},{29,25},{30,26},{31,27}} | collective-permute-start | bytes 3145736 | tf_op jit(solution)/shard_map/ppermute | solution.py:1178
  346.3 35.4 %collective-permute-start.22 = (bf16[512,1024]{1,0:T(8,128)(2,1)}, bf16[512,1024]{1,0:T(8,128)(2,1)}, u32[]{:S(2)}, u32[]{:S(2)}) collective-permute-start(bf16[512,1024]{1,0:T(8,128)(2,1)} %combine.15), channel_id=1, source_target_pairs={{0,16},{16,0},{1,17},{17,1},{2,18},{18,2},{3,19},{19,3},{4,20},{20... | collective-permute-start | bytes 3145736 | tf_op jit(solution)/shard_map/ppermute | solution.py:71
  347.7 34.0 %collective-permute-start.21 = (bf16[512,1024]{1,0:T(8,128)(2,1)S(1)}, bf16[512,1024]{1,0:T(8,128)(2,1)}, u32[]{:S(2)}, u32[]{:S(2)}) collective-permute-start(bf16[512,1024]{1,0:T(8,128)(2,1)S(1)} %copy-done.36), channel_id=1, source_target_pairs={{0,2},{1,3},{2,0},{3,1},{4,6},{5,7},{6,4},{7,5},{8,10},{9,11},{10,... | collective-permute-start | bytes 3145736 | tf_op jit(solution)/shard_map/ppermute | solution.py:66
  368.6 16.4 %collective-permute-start.20 = (bf16[2,512,512]{2,1,0:T(8,128)(2,1)}, bf16[2,512,512]{2,1,0:T(8,128)(2,1)}, u32[]{:S(2)}, u32[]{:S(2)}) collective-permute-start(bf16[2,512,512]{2,1,0:T(8,128)(2,1)} %get-tuple-element.308), channel_id=1, source_target_pairs={{8,4},{12,8},{9,5},{13,9},{10,6},{14,10},{11,7},{15,11},{24,20},{2... | collective-permute-start | bytes 3145736 | tf_op jit(solution)/shard_map/ppermute | solution.py:1178
  371.4 16.2 %collective-permute-start.23 = (bf16[2,128,1536]{2,1,0:T(8,128)(2,1)S(1)}, bf16[2,128,1536]{2,1,0:T(8,128)(2,1)S(1)}, u32[]{:S(2)}, u32[]{:S(2)}) collective-permute-start(bf16[2,128,1536]{2,1,0:T(8,128)(2,1)S(1)} %slice.196), channel_id=1, source_target_pairs={{0,2},{1,3},{2,0},{3,1},{4,6},{5,7},{6,4},{7,5},{8,10},{9,11},{10,... | collective-permute-start | bytes 2359304 | tf_op jit(solution)/shard_map/ppermute | solution.py:66
  396.6 123.1 %collective-permute-start.24 = (bf16[2,512,512]{2,1,0:T(8,128)(2,1)}, bf16[2,512,512]{2,1,0:T(8,128)(2,1)S(1)}, u32[]{:S(2)}, u32[]{:S(2)}) collective-permute-start(bf16[2,512,512]{2,1,0:T(8,128)(2,1)} %get-tuple-element.320), channel_id=1, source_target_pairs={{4,0},{8,4},{12,8},{5,1},{9,5},{13,9},{6,2},{10,6},{14,10},{7,3},{... | collective-permute-start | bytes 3145736 | tf_op jit(solution)/shard_map/ppermute | solution.py:1178
  519.7 15.2 %collective-permute-start.28 = (bf16[256,1152]{1,0:T(8,128)(2,1)S(1)}, bf16[256,1152]{1,0:T(8,128)(2,1)S(1)}, u32[]{:S(2)}, u32[]{:S(2)}) collective-permute-start(bf16[256,1152]{1,0:T(8,128)(2,1)S(1)} %slice.304), channel_id=1, source_target_pairs={{0,16},{16,0},{1,17},{17,1},{2,18},{18,2},{3,19},{19,3},{4,20},{20... | collective-permute-start | bytes 1769480 | tf_op jit(solution)/shard_map/ppermute | solution.py:66
  520.5 14.6 %collective-permute-start.27 = (bf16[512,1024]{1,0:T(8,128)(2,1)S(1)}, bf16[512,1024]{1,0:T(8,128)(2,1)S(1)}, u32[]{:S(2)}, u32[]{:S(2)}) collective-permute-start(bf16[512,1024]{1,0:T(8,128)(2,1)S(1)} %copy-done.63), channel_id=1, source_target_pairs={{0,1},{1,0},{2,3},{3,2},{4,5},{5,4},{6,7},{7,6},{8,9},{9,8},{10,11... | collective-permute-start | bytes 3145736 | tf_op jit(solution)/shard_map/ppermute | solution.py:66
  537.3 15.0 %collective-permute-start.29 = (bf16[512,1152]{1,0:T(8,128)(2,1)S(1)}, bf16[512,1152]{1,0:T(8,128)(2,1)S(1)}, u32[]{:S(2)}, u32[]{:S(2)}) collective-permute-start(bf16[512,1152]{1,0:T(8,128)(2,1)S(1)} %copy-done.62), channel_id=1, source_target_pairs={{0,1},{1,0},{2,3},{3,2},{4,5},{5,4},{6,7},{7,6},{8,9},{9,8},{10,11... | collective-permute-start | bytes 3538952 | tf_op jit(solution)/shard_map/ppermute | solution.py:66
  555.3 18.5 %collective-permute-start.32 = (bf16[256,1152]{1,0:T(8,128)(2,1)S(1)}, bf16[256,1152]{1,0:T(8,128)(2,1)S(1)}, u32[]{:S(2)}, u32[]{:S(2)}) collective-permute-start(bf16[256,1152]{1,0:T(8,128)(2,1)S(1)} %slice.303), channel_id=1, source_target_pairs={{0,2},{1,3},{2,0},{3,1},{4,6},{5,7},{6,4},{7,5},{8,10},{9,11},{10,... | collective-permute-start | bytes 1769480 | tf_op jit(solution)/shard_map/ppermute | solution.py:66
  584.9 17.7 %collective-permute-start.41 = (bf16[2,128,1536]{2,1,0:T(8,128)(2,1)S(1)}, bf16[2,128,1536]{2,1,0:T(8,128)(2,1)S(1)}, u32[]{:S(2)}, u32[]{:S(2)}) collective-permute-start(bf16[2,128,1536]{2,1,0:T(8,128)(2,1)S(1)} %slice.232), channel_id=1, source_target_pairs={{0,2},{1,3},{2,0},{3,1},{4,6},{5,7},{6,4},{7,5},{8,10},{9,11},{10,... | collective-permute-start | bytes 2359304 | tf_op jit(solution)/shard_map/ppermute | solution.py:66
  (95 other events, 958.1 us)
Sparse Core Ops, SparseCore 0:
  214.5 135.1 reduce-scatter.2
  352.0 160.9 reduce-scatter.4

commit v4 on v3

--- a/solution.py
+++ b/solution.py
@@ -1107,6 +1107,11 @@
                 outs[slot], rows[slot], terms[slot] = results[number - start]
             gate = results[-1][2]
             if own:
+                following = range(start + count, min(start + 2 * count, own_experts))
+                if following:
+                    pieces, crossed_pieces = lax.optimization_barrier((pieces, crossing[following[0]][0]))
+                    for number in following:
+                        crossing[number] = (crossed_pieces, number - following[0])
                 finals.append(lax.psum_scatter(pieces, "context", scatter_dimension=0, tiled=False))
             else:
                 crossed_pieces = core_hop(pieces)

time: 640 us -> 634 us (level)
    ppermute x8, waiting for transfers between devices: 30 us -> 14.6 us  [turn(): lax.ppermute(value, axis, [(i, (i + step) % count) for i in range(count)])]
    ppermute x3, waiting for transfers between devices: 111 us -> 118 us  [down(): return lax.ppermute(grad_chunk, 'context', pairs)]
    unnamed x133 -> x129, local copies, waits for them, and re-layouts: 14 us -> 13.3 us
  transfers between devices with their start and end apart: 45 -> 45, of which waited for: 22 -> 22; matrix products, arithmetic and copies ran while one was open for 9% -> 9% of each run, Pallas kernels for 31% -> 35%
where the time goes in v4:
time: 634 us; the launch traced here: 625 us
  Pallas kernels  250 us (39%)
  waiting for transfers between devices  230 us (36%)
  starting transfers between devices  47.1 us (7%)
  local copies, waits for them, and re-layouts  40.7 us (6%)
  other arithmetic  27.4 us (4%)
  between operations  15.6 us (2%)
  matrix products  13.9 us (2%)
    ppermute x3, waiting for transfers between devices, down(): return lax.ppermute(grad_chunk, 'context', pairs)  118 us
    ppermute x29, waiting for transfers between devices, hop(): return lax.ppermute(value, axis, [(i, i ^ stride) for i in range(count)])  97 us
    pallas_call x4, Pallas kernels, experts_work(): pl.pallas_call(functools.partial(experts_kernel, first_slot, count, chunk...  83.3 us
    pallas_call x8, Pallas kernels, combine(): pl.pallas_call(functools.partial(combine_kernel, pair_experts, half, extr...  41.9 us
    pallas_call x8, Pallas kernels, dispatch(): pl.pallas_call(functools.partial(dispatch_kernel, pair_experts, half, len...  40.5 us
    pallas_call x4, Pallas kernels, back_chunk(): pl.pallas_call(functools.partial(back_kernel, dq is None, distance == 0,...  29.2 us
    ppermute x29, starting transfers between devices, hop(): return lax.ppermute(value, axis, [(i, i ^ stride) for i in range(count)])  28.6 us
    pallas_call x4, Pallas kernels, attend_chunk(): pl.pallas_call(functools.partial(attend_kernel, first, last, distance), o...  25 us
  transfers between devices with their start and end apart: 45, of which 22 were waited for; matrix products, arithmetic and copies ran while one was open for 9% of the time, Pallas kernels for 35%

profile of v4, /device:TPU:0, one launch (start us, length us, event | category | flops | bytes accessed | tf_op | source)
XLA Modules:
  0.0 624.9 jit_solution(11448391389591276446)
XLA Ops:
  40.7 11.7 %attend.4 = (f32[1024,512]{1,0:T(8,128)}, f32[4,8,512]{2,1,0:T(8,128)}) custom-call(s32[1]{0:T(128)} %bitcast.place_ref, bf16[512,1024]{1,0:T(8,128)(2,1)} %copy.104.q_ref, bf16[512,1024]{1,0:T(8,128)(2,1)} %copy-done.4, bf16[512,1024]{1,0:T(8,128)(2,1)} %copy-done.4), custom_call_target="tpu_custom_call" | custom-call | flops 1 | bytes 1 | tf_op jit(solution)/shard_map/attend/pallas_call | solution.py:570
  81.2 7.3 %collective-permute-done.5.refs_0_ = bf16[256,1024]{1,0:T(8,128)(2,1)S(1)} collective-permute-done((bf16[256,1024]{1,0:T(8,128)(2,1)S(1)}, bf16[256,1024]{1,0:T(8,128)(2,1)S(1)}, u32[]{:S(2)}, u32[]{:S(2)}) %collective-permute-start.5) | collective-permute-done | bytes 524320 | tf_op jit(solution)/shard_map/ppermute | solution.py:66
  115.9 15.6 %collective-permute-done.7.refs_0_ = bf16[528,1024]{1,0:T(8,128)(2,1)S(1)} collective-permute-done((bf16[528,1024]{1,0:T(8,128)(2,1)S(1)}, bf16[528,1024]{1,0:T(8,128)(2,1)S(1)}, u32[]{:S(2)}, u32[]{:S(2)}) %collective-permute-start.7) | collective-permute-done | bytes 1081376 | tf_op jit(solution)/shard_map/ppermute | solution.py:66
  154.3 19.6 %experts.4 = (bf16[640,1024]{1,0:T(8,128)(2,1)}, bf16[640,1024]{1,0:T(8,128)(2,1)}, f32[640,128]{1,0:T(8,128)}, bf16[640,1024]{1,0:T(8,128)(2,1)}, bf16[640,1024...) custom-call(s32[2]{0:T(128)} %get-tuple-element.423.place_ref, ...), custom_call_target="tpu_custom_call" | custom-call | flops 1 | bytes 1 | tf_op jit(solution)/shard_map/experts/pallas_call | solution.py:364
  174.0 19.7 %experts.5 = (bf16[640,1024]{1,0:T(8,128)(2,1)}, bf16[640,1024]{1,0:T(8,128)(2,1)}, f32[640,128]{1,0:T(8,128)}, bf16[640,1024]{1,0:T(8,128)(2,1)}, bf16[640,1024...) custom-call(s32[2]{0:T(128)} %get-tuple-element.422.place_ref, ...), custom_call_target="tpu_custom_call" | custom-call | flops 1 | bytes 1 | tf_op jit(solution)/shard_map/experts/pallas_call | solution.py:364
  194.8 22.1 %experts.6 = (bf16[640,1024]{1,0:T(8,128)(2,1)}, bf16[640,1024]{1,0:T(8,128)(2,1)}, f32[640,128]{1,0:T(8,128)}, bf16[640,1024]{1,0:T(8,128)(2,1)}, bf16[640,1024...) custom-call(s32[2]{0:T(128)} %pad_add_fusion.1.place_ref, bf16[8,640,1024]{2,1,0:T(8,128)(2,1)} %bitcast.92, ...), custom_call_target="tpu_custom_call" | custom-call | flops 1 | bytes 1 | tf_op jit(solution)/shard_map/experts/pallas_call | solution.py:364
  217.1 21.9 %experts.7 = (bf16[640,1024]{1,0:T(8,128)(2,1)}, bf16[640,1024]{1,0:T(8,128)(2,1)}, f32[640,128]{1,0:T(8,128)}, bf16[640,1024]{1,0:T(8,128)(2,1)}, bf16[640,1024...) custom-call(s32[2]{0:T(128)} %get-tuple-element.424.place_ref, ...), custom_call_target="tpu_custom_call" | custom-call | flops 1 | bytes 1 | tf_op jit(solution)/shard_map/experts/pallas_call | solution.py:364
  245.3 5.9 combine.8
  277.3 12.3 %collective-permute-done.16 = bf16[528,1024]{1,0:T(8,128)(2,1)} collective-permute-done((bf16[528,1024]{1,0:T(8,128)(2,1)}, bf16[528,1024]{1,0:T(8,128)(2,1)}, u32[]{:S(2)}, u32[]{:S(2)}) %collective-permute-start.16) | collective-permute-done | bytes 1081376 | tf_op jit(solution)/shard_map/ppermute | solution.py:71
  289.6 6.6 %collective-permute-done.15 = bf16[528,1024]{1,0:T(8,128)(2,1)} collective-permute-done((bf16[528,1024]{1,0:T(8,128)(2,1)}, bf16[528,1024]{1,0:T(8,128)(2,1)}, u32[]{:S(2)}, u32[]{:S(2)}) %collective-permute-start.15) | collective-permute-done | bytes 1081376 | tf_op jit(solution)/shard_map/ppermute | solution.py:66
  315.5 10.2 %collective-permute-done.18.refs_9_ = bf16[256,1024]{1,0:T(8,128)(2,1)S(1)} collective-permute-done((bf16[256,1024]{1,0:T(8,128)(2,1)S(1)}, bf16[256,1024]{1,0:T(8,128)(2,1)S(1)}, u32[]{:S(2)}, u32[]{:S(2)}) %collective-permute-start.18) | collective-permute-done | bytes 524320 | tf_op jit(solution)/shard_map/ppermute | solution.py:66
  339.2 13.0 %back.5 = (bf16[2,512,512]{2,1,0:T(8,128)(2,1)}, f32[1024,512]{1,0:T(8,128)}) custom-call(s32[1]{0:T(128)} %bitcast.place_ref, bf16[512,1024]{1,0:T(8,128)(2,1)} %copy.104.q_ref, bf16[512,1024]{1,0:T(8,128)(2,1)} %copy-done.4, bf16[512,1024]{1,0:T(8,128)(2,1)} %copy-done.4, bf16[512,1024]{1,0:T(8,128)(2,1)} %convolution_convert_fusion.grad_ref, ...), custom_call_target="tpu_custom_call" | custom-call | flops 1 | bytes 1 | tf_op jit(solution)/shard_map/back/pallas_call | solution.py:677
  353.1 5.6 back.6
  363.7 9.1 %out_grad.1 = (bf16[512,1152]{1,0:T(8,128)(2,1)}, bf16[512,1152]{1,0:T(8,128)(2,1)}) custom-call(s32[3]{0:T(128)} %pad_add_fusion.5.place_ref, bf16[512,1024]{1,0:T(8,128)(2,1)} %get-tuple-element.231.low_ref, bf16[512,1024]{1,0:T(8,128)(2,1)} %copy-done.15, bf16[512,1024]{1,0:T(8,128)(2,1)} %copy-done.5, bf16[512,128]{1,0:T(8,128)(2,1)} %pad.4.logits_ref, ...), custom_call_target="tpu_custom_call" | custom-call | flops 1 | bytes 1 | tf_op jit(solution)/shard_map/out_grad/pallas_call | solution.py:788
  377.3 5.7 back.7
  387.8 9.0 %query_grad.1 = (bf16[512,1024]{1,0:T(8,128)(2,1)}, bf16[512,1024]{1,0:T(8,128)(2,1)}, f32[512,1024]{1,0:T(8,128)}) custom-call(s32[3]{0:T(128)} %pad_add_fusion.5.place_ref, f32[1024,512]{1,0:T(8,128)} %get-tuple-element.325.dq_ref, f32[32,512]{1,0:T(8,128)} %get-tuple-element.410.cos_ref, f32[32,512]{1,0:T(8,128)} %get-tuple-element.409.sin_ref, ...), custom_call_target="tpu_custom_call" | custom-call | flops 1 | bytes 1 | tf_op jit(solution)/shard_map/query_grad/pallas_call | solution.py:834
  398.9 118.5 %collective-permute-done.24.arrived_ref = bf16[2,512,512]{2,1,0:T(8,128)(2,1)S(1)} collective-permute-done((bf16[2,512,512]{2,1,0:T(8,128)(2,1)}, bf16[2,512,512]{2,1,0:T(8,128)(2,1)S(1)}, u32[]{:S(2)}, u32[]{:S(2)}) %collective-permute-start.24) | collective-permute-done | bytes 1048608 | tf_op jit(solution)/shard_map/ppermute | solution.py:1183
  519.7 12.0 %keyval_grad.1 = (bf16[512,1152]{1,0:T(8,128)(2,1)}, bf16[512,1152]{1,0:T(8,128)(2,1)}, bf16[512,1024]{1,0:T(8,128)(2,1)}) custom-call(s32[3]{0:T(128)} %pad_add_fusion.5.place_ref, bf16[2,512,512]{2,1,0:T(8,128)(2,1)} %get-tuple-element.321.own_ref, bf16[2,512,512]{2,1,0:T(8,128)(2,1)} %copy-done.36, f32[32,512]{1,0:T(8,128)} %get-tuple-element.410.cos_ref, ...), custom_call_target="tpu_custom_call" | custom-call | flops 1 | bytes 1 | tf_op jit(solution)/shard_map/keyval_grad/pallas_call | solution.py:911
  537.3 6.7 %collective-permute-done.31 = bf16[128,1152]{1,0:T(8,128)(2,1)S(1)} collective-permute-done((bf16[128,1152]{1,0:T(8,128)(2,1)S(1)}, bf16[128,1152]{1,0:T(8,128)(2,1)S(1)}, u32[]{:S(2)}, u32[]{:S(2)}) %collective-permute-start.31) | collective-permute-done | bytes 294944 | tf_op jit(solution)/shard_map/ppermute | solution.py:66
  544.1 6.0 collective-permute-done.30
  562.5 9.4 %collective-permute-done.32 = bf16[256,1152]{1,0:T(8,128)(2,1)S(1)} collective-permute-done((bf16[256,1152]{1,0:T(8,128)(2,1)S(1)}, bf16[256,1152]{1,0:T(8,128)(2,1)S(1)}, u32[]{:S(2)}, u32[]{:S(2)}) %collective-permute-start.32) | collective-permute-done | bytes 589856 | tf_op jit(solution)/shard_map/ppermute | solution.py:66
  587.9 7.4 %collective-permute-done.41 = bf16[2,128,1536]{2,1,0:T(8,128)(2,1)S(1)} collective-permute-done((bf16[2,128,1536]{2,1,0:T(8,128)(2,1)S(1)}, bf16[2,128,1536]{2,1,0:T(8,128)(2,1)S(1)}, u32[]{:S(2)}, u32[]{:S(2)}) %collective-permute-start.41) | collective-permute-done | bytes 786464 | tf_op jit(solution)/shard_map/ppermute | solution.py:66
  596.0 6.3 %collective-permute-done.39 = bf16[32,1024]{1,0:T(8,128)(2,1)S(1)} collective-permute-done((bf16[32,1024]{1,0:T(8,128)(2,1)S(1)}, bf16[32,1024]{1,0:T(8,128)(2,1)S(1)}, u32[]{:S(2)}, u32[]{:S(2)}) %collective-permute-start.39) | collective-permute-done | bytes 65568 | tf_op jit(solution)/shard_map/ppermute | solution.py:66
  603.3 5.6 collective-permute-done.40
  (353 shorter events, 242.3 us)
Async XLA Ops:
  7.2 353.2 %reduce-scatter.3.cloned.1.call-start = ((), (), s32[]{:S(2)}) async-start(), calls=%async_computation.2 | async-start | bytes 7864320 | tf_op jit(solution)/shard_map/reduce_scatter | solution.py:1115
  11.7 45.6 %collective-permute-start.1 = (bf16[528,1024]{1,0:T(8,128)(2,1)}, bf16[528,1024]{1,0:T(8,128)(2,1)}, u32[]{:S(2)}, u32[]{:S(2)}) collective-permute-start(bf16[528,1024]{1,0:T(8,128)(2,1)} %pad_maximum_fusion.1.refs_0_), channel_id=1, source_target_pairs={{0,2},{1,3},{2,0},{3,1},{4,6},{5,7},{6,4},{7,5},{8,10},{9,11},{10,... | collective-permute-start | bytes 3244040 | tf_op jit(solution)/shard_map/ppermute | solution.py:66
  23.0 39.4 %collective-permute-start = (bf16[512,1024]{1,0:T(8,128)(2,1)S(1)}, bf16[512,1024]{1,0:T(8,128)(2,1)}, u32[]{:S(2)}, u32[]{:S(2)}) collective-permute-start(bf16[512,1024]{1,0:T(8,128)(2,1)S(1)} %pad_maximum_fusion.3.k_ref.v_ref), channel_id=1, source_target_pairs={{0,4},{4,8},{8,12},{1,5},{5,9},{9,13},{2,6},{6,10},{10,14},{3,7},{... | collective-permute-start | bytes 3145736 | tf_op jit(solution)/shard_map/ppermute | solution.py:1015
  27.5 40.0 %collective-permute-start.3 = (bf16[528,1024]{1,0:T(8,128)(2,1)}, bf16[528,1024]{1,0:T(8,128)(2,1)}, u32[]{:S(2)}, u32[]{:S(2)}) collective-permute-start(bf16[528,1024]{1,0:T(8,128)(2,1)} %pad_maximum_fusion.1.refs_0_), channel_id=1, source_target_pairs={{0,16},{16,0},{1,17},{17,1},{2,18},{18,2},{3,19},{19,3},{4,20},{20... | collective-permute-start | bytes 3244040 | tf_op jit(solution)/shard_map/ppermute | solution.py:71
  72.4 21.9 %collective-permute-start.4 = (bf16[512,1024]{1,0:T(8,128)(2,1)S(1)}, bf16[512,1024]{1,0:T(8,128)(2,1)S(1)}, u32[]{:S(2)}, u32[]{:S(2)}) collective-permute-start(bf16[512,1024]{1,0:T(8,128)(2,1)S(1)} %collective-permute-done.2.k_ref.v_ref), channel_id=1, source_target_pairs={{8,12},{9,13},{10,14},{11,15},{24,28},{25,29},{26,30},{27,31}} | collective-permute-start | bytes 3145736 | tf_op jit(solution)/shard_map/ppermute | solution.py:1015
  107.8 23.6 %collective-permute-start.7 = (bf16[528,1024]{1,0:T(8,128)(2,1)S(1)}, bf16[528,1024]{1,0:T(8,128)(2,1)S(1)}, u32[]{:S(2)}, u32[]{:S(2)}) collective-permute-start(bf16[528,1024]{1,0:T(8,128)(2,1)S(1)} %pad_maximum_fusion.2.refs_0_), channel_id=1, source_target_pairs={{0,2},{1,3},{2,0},{3,1},{4,6},{5,7},{6,4},{7,5},{8,10},{9,11},{10,... | collective-permute-start | bytes 3244040 | tf_op jit(solution)/shard_map/ppermute | solution.py:66
  109.1 23.6 %collective-permute-start.8 = (bf16[528,1024]{1,0:T(8,128)(2,1)S(1)}, bf16[528,1024]{1,0:T(8,128)(2,1)S(1)}, u32[]{:S(2)}, u32[]{:S(2)}) collective-permute-start(bf16[528,1024]{1,0:T(8,128)(2,1)S(1)} %pad_maximum_fusion.2.refs_0_), channel_id=1, source_target_pairs={{0,16},{16,0},{1,17},{17,1},{2,18},{18,2},{3,19},{19,3},{4,20},{20... | collective-permute-start | bytes 3244040 | tf_op jit(solution)/shard_map/ppermute | solution.py:71
  173.9 20.9 %collective-permute-start.11 = (bf16[4,2,256,1536]{3,2,1,0:T(8,128)(2,1)}, bf16[4,2,256,1536]{3,2,1,0:T(8,128)(2,1)}, u32[]{:S(2)}, u32[]{:S(2)}) collective-permute-start(bf16[4,2,256,1536]{3,2,1,0:T(8,128)(2,1)} %get-tuple-element.260), channel_id=1, source_target_pairs={{0,1},{1,0},{2,3},{3,2},{4,5},{5,4},{6,7},{7,6},{8,9},{9,8},{10,11... | collective-permute-start | bytes 18874376 | tf_op jit(solution)/shard_map/ppermute | solution.py:66
  193.7 23.3 %collective-permute-start.12 = (bf16[4,2,256,1536]{3,2,1,0:T(8,128)(2,1)}, bf16[4,2,256,1536]{3,2,1,0:T(8,128)(2,1)}, u32[]{:S(2)}, u32[]{:S(2)}) collective-permute-start(bf16[4,2,256,1536]{3,2,1,0:T(8,128)(2,1)} %get-tuple-element.266), channel_id=1, source_target_pairs={{0,1},{1,0},{2,3},{3,2},{4,5},{5,4},{6,7},{7,6},{8,9},{9,8},{10,11... | collective-permute-start | bytes 18874376 | tf_op jit(solution)/shard_map/ppermute | solution.py:66
  217.0 359.9 %reduce-scatter.5.cloned.1.call-start = ((), (), s32[]{:S(2)}) async-start(), calls=%async_computation.3 | async-start | bytes 7864320 | tf_op jit(solution)/shard_map/reduce_scatter | solution.py:1115
  264.4 25.2 %collective-permute-start.16 = (bf16[528,1024]{1,0:T(8,128)(2,1)}, bf16[528,1024]{1,0:T(8,128)(2,1)}, u32[]{:S(2)}, u32[]{:S(2)}) collective-permute-start(bf16[528,1024]{1,0:T(8,128)(2,1)} %combine.12), channel_id=1, source_target_pairs={{0,16},{16,0},{1,17},{17,1},{2,18},{18,2},{3,19},{19,3},{4,20},{20... | collective-permute-start | bytes 3244040 | tf_op jit(solution)/shard_map/ppermute | solution.py:71
  271.5 24.7 %collective-permute-start.15 = (bf16[528,1024]{1,0:T(8,128)(2,1)}, bf16[528,1024]{1,0:T(8,128)(2,1)}, u32[]{:S(2)}, u32[]{:S(2)}) collective-permute-start(bf16[528,1024]{1,0:T(8,128)(2,1)} %combine.11), channel_id=1, source_target_pairs={{0,2},{1,3},{2,0},{3,1},{4,6},{5,7},{6,4},{7,5},{8,10},{9,11},{10,... | collective-permute-start | bytes 3244040 | tf_op jit(solution)/shard_map/ppermute | solution.py:66
  313.2 39.0 %collective-permute-start.17 = (bf16[2,512,512]{2,1,0:T(8,128)(2,1)}, bf16[2,512,512]{2,1,0:T(8,128)(2,1)S(1)}, u32[]{:S(2)}, u32[]{:S(2)}) collective-permute-start(bf16[2,512,512]{2,1,0:T(8,128)(2,1)} %get-tuple-element.300), channel_id=1, source_target_pairs={{12,8},{13,9},{14,10},{15,11},{28,24},{29,25},{30,26},{31,27}} | collective-permute-start | bytes 3145736 | tf_op jit(solution)/shard_map/ppermute | solution.py:1183
  337.4 35.4 %collective-permute-start.22 = (bf16[512,1024]{1,0:T(8,128)(2,1)}, bf16[512,1024]{1,0:T(8,128)(2,1)}, u32[]{:S(2)}, u32[]{:S(2)}) collective-permute-start(bf16[512,1024]{1,0:T(8,128)(2,1)} %combine.15), channel_id=1, source_target_pairs={{0,16},{16,0},{1,17},{17,1},{2,18},{18,2},{3,19},{19,3},{4,20},{20... | collective-permute-start | bytes 3145736 | tf_op jit(solution)/shard_map/ppermute | solution.py:71
  338.0 34.8 %collective-permute-start.21 = (bf16[512,1024]{1,0:T(8,128)(2,1)S(1)}, bf16[512,1024]{1,0:T(8,128)(2,1)}, u32[]{:S(2)}, u32[]{:S(2)}) collective-permute-start(bf16[512,1024]{1,0:T(8,128)(2,1)S(1)} %copy-done.35), channel_id=1, source_target_pairs={{0,2},{1,3},{2,0},{3,1},{4,6},{5,7},{6,4},{7,5},{8,10},{9,11},{10,... | collective-permute-start | bytes 3145736 | tf_op jit(solution)/shard_map/ppermute | solution.py:66
  358.7 17.3 %collective-permute-start.20 = (bf16[2,512,512]{2,1,0:T(8,128)(2,1)}, bf16[2,512,512]{2,1,0:T(8,128)(2,1)}, u32[]{:S(2)}, u32[]{:S(2)}) collective-permute-start(bf16[2,512,512]{2,1,0:T(8,128)(2,1)} %get-tuple-element.312), channel_id=1, source_target_pairs={{8,4},{12,8},{9,5},{13,9},{10,6},{14,10},{11,7},{15,11},{24,20},{2... | collective-permute-start | bytes 3145736 | tf_op jit(solution)/shard_map/ppermute | solution.py:1183
  361.6 15.8 %collective-permute-start.23 = (bf16[2,128,1536]{2,1,0:T(8,128)(2,1)S(1)}, bf16[2,128,1536]{2,1,0:T(8,128)(2,1)S(1)}, u32[]{:S(2)}, u32[]{:S(2)}) collective-permute-start(bf16[2,128,1536]{2,1,0:T(8,128)(2,1)S(1)} %slice.196), channel_id=1, source_target_pairs={{0,2},{1,3},{2,0},{3,1},{4,6},{5,7},{6,4},{7,5},{8,10},{9,11},{10,... | collective-permute-start | bytes 2359304 | tf_op jit(solution)/shard_map/ppermute | solution.py:66
  386.3 131.0 %collective-permute-start.24 = (bf16[2,512,512]{2,1,0:T(8,128)(2,1)}, bf16[2,512,512]{2,1,0:T(8,128)(2,1)S(1)}, u32[]{:S(2)}, u32[]{:S(2)}) collective-permute-start(bf16[2,512,512]{2,1,0:T(8,128)(2,1)} %get-tuple-element.324), channel_id=1, source_target_pairs={{4,0},{8,4},{12,8},{5,1},{9,5},{13,9},{6,2},{10,6},{14,10},{7,3},{... | collective-permute-start | bytes 3145736 | tf_op jit(solution)/shard_map/ppermute | solution.py:1183
  517.4 15.1 %collective-permute-start.28 = (bf16[256,1152]{1,0:T(8,128)(2,1)S(1)}, bf16[256,1152]{1,0:T(8,128)(2,1)S(1)}, u32[]{:S(2)}, u32[]{:S(2)}) collective-permute-start(bf16[256,1152]{1,0:T(8,128)(2,1)S(1)} %slice.304), channel_id=1, source_target_pairs={{0,16},{16,0},{1,17},{17,1},{2,18},{18,2},{3,19},{19,3},{4,20},{20... | collective-permute-start | bytes 1769480 | tf_op jit(solution)/shard_map/ppermute | solution.py:66
  534.6 15.7 %collective-permute-start.29 = (bf16[512,1152]{1,0:T(8,128)(2,1)S(1)}, bf16[512,1152]{1,0:T(8,128)(2,1)S(1)}, u32[]{:S(2)}, u32[]{:S(2)}) collective-permute-start(bf16[512,1152]{1,0:T(8,128)(2,1)S(1)} %copy-done.60), channel_id=1, source_target_pairs={{0,1},{1,0},{2,3},{3,2},{4,5},{5,4},{6,7},{7,6},{8,9},{9,8},{10,11... | collective-permute-start | bytes 3538952 | tf_op jit(solution)/shard_map/ppermute | solution.py:66
  553.0 18.8 %collective-permute-start.32 = (bf16[256,1152]{1,0:T(8,128)(2,1)S(1)}, bf16[256,1152]{1,0:T(8,128)(2,1)S(1)}, u32[]{:S(2)}, u32[]{:S(2)}) collective-permute-start(bf16[256,1152]{1,0:T(8,128)(2,1)S(1)} %slice.303), channel_id=1, source_target_pairs={{0,2},{1,3},{2,0},{3,1},{4,6},{5,7},{6,4},{7,5},{8,10},{9,11},{10,... | collective-permute-start | bytes 1769480 | tf_op jit(solution)/shard_map/ppermute | solution.py:66
  578.1 17.1 %collective-permute-start.41 = (bf16[2,128,1536]{2,1,0:T(8,128)(2,1)S(1)}, bf16[2,128,1536]{2,1,0:T(8,128)(2,1)S(1)}, u32[]{:S(2)}, u32[]{:S(2)}) collective-permute-start(bf16[2,128,1536]{2,1,0:T(8,128)(2,1)S(1)} %slice.232), channel_id=1, source_target_pairs={{0,2},{1,3},{2,0},{3,1},{4,6},{5,7},{6,4},{7,5},{8,10},{9,11},{10,... | collective-permute-start | bytes 2359304 | tf_op jit(solution)/shard_map/ppermute | solution.py:66
  587.5 15.6 %collective-permute-start.38 = (bf16[64,1152]{1,0:T(8,128)(2,1)S(1)}, bf16[64,1152]{1,0:T(8,128)(2,1)S(1)}, u32[]{:S(2)}, u32[]{:S(2)}) collective-permute-start(bf16[64,1152]{1,0:T(8,128)(2,1)S(1)} %slice.310), channel_id=1, source_target_pairs={{0,4},{4,0},{8,12},{12,8},{1,5},{5,1},{9,13},{13,9},{2,6},{6,2},{1... | collective-permute-start | bytes 442376 | tf_op jit(solution)/shard_map/ppermute | solution.py:66
  595.5 16.7 %collective-permute-start.42 = (bf16[2,128,1536]{2,1,0:T(8,128)(2,1)S(1)}, bf16[2,128,1536]{2,1,0:T(8,128)(2,1)S(1)}, u32[]{:S(2)}, u32[]{:S(2)}) collective-permute-start(bf16[2,128,1536]{2,1,0:T(8,128)(2,1)S(1)} %pad_maximum_fusion.5), channel_id=1, source_target_pairs={{0,1},{1,0},{2,3},{3,2},{4,5},{5,4},{6,7},{7,6},{8,9},{9,8},{10,11... | collective-permute-start | bytes 2359304 | tf_op jit(solution)/shard_map/ppermute | solution.py:66
  (92 other events, 950.9 us)
Sparse Core Ops, SparseCore 0:
  217.1 134.8 reduce-scatter.2
  354.3 145.0 reduce-scatter.4
